TPU v7x, 256 devices: a whole 4x4x8 slice. The times are simulated.
256 devices in a mesh: ao: 16 (over x_hi, z), pair: 16 (over y, x_lo, core).
Axes of the slice: x: 4 (x_hi: 2, x_lo: 2; x = x_hi * 2 + x_lo), y: 4, z: 8, core: 2. Of those that a mesh axis runs over, the one named last changes fastest.
Arguments:
- green_occ: bfloat16 [2048, 2048], P(None, 'ao'), may hold values from -0.75 to 0.75
- green_virtual: bfloat16 [2048, 2048], P(None, 'ao'), may hold values from -0.75 to 0.75
- tile_values: bfloat16 [4096, 64, 128], P(('ao', 'pair')), may hold values from -0.4375 to 0.4375
- tile_orbital: int32 [4096], P(('ao', 'pair')), may hold values from 0 to 31
- tile_window: int32 [4096], P(('ao', 'pair')), may hold values from 0 to 15
- tile_count: int32 [256], P(('ao', 'pair')), may hold values from 1 to 16, as said below
Outputs:
- polarizability: float32 [8192, 1536], P(('ao', 'pair'))
Inputs may be any that keep to these rules, and one draw needn't show every extreme that they name: `tile_count`: some row group in every draw has all 16 slots live.
All inputs are finite; a program needn't handle non-finite values.
Results may differ from a plain program's by a relative error of at most 0.0041.
Values may be sent and summed in bfloat16 or wider, within the bound.
No kernel may reach another device: no remote copies, remote signals or barrier semaphores. Data moves between devices by JAX's collectives and lax.ppermute only.
A program may use at most 64 MiB of HBM per device.

v0:
```python
import functools

import jax
import jax.numpy as jnp
from jax import lax
from jax.experimental import pallas as pl
from jax.experimental.pallas import tpu as pltpu
from jax.sharding import PartitionSpec as P

AXES = ("ao", "pair")
BLK = 64
TILES = 16
PAIRS = TILES // 2
NAO = 2048
RW = 1024
COLS = 128
PIECE = NAO // 8
META = 16
BODY = PAIRS * 128
PAY = BODY + META
GROUPS = 8
DEPTH = GROUPS * 512
BF = jnp.bfloat16
F32 = jnp.float32


def device_of(index):
    ao, pair = index // 16, index % 16
    return ao // 8, ao % 8, pair // 4, (pair // 2) % 2, pair % 2


def index_of(x_hi, z, y, x_lo, core):
    return ((x_hi % 2) * 8 + z % 8) * 16 + ((y % 4) * 2 + x_lo % 2) * 2 + core % 2


def permute(value, where):
    pairs = [(source, index_of(*where(*device_of(source)))) for source in range(256)]
    return lax.ppermute(value, AXES, pairs)


def along_y(value, steps):
    return permute(value, lambda x_hi, z, y, x_lo, core: (x_hi, z, y + steps, x_lo, core))


def along_z(value, steps):
    return permute(value, lambda x_hi, z, y, x_lo, core: (x_hi, z + steps, y, x_lo, core))


def swap_x(value):
    return permute(value, lambda x_hi, z, y, x_lo, core: (x_hi, z, y, x_lo + 1, core))


def swap_core(value):
    return permute(value, lambda x_hi, z, y, x_lo, core: (x_hi, z, y, x_lo, core + 1))


def next_group(value, flip):
    def where(x_hi, z, y, x_lo, core):
        return (x_hi + (z == 7), z + 1, y, x_lo + flip, core)

    return permute(value, where)


Z_OFFSETS = (3, 6, 1, 5, 7, 0, 4, 2)


def scatter_target(x_hi, z, y, x_lo, core):
    target_y, target_x, target_core = z % 4, x_hi, z // 4
    target_hi = x_hi + (x_lo - target_x) % 2
    return target_hi, z + Z_OFFSETS[(y - target_y) % 4 * 2 + core], target_y, target_x, target_core


def piece_copies(occ_ref, vir_ref, out_ref, sems):
    ao, pair = lax.axis_index("ao"), lax.axis_index("pair")
    z, y, core = lax.rem(ao, 8), pair // 4, lax.rem(pair, 2)
    case = lax.rem(y - lax.rem(z, 4) + 4, 4) * 2 + core
    target_z = z
    for number, offset in enumerate(Z_OFFSETS):
        target_z = target_z + jnp.where(case == number, offset, 0)
    copies = []
    for spot in range(2):
        start = pl.multiple_of(lax.rem(target_z + 4 * spot, 8) * PIECE, PIECE)
        for part, ref in enumerate((occ_ref, vir_ref)):
            copies.append(pltpu.make_async_copy(
                ref.at[pl.ds(start, PIECE)],
                out_ref.at[pl.ds(spot * PIECE, PIECE), pl.ds(part * COLS, COLS)],
                sems.at[spot * 2 + part],
            ))
    return copies


def pack_kernel(
    orbital_ref, window_ref, count_ref, tile_ref, occ_ref, vir_ref, out_ref, piece_ref, order_ref, sems
):
    copies = piece_copies(occ_ref, vir_ref, piece_ref, sems)
    for copy in copies:
        copy.start()
    live = count_ref[0]
    windows = [window_ref[slot] for slot in range(TILES)]
    keys = [
        jnp.where(slot < live, windows[slot], TILES) * TILES + slot for slot in range(TILES)
    ]
    ranks = [jnp.int32(0) for slot in range(TILES)]
    for first in range(TILES):
        for second in range(first + 1, TILES):
            later = (keys[second] < keys[first]).astype(jnp.int32)
            ranks[first] = ranks[first] + later
            ranks[second] = ranks[second] + (1 - later)
    for slot in range(TILES):
        order_ref[ranks[slot]] = slot
    lane = lax.broadcasted_iota(jnp.int32, (META, 128), 1)
    meta = jnp.where(lane == 32, live, jnp.zeros((META, 128), jnp.int32))
    last = jnp.int32(0)
    for slot in range(TILES):
        source = order_ref[slot]
        last = jnp.where(slot < live, window_ref[source], last)
        meta = jnp.where(lane == slot, last, meta)
        meta = jnp.where(lane == TILES + slot, orbital_ref[source], meta)
    for index in range(PAIRS):
        rows = []
        for slot in (2 * index, 2 * index + 1):
            rows.append(jnp.where(slot < live, tile_ref[order_ref[slot]].astype(F32), 0.0))
        both = jnp.concatenate(rows, axis=0)
        out_ref[pl.ds(index * 128, 128), :] = both.T.astype(BF)
    out_ref[pl.ds(BODY, META), :] = meta.astype(F32).astype(BF)
    for copy in copies:
        copy.wait()


def pack(tile_orbital, tile_window, tile_count, tile_values, green_occ, green_virtual):
    smem = pl.BlockSpec(memory_space=pltpu.SMEM)
    vmem = pl.BlockSpec(memory_space=pltpu.VMEM)
    anywhere = pl.BlockSpec(memory_space=pl.ANY)
    return pl.pallas_call(
        pack_kernel,
        out_shape=(
            jax.ShapeDtypeStruct((PAY, 128), BF), jax.ShapeDtypeStruct((2 * PIECE, 2 * COLS), BF)
        ),
        in_specs=[smem, smem, smem, vmem, anywhere, anywhere],
        out_specs=(vmem, vmem),
        scratch_shapes=[pltpu.SMEM((TILES,), jnp.int32), pltpu.SemaphoreType.DMA((4,))],
    )(tile_orbital, tile_window, tile_count, tile_values, green_occ, green_virtual)


PART_OFFSETS = ((0, 4), (1, 5), (7, 3), (6, 2))


def chi_kernel(place_ref, meta_ref, *refs):
    tile_parts, green_parts = refs[:8], refs[8:16]
    keep_refs, send_ref = refs[16:20], refs[20]
    tiles_ref, green_ref, occ_ref, vir_ref, sems = refs[21:]
    my_z, my_y, my_x, my_core = place_ref[0], place_ref[1], place_ref[2], place_ref[3]

    copies = []
    for number, ref in enumerate(green_parts):
        for spot, offset in enumerate(PART_OFFSETS[number % 4]):
            start = pl.multiple_of(lax.rem(my_z + offset, 8) * PIECE, PIECE)
            lanes = number // 4 * 256
            copies.append((
                ref.at[pl.ds(spot * PIECE, PIECE)], green_ref.at[pl.ds(start, PIECE), pl.ds(lanes, 256)]
            ))
    for number, ref in enumerate(tile_parts):
        copies.append((ref, tiles_ref.at[pl.ds(number * PAY, PAY)]))
    copies = [pltpu.make_async_copy(source, target, sems.at[k]) for k, (source, target) in enumerate(copies)]
    for copy in copies:
        copy.start()
    occ_ref[...] = jnp.zeros_like(occ_ref)
    vir_ref[...] = jnp.zeros_like(vir_ref)
    for copy in copies:
        copy.wait()

    def rows_of(orbital):
        return green_ref[pl.ds(pl.multiple_of(orbital * BLK, BLK), BLK), :]

    def store(block, window, column):
        high, y, x = window // 8, lax.rem(window // 2, 4), lax.rem(window, 2)
        dy, dx = lax.rem(y - my_y + 4, 4), lax.rem(x - my_x + 2, 2)
        spot = ((dy * 2 + dx) * 2 + high) * 32
        vir_row = pl.multiple_of(window * BLK, BLK)
        for i in range(2):
            part = block[i * BLK:(i + 1) * BLK]
            occ = jnp.concatenate([part[:, 0:128], part[:, 256:384]], axis=1)
            vir = jnp.concatenate([part[:, 128:256], part[:, 384:512]], axis=1)
            vir_ref[pl.ds(vir_row, BLK), pl.ds(column + i * 256, 256)] = vir
            for core in range(2):
                row = pl.multiple_of(jnp.where(my_core == core, 0, 512) + spot, 32)
                occ_ref[pl.ds(row, 32), pl.ds(column + i * 256, 256)] = occ[core * 32:(core + 1) * 32]

    lane = lax.broadcasted_iota(jnp.int32, (1, 128), 1)
    low = jnp.where(lane < BLK, 1.0, 0.0).astype(BF)
    high = jnp.where(lane < BLK, 0.0, 1.0).astype(BF)
    blank = jnp.zeros((128, 128), BF)

    def slots_of(base, number, quads):
        column = pl.multiple_of(number * 512, 512)
        total = None
        for quad in range(quads):
            pair = [
                tiles_ref[pl.ds(pl.multiple_of(base + quad * 256 + k * 128, 16), 128), :] for k in range(2)
            ]
            stacked = jnp.concatenate([
                jnp.concatenate([pair[0] * low, blank], axis=1),
                jnp.concatenate([pair[0] * high, blank], axis=1),
                jnp.concatenate([blank, pair[1] * low], axis=1),
                jnp.concatenate([blank, pair[1] * high], axis=1),
            ], axis=0)
            slots = [4 * quad + t for t in range(4)]
            rows = jnp.concatenate([rows_of(meta_ref[number, TILES + slot]) for slot in slots], axis=0)
            product = jnp.dot(stacked, rows, preferred_element_type=F32)
            for t, slot in enumerate(slots):
                window = meta_ref[number, slot]
                fresh = product[t * 128:(t + 1) * 128]
                if total is None:
                    total = fresh
                else:
                    total = fresh + jnp.where(window == meta_ref[number, slot - 1], total, 0.0)
                store(total.astype(BF), window, column)

    @pl.loop(0, GROUPS)
    def _(number):
        base = number * PAY
        live = meta_ref[number, 2 * TILES]

        @pl.when(live <= 8)
        def _():
            slots_of(base, number, 2)

        @pl.when(live > 8)
        def _():
            slots_of(base, number, 4)

    def chi(row, rows):
        return lax.dot_general(
            occ_ref[pl.ds(row, rows), :], vir_ref[...], (((1,), (1,)), ((), ())), preferred_element_type=F32
        )

    send_ref[...] = chi(512, 512).astype(BF)
    product = chi(0, 512)
    for quarter in range(4):
        keep_refs[quarter][...] = product[quarter * 128:(quarter + 1) * 128]


def chi_call(place, meta, tiles, parts):
    smem = pl.BlockSpec(memory_space=pltpu.SMEM)
    vmem = pl.BlockSpec(memory_space=pltpu.VMEM)
    return pl.pallas_call(
        chi_kernel,
        out_shape=(jax.ShapeDtypeStruct((128, RW), F32),) * 4 + (jax.ShapeDtypeStruct((512, RW), BF),),
        in_specs=[smem, smem] + [pl.BlockSpec(memory_space=pl.ANY)] * 16,
        out_specs=(vmem,) * 5,
        scratch_shapes=[
            pltpu.VMEM((GROUPS * PAY, 128), BF),
            pltpu.VMEM((NAO, 512), BF),
            pltpu.VMEM((RW, DEPTH), BF),
            pltpu.VMEM((RW, DEPTH), BF),
            pltpu.SemaphoreType.DMA((24,)),
        ],
        compiler_params=pltpu.CompilerParams(vmem_limit_bytes=32 * 1024 * 1024),
        cost_estimate=pl.CostEstimate(flops=12 * 10**9, bytes_accessed=8 * 2**20, transcendentals=0),
    )(place, meta, *tiles, *parts)


def gather_tiles(payload):
    across = swap_x(payload)
    east, west = along_y(payload, 1), along_y(payload, -1)
    east_across, west_across = along_y(across, 1), along_y(across, -1)
    return payload, across, east, west, east_across, west_across, along_y(east, 1), along_y(west_across, -1)


def gather_green(pieces):
    first = permute(pieces, scatter_target)
    above, below = along_z(first, -1), along_z(first, 1)
    parts = (first, above, below, along_z(below, 1))
    return parts + tuple(swap_core(part) for part in parts)


def reduce_band(keeps, send):
    got = swap_core(send)
    parts = [got[quarter * 128:(quarter + 1) * 128] for quarter in range(4)]
    across = keeps[2] + parts[2].astype(F32)
    ahead = along_y(across[:64].astype(BF), 1)
    behind = along_y(across[64:].astype(BF), -1)
    one, three = keeps[1] + parts[1].astype(F32), keeps[3] + parts[3].astype(F32)
    up = jnp.concatenate([one[:64] + ahead.astype(F32), one[64:]], axis=0).astype(BF)
    down = jnp.concatenate([three[:64], three[64:] + behind.astype(F32)], axis=0).astype(BF)
    up, down = along_y(up, 1), along_y(down, -1)
    total = keeps[0] + parts[0].astype(F32) + up.astype(F32) + down.astype(F32)
    upper = total[:32] + swap_x(total[64:96].astype(BF)).astype(F32)
    lower = next_group(total[32:64].astype(BF), 0).astype(F32) + next_group(total[96:].astype(BF), 1).astype(F32)
    return jnp.concatenate([lower[:, :512], lower[:, 512:] + upper[:, :512], upper[:, 512:]], axis=1)


def per_device(green_occ, green_virtual, tile_values, tile_orbital, tile_window, tile_count):
    ao, pair = lax.axis_index("ao"), lax.axis_index("pair")
    x_hi, z, y, x_lo, core = device_of(ao * 16 + pair)
    place = jnp.stack([z, y, x_lo, core]).astype(jnp.int32)
    payload, pieces = pack(
        tile_orbital, tile_window, tile_count, tile_values, green_occ, green_virtual
    )
    tiles, parts = gather_tiles(payload), gather_green(pieces)
    rows = [part[BODY:BODY + 1, :64] for part in tiles]
    meta = jnp.concatenate(rows, axis=0).astype(jnp.int32)
    *keeps, send = chi_call(place, meta, tiles, parts)
    return reduce_band(keeps, send)


def solution(mesh):
    in_specs = (
        P(None, "ao"),
        P(None, "ao"),
        P(("ao", "pair"), None, None),
        P(("ao", "pair")),
        P(("ao", "pair")),
        P(("ao", "pair")),
    )
    out_specs = P(("ao", "pair"), None)
    return jax.shard_map(
        per_device, mesh=mesh, in_specs=in_specs, out_specs=out_specs, check_vma=False
    )
```

profile of v0, /device:TPU:6, one launch (start us, length us, event | category | flops | bytes accessed | tf_op | source)
XLA Modules:
  0.0 90.5 jit_solution(12367580746420630579)
XLA Ops:
  0.7 3.1 %shard_map.64 = (bf16[1040,128]{1,0:T(8,128)(2,1)}, bf16[512,256]{1,0:T(8,128)(2,1)}) custom-call(s32[16]{0:T(128)} %orbital_ref.1, s32[16]{0:T(128)} %window_ref.1, s32[1]{0:T(128)S(6)} %copy.7.count_ref, bf16[16,64,128]{2,1,0:T(8,128)(2,1)} %tile_ref.1, bf16[2048,128]{1,0:T(8,128)(2,1)} %occ_ref.1, bf16[2048,128]{1,0:T(8,128)(2,1)} %vir_ref.1), custom_call_target="tpu_custom_call" | custom-call | tf_op jit(solution)/shard_map/pallas_call | solution.py:134
  3.7 4.7 %collective-permute-start.7 = (bf16[512,256]{1,0:T(8,128)(2,1)}, bf16[512,256]{1,0:T(8,128)(2,1)S(1)}, u32[]{:S(2)}, u32[]{:S(2)}) collective-permute-start(bf16[512,256]{1,0:T(8,128)(2,1)} %get-tuple-element.13), channel_id=1, source_target_pairs={{0,48},{1,96},{2,176},{3,224},{4,16},{5,80},{6,144},{7,208},{8,112... | collective-permute-start | bytes 786440 | tf_op jit(solution)/shard_map/ppermute | solution.py:38
  8.4 0.8 collective-permute-start
  9.2 0.0 collective-permute-start.1
  9.2 5.2 %collective-permute-start.2 = (bf16[1040,128]{1,0:T(8,128)(2,1)}, bf16[1040,128]{1,0:T(8,128)(2,1)S(1)}, u32[]{:S(2)}, u32[]{:S(2)}) collective-permute-start(bf16[1040,128]{1,0:T(8,128)(2,1)} %get-tuple-element.12.refs_0_), channel_id=1, source_target_pairs={{0,12},{1,13},{2,14},{3,15},{4,0},{5,1},{6,2},{7,3},{8,4},{9,5},{1... | collective-permute-start | bytes 798728 | tf_op jit(solution)/shard_map/ppermute | solution.py:38
  14.5 0.0 collective-permute-done.7.refs_8_
  14.5 2.8 %collective-permute-start.9 = (bf16[512,256]{1,0:T(8,128)(2,1)S(1)}, bf16[512,256]{1,0:T(8,128)(2,1)S(1)}, u32[]{:S(2)}, u32[]{:S(2)}) collective-permute-start(bf16[512,256]{1,0:T(8,128)(2,1)S(1)} %collective-permute-done.7.refs_8_), channel_id=1, source_target_pairs={{0,16},{1,17},{2,18},{3,19},{4,20},{5,21},{6,22},{7,23},{8,24},{9,... | collective-permute-start | bytes 786440 | tf_op jit(solution)/shard_map/ppermute | solution.py:38
  17.2 0.0 collective-permute-done.refs_1_
  17.2 5.2 %collective-permute-start.4 = (bf16[1040,128]{1,0:T(8,128)(2,1)S(1)}, bf16[1040,128]{1,0:T(8,128)(2,1)S(1)}, u32[]{:S(2)}, u32[]{:S(2)}) collective-permute-start(bf16[1040,128]{1,0:T(8,128)(2,1)S(1)} %collective-permute-done.refs_1_), channel_id=1, source_target_pairs={{0,12},{1,13},{2,14},{3,15},{4,0},{5,1},{6,2},{7,3},{8,4},{9,5},{1... | collective-permute-start | bytes 798728 | tf_op jit(solution)/shard_map/ppermute | solution.py:38
  22.5 0.4 collective-permute-done.1.refs_2_
  22.9 0.0 collective-permute-start.5
  22.9 0.0 collective-permute-start.3
  22.9 0.0 collective-permute-done.2.refs_3_
  22.9 4.7 %collective-permute-start.8 = (bf16[512,256]{1,0:T(8,128)(2,1)S(1)}, bf16[512,256]{1,0:T(8,128)(2,1)S(1)}, u32[]{:S(2)}, u32[]{:S(2)}) collective-permute-start(bf16[512,256]{1,0:T(8,128)(2,1)S(1)} %collective-permute-done.7.refs_8_), channel_id=1, source_target_pairs={{0,112},{1,113},{2,114},{3,115},{4,116},{5,117},{6,118},{7,119},{8... | collective-permute-start | bytes 786440 | tf_op jit(solution)/shard_map/ppermute | solution.py:38
  27.6 4.9 %collective-permute-done.9.refs_10_ = bf16[512,256]{1,0:T(8,128)(2,1)S(1)} collective-permute-done((bf16[512,256]{1,0:T(8,128)(2,1)S(1)}, bf16[512,256]{1,0:T(8,128)(2,1)S(1)}, u32[]{:S(2)}, u32[]{:S(2)}) %collective-permute-start.9) | collective-permute-done | bytes 262176 | tf_op jit(solution)/shard_map/ppermute | solution.py:38
  32.5 0.0 collective-permute-start.10
  32.5 0.0 collective-permute-done.4.refs_5_
  32.5 0.1 collective-permute-start.6
  32.7 1.0 %collective-permute-done.8.refs_9_ = bf16[512,256]{1,0:T(8,128)(2,1)S(1)} collective-permute-done((bf16[512,256]{1,0:T(8,128)(2,1)S(1)}, bf16[512,256]{1,0:T(8,128)(2,1)S(1)}, u32[]{:S(2)}, u32[]{:S(2)}) %collective-permute-start.8) | collective-permute-done | bytes 262176 | tf_op jit(solution)/shard_map/ppermute | solution.py:38
  33.7 0.0 collective-permute-start.11
  33.7 0.0 collective-permute-done.5.refs_6_
  33.7 0.5 collective-permute-start.13
  34.2 4.6 %collective-permute-done.3.refs_4_ = bf16[1040,128]{1,0:T(8,128)(2,1)S(1)} collective-permute-done((bf16[1040,128]{1,0:T(8,128)(2,1)S(1)}, bf16[1040,128]{1,0:T(8,128)(2,1)S(1)}, u32[]{:S(2)}, u32[]{:S(2)}) %collective-permute-start.3) | collective-permute-done | bytes 266272 | tf_op jit(solution)/shard_map/ppermute | solution.py:38
  38.8 0.0 collective-permute-start.12
  38.8 3.4 %collective-permute-done.10.refs_11_ = bf16[512,256]{1,0:T(8,128)(2,1)S(1)} collective-permute-done((bf16[512,256]{1,0:T(8,128)(2,1)S(1)}, bf16[512,256]{1,0:T(8,128)(2,1)S(1)}, u32[]{:S(2)}, u32[]{:S(2)}) %collective-permute-start.10) | collective-permute-done | bytes 262176 | tf_op jit(solution)/shard_map/ppermute | solution.py:38
  42.2 0.0 collective-permute-start.14
  42.2 0.7 slice.85
  42.9 0.1 pad_add_fusion.place_ref
  43.0 0.0 collective-permute-done.6.refs_7_
  43.1 0.0 collective-permute-done.11.refs_12_
  43.1 0.0 collective-permute-done.13.refs_14_
  43.1 0.0 collective-permute-done.12.refs_13_
  43.1 0.8 collective-permute-done.14.refs_15_
  43.9 0.0 copy-start
  43.9 0.9 %copy-done = bf16[1040,128]{1,0:T(8,128)(2,1)S(1)} copy-done((bf16[1040,128]{1,0:T(8,128)(2,1)S(1)}, bf16[1040,128]{1,0:T(8,128)(2,1)}, u32[]{:S(2)}) %copy-start) | copy-done | bytes 266264
  44.9 15.6 %shard_map.65 = (f32[128,1024]{1,0:T(8,128)S(1)}, f32[128,1024]{1,0:T(8,128)S(1)}, f32[128,1024]{1,0:T(8,128)S(1)}, f32[128,1024]{1,0:T(8,128)S(1)}, bf16[512,1024]{1,0:T(8,128)(2,1)S(1)}) custom-call(s32[4]{0:T(128)S(1)} %pad_add_fusion.place_ref, s32[8,64]{1,0:T(8,128)S(1)} %convert_element_type.43.meta_ref, bf16[1040,128]{1,0:T(8,128)(2,1)S(1)} %copy-done, ...), custom_call_target="tpu_custom_call" | custom-call | flops 12000000000 | bytes 8388608 | tf_op jit(solution)/shard_map/pallas_call | solution.py:246
  60.5 0.2 collective-permute-start.15
  60.7 2.5 %collective-permute-done.15 = bf16[512,1024]{1,0:T(8,128)(2,1)S(1)} collective-permute-done((bf16[512,1024]{1,0:T(8,128)(2,1)S(1)}, bf16[512,1024]{1,0:T(8,128)(2,1)S(1)}, u32[]{:S(2)}, u32[]{:S(2)}) %collective-permute-start.15) | collective-permute-done | bytes 1048608 | tf_op jit(solution)/shard_map/ppermute | solution.py:38
  63.3 0.2 convert_add_fusion.2
  63.5 0.1 collective-permute-start.18
  63.7 2.3 %collective-permute-start.16 = (bf16[64,1024]{1,0:T(8,128)(2,1)S(1)}, bf16[64,1024]{1,0:T(8,128)(2,1)S(1)}, u32[]{:S(2)}, u32[]{:S(2)}) collective-permute-start(bf16[64,1024]{1,0:T(8,128)(2,1)S(1)} %get-tuple-element.27), channel_id=1, source_target_pairs={{0,4},{1,5},{2,6},{3,7},{4,8},{5,9},{6,10},{7,11},{8,12},{9,13},{1... | collective-permute-start | bytes 393224 | tf_op jit(solution)/shard_map/ppermute | solution.py:38
  66.0 3.2 %collective-permute-done.18 = bf16[64,1024]{1,0:T(8,128)(2,1)S(1)} collective-permute-done((bf16[64,1024]{1,0:T(8,128)(2,1)S(1)}, bf16[64,1024]{1,0:T(8,128)(2,1)S(1)}, u32[]{:S(2)}, u32[]{:S(2)}) %collective-permute-start.18) | collective-permute-done | bytes 131104 | tf_op jit(solution)/shard_map/ppermute | solution.py:38
  69.2 1.6 %collective-permute-start.19 = (bf16[128,1024]{1,0:T(8,128)(2,1)S(1)}, bf16[128,1024]{1,0:T(8,128)(2,1)S(1)}, u32[]{:S(2)}, u32[]{:S(2)}) collective-permute-start(bf16[128,1024]{1,0:T(8,128)(2,1)S(1)} %pad_maximum_fusion.1), channel_id=1, source_target_pairs={{0,12},{1,13},{2,14},{3,15},{4,0},{5,1},{6,2},{7,3},{8,4},{9,5},{1... | collective-permute-start | bytes 786440 | tf_op jit(solution)/shard_map/ppermute | solution.py:38
  70.8 0.0 collective-permute-done.16
  70.9 0.6 collective-permute-start.17
  71.5 5.3 %collective-permute-done.19 = bf16[128,1024]{1,0:T(8,128)(2,1)S(1)} collective-permute-done((bf16[128,1024]{1,0:T(8,128)(2,1)S(1)}, bf16[128,1024]{1,0:T(8,128)(2,1)S(1)}, u32[]{:S(2)}, u32[]{:S(2)}) %collective-permute-start.19) | collective-permute-done | bytes 262176 | tf_op jit(solution)/shard_map/ppermute | solution.py:38
  76.8 2.9 %collective-permute-done.17 = bf16[128,1024]{1,0:T(8,128)(2,1)S(1)} collective-permute-done((bf16[128,1024]{1,0:T(8,128)(2,1)S(1)}, bf16[128,1024]{1,0:T(8,128)(2,1)S(1)}, u32[]{:S(2)}, u32[]{:S(2)}) %collective-permute-start.17) | collective-permute-done | bytes 262176 | tf_op jit(solution)/shard_map/ppermute | solution.py:38
  79.7 0.2 fusion.2
  79.9 0.1 collective-permute-start.22
  80.0 0.1 collective-permute-start.20
  80.1 1.1 %collective-permute-start.21 = (bf16[32,1024]{1,0:T(8,128)(2,1)S(1)}, bf16[32,1024]{1,0:T(8,128)(2,1)S(1)}, u32[]{:S(2)}, u32[]{:S(2)}) collective-permute-start(bf16[32,1024]{1,0:T(8,128)(2,1)S(1)} %get-tuple-element.26), channel_id=1, source_target_pairs={{0,18},{1,19},{2,16},{3,17},{4,22},{5,23},{6,20},{7,21},{8,26},{9,... | collective-permute-start | bytes 196616 | tf_op jit(solution)/shard_map/ppermute | solution.py:38
  81.2 3.1 %collective-permute-done.22 = bf16[32,1024]{1,0:T(8,128)(2,1)S(1)} collective-permute-done((bf16[32,1024]{1,0:T(8,128)(2,1)S(1)}, bf16[32,1024]{1,0:T(8,128)(2,1)S(1)}, u32[]{:S(2)}, u32[]{:S(2)}) %collective-permute-start.22) | collective-permute-done | bytes 65568 | tf_op jit(solution)/shard_map/ppermute | solution.py:38
  84.3 3.7 %collective-permute-done.20 = bf16[32,1024]{1,0:T(8,128)(2,1)S(1)} collective-permute-done((bf16[32,1024]{1,0:T(8,128)(2,1)S(1)}, bf16[32,1024]{1,0:T(8,128)(2,1)S(1)}, u32[]{:S(2)}, u32[]{:S(2)}) %collective-permute-start.20) | collective-permute-done | bytes 65568 | tf_op jit(solution)/shard_map/ppermute | solution.py:38
  88.0 1.8 %collective-permute-done.21 = bf16[32,1024]{1,0:T(8,128)(2,1)S(1)} collective-permute-done((bf16[32,1024]{1,0:T(8,128)(2,1)S(1)}, bf16[32,1024]{1,0:T(8,128)(2,1)S(1)}, u32[]{:S(2)}, u32[]{:S(2)}) %collective-permute-start.21) | collective-permute-done | bytes 65568 | tf_op jit(solution)/shard_map/ppermute | solution.py:38
  89.8 0.7 pad_maximum_fusion.2
  (20 shorter events, 0.3 us)
Async XLA Ops:
  3.7 10.8 %collective-permute-start.7 = (bf16[512,256]{1,0:T(8,128)(2,1)}, bf16[512,256]{1,0:T(8,128)(2,1)S(1)}, u32[]{:S(2)}, u32[]{:S(2)}) collective-permute-start(bf16[512,256]{1,0:T(8,128)(2,1)} %get-tuple-element.13), channel_id=1, source_target_pairs={{0,48},{1,96},{2,176},{3,224},{4,16},{5,80},{6,144},{7,208},{8,112... | collective-permute-start | bytes 786440 | tf_op jit(solution)/shard_map/ppermute | solution.py:38
  8.4 8.8 %collective-permute-start = (bf16[1040,128]{1,0:T(8,128)(2,1)}, bf16[1040,128]{1,0:T(8,128)(2,1)S(1)}, u32[]{:S(2)}, u32[]{:S(2)}) collective-permute-start(bf16[1040,128]{1,0:T(8,128)(2,1)} %get-tuple-element.12.refs_0_), channel_id=1, source_target_pairs={{0,2},{1,3},{2,0},{3,1},{4,6},{5,7},{6,4},{7,5},{8,10},{9,11},{10,... | collective-permute-start | bytes 798728 | tf_op jit(solution)/shard_map/ppermute | solution.py:38
  9.2 13.7 %collective-permute-start.1 = (bf16[1040,128]{1,0:T(8,128)(2,1)}, bf16[1040,128]{1,0:T(8,128)(2,1)S(1)}, u32[]{:S(2)}, u32[]{:S(2)}) collective-permute-start(bf16[1040,128]{1,0:T(8,128)(2,1)} %get-tuple-element.12.refs_0_), channel_id=1, source_target_pairs={{0,4},{1,5},{2,6},{3,7},{4,8},{5,9},{6,10},{7,11},{8,12},{9,13},{1... | collective-permute-start | bytes 798728 | tf_op jit(solution)/shard_map/ppermute | solution.py:38
  9.2 13.7 %collective-permute-start.2 = (bf16[1040,128]{1,0:T(8,128)(2,1)}, bf16[1040,128]{1,0:T(8,128)(2,1)S(1)}, u32[]{:S(2)}, u32[]{:S(2)}) collective-permute-start(bf16[1040,128]{1,0:T(8,128)(2,1)} %get-tuple-element.12.refs_0_), channel_id=1, source_target_pairs={{0,12},{1,13},{2,14},{3,15},{4,0},{5,1},{6,2},{7,3},{8,4},{9,5},{1... | collective-permute-start | bytes 798728 | tf_op jit(solution)/shard_map/ppermute | solution.py:38
  14.5 18.0 %collective-permute-start.9 = (bf16[512,256]{1,0:T(8,128)(2,1)S(1)}, bf16[512,256]{1,0:T(8,128)(2,1)S(1)}, u32[]{:S(2)}, u32[]{:S(2)}) collective-permute-start(bf16[512,256]{1,0:T(8,128)(2,1)S(1)} %collective-permute-done.7.refs_8_), channel_id=1, source_target_pairs={{0,16},{1,17},{2,18},{3,19},{4,20},{5,21},{6,22},{7,23},{8,24},{9,... | collective-permute-start | bytes 786440 | tf_op jit(solution)/shard_map/ppermute | solution.py:38
  17.2 15.3 %collective-permute-start.4 = (bf16[1040,128]{1,0:T(8,128)(2,1)S(1)}, bf16[1040,128]{1,0:T(8,128)(2,1)S(1)}, u32[]{:S(2)}, u32[]{:S(2)}) collective-permute-start(bf16[1040,128]{1,0:T(8,128)(2,1)S(1)} %collective-permute-done.refs_1_), channel_id=1, source_target_pairs={{0,12},{1,13},{2,14},{3,15},{4,0},{5,1},{6,2},{7,3},{8,4},{9,5},{1... | collective-permute-start | bytes 798728 | tf_op jit(solution)/shard_map/ppermute | solution.py:38
  22.9 10.7 %collective-permute-start.5 = (bf16[1040,128]{1,0:T(8,128)(2,1)S(1)}, bf16[1040,128]{1,0:T(8,128)(2,1)S(1)}, u32[]{:S(2)}, u32[]{:S(2)}) collective-permute-start(bf16[1040,128]{1,0:T(8,128)(2,1)S(1)} %collective-permute-done.1.refs_2_), channel_id=1, source_target_pairs={{0,4},{1,5},{2,6},{3,7},{4,8},{5,9},{6,10},{7,11},{8,12},{9,13},{1... | collective-permute-start | bytes 798728 | tf_op jit(solution)/shard_map/ppermute | solution.py:38
  22.9 15.9 %collective-permute-start.3 = (bf16[1040,128]{1,0:T(8,128)(2,1)S(1)}, bf16[1040,128]{1,0:T(8,128)(2,1)S(1)}, u32[]{:S(2)}, u32[]{:S(2)}) collective-permute-start(bf16[1040,128]{1,0:T(8,128)(2,1)S(1)} %collective-permute-done.refs_1_), channel_id=1, source_target_pairs={{0,4},{1,5},{2,6},{3,7},{4,8},{5,9},{6,10},{7,11},{8,12},{9,13},{1... | collective-permute-start | bytes 798728 | tf_op jit(solution)/shard_map/ppermute | solution.py:38
  22.9 10.7 %collective-permute-start.8 = (bf16[512,256]{1,0:T(8,128)(2,1)S(1)}, bf16[512,256]{1,0:T(8,128)(2,1)S(1)}, u32[]{:S(2)}, u32[]{:S(2)}) collective-permute-start(bf16[512,256]{1,0:T(8,128)(2,1)S(1)} %collective-permute-done.7.refs_8_), channel_id=1, source_target_pairs={{0,112},{1,113},{2,114},{3,115},{4,116},{5,117},{6,118},{7,119},{8... | collective-permute-start | bytes 786440 | tf_op jit(solution)/shard_map/ppermute | solution.py:38
  32.5 9.7 %collective-permute-start.10 = (bf16[512,256]{1,0:T(8,128)(2,1)S(1)}, bf16[512,256]{1,0:T(8,128)(2,1)S(1)}, u32[]{:S(2)}, u32[]{:S(2)}) collective-permute-start(bf16[512,256]{1,0:T(8,128)(2,1)S(1)} %collective-permute-done.9.refs_10_), channel_id=1, source_target_pairs={{0,16},{1,17},{2,18},{3,19},{4,20},{5,21},{6,22},{7,23},{8,24},{9,... | collective-permute-start | bytes 786440 | tf_op jit(solution)/shard_map/ppermute | solution.py:38
  32.5 10.5 %collective-permute-start.6 = (bf16[1040,128]{1,0:T(8,128)(2,1)S(1)}, bf16[1040,128]{1,0:T(8,128)(2,1)S(1)}, u32[]{:S(2)}, u32[]{:S(2)}) collective-permute-start(bf16[1040,128]{1,0:T(8,128)(2,1)S(1)} %collective-permute-done.4.refs_5_), channel_id=1, source_target_pairs={{0,12},{1,13},{2,14},{3,15},{4,0},{5,1},{6,2},{7,3},{8,4},{9,5},{1... | collective-permute-start | bytes 798728 | tf_op jit(solution)/shard_map/ppermute | solution.py:38
  33.7 9.4 %collective-permute-start.11 = (bf16[512,256]{1,0:T(8,128)(2,1)S(1)}, bf16[512,256]{1,0:T(8,128)(2,1)S(1)}, u32[]{:S(2)}, u32[]{:S(2)}) collective-permute-start(bf16[512,256]{1,0:T(8,128)(2,1)S(1)} %collective-permute-done.7.refs_8_), channel_id=1, source_target_pairs={{0,1},{1,0},{2,3},{3,2},{4,5},{5,4},{6,7},{7,6},{8,9},{9,8},{10,11... | collective-permute-start | bytes 786440 | tf_op jit(solution)/shard_map/ppermute | solution.py:38
  33.7 9.4 %collective-permute-start.13 = (bf16[512,256]{1,0:T(8,128)(2,1)S(1)}, bf16[512,256]{1,0:T(8,128)(2,1)S(1)}, u32[]{:S(2)}, u32[]{:S(2)}) collective-permute-start(bf16[512,256]{1,0:T(8,128)(2,1)S(1)} %collective-permute-done.9.refs_10_), channel_id=1, source_target_pairs={{0,1},{1,0},{2,3},{3,2},{4,5},{5,4},{6,7},{7,6},{8,9},{9,8},{10,11... | collective-permute-start | bytes 786440 | tf_op jit(solution)/shard_map/ppermute | solution.py:38
  38.8 4.3 %collective-permute-start.12 = (bf16[512,256]{1,0:T(8,128)(2,1)S(1)}, bf16[512,256]{1,0:T(8,128)(2,1)}, u32[]{:S(2)}, u32[]{:S(2)}) collective-permute-start(bf16[512,256]{1,0:T(8,128)(2,1)S(1)} %collective-permute-done.8.refs_9_), channel_id=1, source_target_pairs={{0,1},{1,0},{2,3},{3,2},{4,5},{5,4},{6,7},{7,6},{8,9},{9,8},{10,11... | collective-permute-start | bytes 786440 | tf_op jit(solution)/shard_map/ppermute | solution.py:38
  42.2 1.7 %collective-permute-start.14 = (bf16[512,256]{1,0:T(8,128)(2,1)S(1)}, bf16[512,256]{1,0:T(8,128)(2,1)}, u32[]{:S(2)}, u32[]{:S(2)}) collective-permute-start(bf16[512,256]{1,0:T(8,128)(2,1)S(1)} %collective-permute-done.10.refs_11_), channel_id=1, source_target_pairs={{0,1},{1,0},{2,3},{3,2},{4,5},{5,4},{6,7},{7,6},{8,9},{9,8},{10,11... | collective-permute-start | bytes 786440 | tf_op jit(solution)/shard_map/ppermute | solution.py:38
  43.9 1.0 %copy-start = (bf16[1040,128]{1,0:T(8,128)(2,1)S(1)}, bf16[1040,128]{1,0:T(8,128)(2,1)}, u32[]{:S(2)}) copy-start(bf16[1040,128]{1,0:T(8,128)(2,1)} %get-tuple-element.12.refs_0_) | copy-start | bytes 798724
  60.5 2.7 %collective-permute-start.15 = (bf16[512,1024]{1,0:T(8,128)(2,1)S(1)}, bf16[512,1024]{1,0:T(8,128)(2,1)S(1)}, u32[]{:S(2)}, u32[]{:S(2)}) collective-permute-start(bf16[512,1024]{1,0:T(8,128)(2,1)S(1)} %get-tuple-element.15), channel_id=1, source_target_pairs={{0,1},{1,0},{2,3},{3,2},{4,5},{5,4},{6,7},{7,6},{8,9},{9,8},{10,11... | collective-permute-start | bytes 3145736 | tf_op jit(solution)/shard_map/ppermute | solution.py:38
  63.5 5.6 %collective-permute-start.18 = (bf16[64,1024]{1,0:T(8,128)(2,1)S(1)}, bf16[64,1024]{1,0:T(8,128)(2,1)S(1)}, u32[]{:S(2)}, u32[]{:S(2)}) collective-permute-start(bf16[64,1024]{1,0:T(8,128)(2,1)S(1)} %get-tuple-element.28), channel_id=1, source_target_pairs={{0,12},{1,13},{2,14},{3,15},{4,0},{5,1},{6,2},{7,3},{8,4},{9,5},{1... | collective-permute-start | bytes 393224 | tf_op jit(solution)/shard_map/ppermute | solution.py:38
  63.7 7.1 %collective-permute-start.16 = (bf16[64,1024]{1,0:T(8,128)(2,1)S(1)}, bf16[64,1024]{1,0:T(8,128)(2,1)S(1)}, u32[]{:S(2)}, u32[]{:S(2)}) collective-permute-start(bf16[64,1024]{1,0:T(8,128)(2,1)S(1)} %get-tuple-element.27), channel_id=1, source_target_pairs={{0,4},{1,5},{2,6},{3,7},{4,8},{5,9},{6,10},{7,11},{8,12},{9,13},{1... | collective-permute-start | bytes 393224 | tf_op jit(solution)/shard_map/ppermute | solution.py:38
  69.2 7.6 %collective-permute-start.19 = (bf16[128,1024]{1,0:T(8,128)(2,1)S(1)}, bf16[128,1024]{1,0:T(8,128)(2,1)S(1)}, u32[]{:S(2)}, u32[]{:S(2)}) collective-permute-start(bf16[128,1024]{1,0:T(8,128)(2,1)S(1)} %pad_maximum_fusion.1), channel_id=1, source_target_pairs={{0,12},{1,13},{2,14},{3,15},{4,0},{5,1},{6,2},{7,3},{8,4},{9,5},{1... | collective-permute-start | bytes 786440 | tf_op jit(solution)/shard_map/ppermute | solution.py:38
  70.9 8.8 %collective-permute-start.17 = (bf16[128,1024]{1,0:T(8,128)(2,1)S(1)}, bf16[128,1024]{1,0:T(8,128)(2,1)S(1)}, u32[]{:S(2)}, u32[]{:S(2)}) collective-permute-start(bf16[128,1024]{1,0:T(8,128)(2,1)S(1)} %pad_maximum_fusion), channel_id=1, source_target_pairs={{0,4},{1,5},{2,6},{3,7},{4,8},{5,9},{6,10},{7,11},{8,12},{9,13},{1... | collective-permute-start | bytes 786440 | tf_op jit(solution)/shard_map/ppermute | solution.py:38
  79.9 4.4 %collective-permute-start.22 = (bf16[32,1024]{1,0:T(8,128)(2,1)S(1)}, bf16[32,1024]{1,0:T(8,128)(2,1)S(1)}, u32[]{:S(2)}, u32[]{:S(2)}) collective-permute-start(bf16[32,1024]{1,0:T(8,128)(2,1)S(1)} %get-tuple-element.25), channel_id=1, source_target_pairs={{0,2},{1,3},{2,0},{3,1},{4,6},{5,7},{6,4},{7,5},{8,10},{9,11},{10,... | collective-permute-start | bytes 196616 | tf_op jit(solution)/shard_map/ppermute | solution.py:38
  80.0 8.0 %collective-permute-start.20 = (bf16[32,1024]{1,0:T(8,128)(2,1)S(1)}, bf16[32,1024]{1,0:T(8,128)(2,1)S(1)}, u32[]{:S(2)}, u32[]{:S(2)}) collective-permute-start(bf16[32,1024]{1,0:T(8,128)(2,1)S(1)} %get-tuple-element.24), channel_id=1, source_target_pairs={{0,16},{1,17},{2,18},{3,19},{4,20},{5,21},{6,22},{7,23},{8,24},{9,... | collective-permute-start | bytes 196616 | tf_op jit(solution)/shard_map/ppermute | solution.py:38
  80.1 9.6 %collective-permute-start.21 = (bf16[32,1024]{1,0:T(8,128)(2,1)S(1)}, bf16[32,1024]{1,0:T(8,128)(2,1)S(1)}, u32[]{:S(2)}, u32[]{:S(2)}) collective-permute-start(bf16[32,1024]{1,0:T(8,128)(2,1)S(1)} %get-tuple-element.26), channel_id=1, source_target_pairs={{0,18},{1,19},{2,16},{3,17},{4,22},{5,23},{6,20},{7,21},{8,26},{9,... | collective-permute-start | bytes 196616 | tf_op jit(solution)/shard_map/ppermute | solution.py:38
where the time goes:
time: 91.2 us; the launch traced here: 90.5 us
  waiting for transfers between devices  37.7 us (41%)
  starting transfers between devices  30.1 us (33%)
  Pallas kernels  18.7 us (21%)
  local copies, waits for them, and re-layouts  1.74 us (2%)
  other arithmetic  1.34 us (1%)
    ppermute x23, waiting for transfers between devices, permute(): return lax.ppermute(value, AXES, pairs)  37.7 us
    ppermute x23, starting transfers between devices, permute(): return lax.ppermute(value, AXES, pairs)  30.1 us
    pallas_call x1, Pallas kernels, chi_call(): pl.pallas_call(chi_kernel, out_shape=(jax.ShapeDtypeStruct((128, RW), F32...  15.6 us
    pallas_call x1, Pallas kernels, pack(): pl.pallas_call(pack_kernel, out_shape=(jax.ShapeDtypeStruct((PAY, 128), B...  3.07 us
  transfers between devices with their start and end apart: 23, of which 13 were waited for; matrix products, arithmetic and copies ran while one was open for 1% of the time, Pallas kernels for 0%

commit v1 on v0

--- a/solution.py
+++ b/solution.py
@@ -89,12 +89,25 @@
     return copies
 
 
-def pack_kernel(
-    orbital_ref, window_ref, count_ref, tile_ref, occ_ref, vir_ref, out_ref, piece_ref, order_ref, sems
-):
+def cut_kernel(occ_ref, vir_ref, piece_ref, sems):
     copies = piece_copies(occ_ref, vir_ref, piece_ref, sems)
     for copy in copies:
         copy.start()
+    for copy in copies:
+        copy.wait()
+
+
+def cut_pieces(green_occ, green_virtual):
+    return pl.pallas_call(
+        cut_kernel,
+        out_shape=jax.ShapeDtypeStruct((2 * PIECE, 2 * COLS), BF),
+        in_specs=[pl.BlockSpec(memory_space=pl.ANY)] * 2,
+        out_specs=pl.BlockSpec(memory_space=pltpu.VMEM),
+        scratch_shapes=[pltpu.SemaphoreType.DMA((4,))],
+    )(green_occ, green_virtual)
+
+
+def pack_kernel(orbital_ref, window_ref, count_ref, tile_ref, unused_ref, out_ref, order_ref):
     live = count_ref[0]
     windows = [window_ref[slot] for slot in range(TILES)]
     keys = [
@@ -123,33 +136,29 @@
         both = jnp.concatenate(rows, axis=0)
         out_ref[pl.ds(index * 128, 128), :] = both.T.astype(BF)
     out_ref[pl.ds(BODY, META), :] = meta.astype(F32).astype(BF)
-    for copy in copies:
-        copy.wait()
-
-
-def pack(tile_orbital, tile_window, tile_count, tile_values, green_occ, green_virtual):
+
+
+def pack(tile_orbital, tile_window, tile_count, tile_values, pieces):
     smem = pl.BlockSpec(memory_space=pltpu.SMEM)
     vmem = pl.BlockSpec(memory_space=pltpu.VMEM)
-    anywhere = pl.BlockSpec(memory_space=pl.ANY)
     return pl.pallas_call(
         pack_kernel,
-        out_shape=(
-            jax.ShapeDtypeStruct((PAY, 128), BF), jax.ShapeDtypeStruct((2 * PIECE, 2 * COLS), BF)
-        ),
-        in_specs=[smem, smem, smem, vmem, anywhere, anywhere],
-        out_specs=(vmem, vmem),
-        scratch_shapes=[pltpu.SMEM((TILES,), jnp.int32), pltpu.SemaphoreType.DMA((4,))],
-    )(tile_orbital, tile_window, tile_count, tile_values, green_occ, green_virtual)
+        out_shape=jax.ShapeDtypeStruct((PAY, 128), BF),
+        in_specs=[smem, smem, smem, vmem, pl.BlockSpec(memory_space=pl.ANY)],
+        out_specs=vmem,
+        scratch_shapes=[pltpu.SMEM((TILES,), jnp.int32)],
+    )(tile_orbital, tile_window, tile_count, tile_values, pieces)
 
 
 PART_OFFSETS = ((0, 4), (1, 5), (7, 3), (6, 2))
 
 
-def chi_kernel(place_ref, meta_ref, *refs):
+def chi_kernel(*refs):
     tile_parts, green_parts = refs[:8], refs[8:16]
     keep_refs, send_ref = refs[16:20], refs[20]
-    tiles_ref, green_ref, occ_ref, vir_ref, sems = refs[21:]
-    my_z, my_y, my_x, my_core = place_ref[0], place_ref[1], place_ref[2], place_ref[3]
+    tiles_ref, green_ref, occ_ref, vir_ref, flat_ref, meta_ref, sems = refs[21:]
+    ao, pair = lax.axis_index("ao"), lax.axis_index("pair")
+    my_z, my_y, my_x, my_core = lax.rem(ao, 8), pair // 4, lax.rem(pair // 2, 2), lax.rem(pair, 2)
 
     copies = []
     for number, ref in enumerate(green_parts):
@@ -165,9 +174,17 @@
     for copy in copies:
         copy.start()
     occ_ref[...] = jnp.zeros_like(occ_ref)
+    for copy in copies[16:]:
+        copy.wait()
+    for number in range(GROUPS):
+        head = tiles_ref[pl.ds(number * PAY + BODY, META), :].astype(F32).astype(jnp.int32)
+        flat_ref[pl.ds(number, 1), :] = head[:1]
+    to_scalars = pltpu.make_async_copy(flat_ref, meta_ref, sems.at[24])
+    to_scalars.start()
     vir_ref[...] = jnp.zeros_like(vir_ref)
-    for copy in copies:
+    for copy in copies[:16]:
         copy.wait()
+    to_scalars.wait()
 
     def rows_of(orbital):
         return green_ref[pl.ds(pl.multiple_of(orbital * BLK, BLK), BLK), :]
@@ -240,24 +257,25 @@
         keep_refs[quarter][...] = product[quarter * 128:(quarter + 1) * 128]
 
 
-def chi_call(place, meta, tiles, parts):
-    smem = pl.BlockSpec(memory_space=pltpu.SMEM)
+def chi_call(tiles, parts):
     vmem = pl.BlockSpec(memory_space=pltpu.VMEM)
     return pl.pallas_call(
         chi_kernel,
         out_shape=(jax.ShapeDtypeStruct((128, RW), F32),) * 4 + (jax.ShapeDtypeStruct((512, RW), BF),),
-        in_specs=[smem, smem] + [pl.BlockSpec(memory_space=pl.ANY)] * 16,
+        in_specs=[pl.BlockSpec(memory_space=pl.ANY)] * 16,
         out_specs=(vmem,) * 5,
         scratch_shapes=[
             pltpu.VMEM((GROUPS * PAY, 128), BF),
             pltpu.VMEM((NAO, 512), BF),
             pltpu.VMEM((RW, DEPTH), BF),
             pltpu.VMEM((RW, DEPTH), BF),
-            pltpu.SemaphoreType.DMA((24,)),
+            pltpu.VMEM((GROUPS, 128), jnp.int32),
+            pltpu.SMEM((GROUPS, 128), jnp.int32),
+            pltpu.SemaphoreType.DMA((25,)),
         ],
         compiler_params=pltpu.CompilerParams(vmem_limit_bytes=32 * 1024 * 1024),
         cost_estimate=pl.CostEstimate(flops=12 * 10**9, bytes_accessed=8 * 2**20, transcendentals=0),
-    )(place, meta, *tiles, *parts)
+    )(*tiles, *parts)
 
 
 def gather_tiles(payload):
@@ -291,16 +309,10 @@
 
 
 def per_device(green_occ, green_virtual, tile_values, tile_orbital, tile_window, tile_count):
-    ao, pair = lax.axis_index("ao"), lax.axis_index("pair")
-    x_hi, z, y, x_lo, core = device_of(ao * 16 + pair)
-    place = jnp.stack([z, y, x_lo, core]).astype(jnp.int32)
-    payload, pieces = pack(
-        tile_orbital, tile_window, tile_count, tile_values, green_occ, green_virtual
-    )
+    pieces = cut_pieces(green_occ, green_virtual)
+    payload = pack(tile_orbital, tile_window, tile_count, tile_values, pieces)
     tiles, parts = gather_tiles(payload), gather_green(pieces)
-    rows = [part[BODY:BODY + 1, :64] for part in tiles]
-    meta = jnp.concatenate(rows, axis=0).astype(jnp.int32)
-    *keeps, send = chi_call(place, meta, tiles, parts)
+    *keeps, send = chi_call(tiles, parts)
     return reduce_band(keeps, send)
 
 

time: 91.2 us -> 90.3 us (level)
  Pallas kernels: 18.7 us -> 19.7 us
    pallas_call x1 -> x2, Pallas kernels: 3.07 us -> 3.75 us  [the longest x1 2.07 us: pack(): pl.pallas_call(pack_kernel, out_shape=jax.ShapeDtypeStruct((PAY, 128), BF...]
  transfers between devices with their start and end apart: 23 -> 23, of which waited for: 13 -> 12; matrix products, arithmetic and copies ran while one was open for 1% -> 0% of each run, Pallas kernels for 0% -> 2%
where the time goes in v1:
time: 90.3 us; the launch traced here: 89.7 us
  waiting for transfers between devices  36.9 us (41%)
  starting transfers between devices  29.9 us (33%)
  Pallas kernels  19.7 us (22%)
  other arithmetic  1.3 us (1%)
  local copies, waits for them, and re-layouts  1.02 us (1%)
    ppermute x23, waiting for transfers between devices, permute(): return lax.ppermute(value, AXES, pairs)  36.9 us
    ppermute x23, starting transfers between devices, permute(): return lax.ppermute(value, AXES, pairs)  29.9 us
    pallas_call x1, Pallas kernels, chi_call(): pl.pallas_call(chi_kernel, out_shape=(jax.ShapeDtypeStruct((128, RW), F32...  15.9 us
    pallas_call x1, Pallas kernels, pack(): pl.pallas_call(pack_kernel, out_shape=jax.ShapeDtypeStruct((PAY, 128), BF...  2.07 us
  transfers between devices with their start and end apart: 23, of which 12 were waited for; matrix products, arithmetic and copies ran while one was open for 0% of the time, Pallas kernels for 2%

profile of v1, /device:TPU:6, one launch (start us, length us, event | category | flops | bytes accessed | tf_op | source)
XLA Modules:
  0.0 89.7 jit_solution(4875584877925041195)
XLA Ops:
  0.0 1.7 %shard_map.64.unused_ref = bf16[512,256]{1,0:T(8,128)(2,1)} custom-call(bf16[2048,128]{1,0:T(8,128)(2,1)} %occ_ref.1, bf16[2048,128]{1,0:T(8,128)(2,1)} %vir_ref.1), custom_call_target="tpu_custom_call" | custom-call | tf_op jit(solution)/shard_map/pallas_call | solution.py:101
  1.7 4.7 %collective-permute-start.7 = (bf16[512,256]{1,0:T(8,128)(2,1)}, bf16[512,256]{1,0:T(8,128)(2,1)S(1)}, u32[]{:S(2)}, u32[]{:S(2)}) collective-permute-start(bf16[512,256]{1,0:T(8,128)(2,1)} %shard_map.64.unused_ref), channel_id=1, source_target_pairs={{0,48},{1,96},{2,176},{3,224},{4,16},{5,80},{6,144},{7,208},{8,112... | collective-permute-start | bytes 786440 | tf_op jit(solution)/shard_map/ppermute | solution.py:38
  7.0 2.1 %shard_map.65.refs_0_ = bf16[1040,128]{1,0:T(8,128)(2,1)} custom-call(s32[16]{0:T(128)} %orbital_ref.1, s32[16]{0:T(128)} %window_ref.1, s32[1]{0:T(128)S(6)} %copy.7.count_ref, bf16[16,64,128]{2,1,0:T(8,128)(2,1)} %tile_ref.1, bf16[512,256]{1,0:T(8,128)(2,1)} %shard_map.64.unused_ref), custom_call_target="tpu_custom_call" | custom-call | tf_op jit(solution)/shard_map/pallas_call | solution.py:144
  9.1 0.8 collective-permute-start
  9.9 0.0 collective-permute-start.1
  9.9 5.2 %collective-permute-start.2 = (bf16[1040,128]{1,0:T(8,128)(2,1)}, bf16[1040,128]{1,0:T(8,128)(2,1)S(1)}, u32[]{:S(2)}, u32[]{:S(2)}) collective-permute-start(bf16[1040,128]{1,0:T(8,128)(2,1)} %shard_map.65.refs_0_), channel_id=1, source_target_pairs={{0,12},{1,13},{2,14},{3,15},{4,0},{5,1},{6,2},{7,3},{8,4},{9,5},{1... | collective-permute-start | bytes 798728 | tf_op jit(solution)/shard_map/ppermute | solution.py:38
  15.2 0.0 collective-permute-done.7.refs_8_
  15.2 2.6 %collective-permute-start.9 = (bf16[512,256]{1,0:T(8,128)(2,1)S(1)}, bf16[512,256]{1,0:T(8,128)(2,1)S(1)}, u32[]{:S(2)}, u32[]{:S(2)}) collective-permute-start(bf16[512,256]{1,0:T(8,128)(2,1)S(1)} %collective-permute-done.7.refs_8_), channel_id=1, source_target_pairs={{0,16},{1,17},{2,18},{3,19},{4,20},{5,21},{6,22},{7,23},{8,24},{9,... | collective-permute-start | bytes 786440 | tf_op jit(solution)/shard_map/ppermute | solution.py:38
  17.8 0.0 collective-permute-done.refs_1_
  17.8 3.2 %collective-permute-start.4 = (bf16[1040,128]{1,0:T(8,128)(2,1)S(1)}, bf16[1040,128]{1,0:T(8,128)(2,1)S(1)}, u32[]{:S(2)}, u32[]{:S(2)}) collective-permute-start(bf16[1040,128]{1,0:T(8,128)(2,1)S(1)} %collective-permute-done.refs_1_), channel_id=1, source_target_pairs={{0,12},{1,13},{2,14},{3,15},{4,0},{5,1},{6,2},{7,3},{8,4},{9,5},{1... | collective-permute-start | bytes 798728 | tf_op jit(solution)/shard_map/ppermute | solution.py:38
  21.0 0.6 collective-permute-start.11
  21.5 1.3 %collective-permute-done.1.refs_2_ = bf16[1040,128]{1,0:T(8,128)(2,1)S(1)} collective-permute-done((bf16[1040,128]{1,0:T(8,128)(2,1)}, bf16[1040,128]{1,0:T(8,128)(2,1)S(1)}, u32[]{:S(2)}, u32[]{:S(2)}) %collective-permute-start.1) | collective-permute-done | bytes 266272 | tf_op jit(solution)/shard_map/ppermute | solution.py:38
  22.8 0.4 collective-permute-start.5
  23.2 0.0 collective-permute-done.2.refs_3_
  23.2 3.0 %collective-permute-start.8 = (bf16[512,256]{1,0:T(8,128)(2,1)S(1)}, bf16[512,256]{1,0:T(8,128)(2,1)S(1)}, u32[]{:S(2)}, u32[]{:S(2)}) collective-permute-start(bf16[512,256]{1,0:T(8,128)(2,1)S(1)} %collective-permute-done.7.refs_8_), channel_id=1, source_target_pairs={{0,112},{1,113},{2,114},{3,115},{4,116},{5,117},{6,118},{7,119},{8... | collective-permute-start | bytes 786440 | tf_op jit(solution)/shard_map/ppermute | solution.py:38
  26.2 4.5 %collective-permute-done.9.refs_10_ = bf16[512,256]{1,0:T(8,128)(2,1)S(1)} collective-permute-done((bf16[512,256]{1,0:T(8,128)(2,1)S(1)}, bf16[512,256]{1,0:T(8,128)(2,1)S(1)}, u32[]{:S(2)}, u32[]{:S(2)}) %collective-permute-start.9) | collective-permute-done | bytes 262176 | tf_op jit(solution)/shard_map/ppermute | solution.py:38
  30.7 0.0 collective-permute-start.10
  30.7 0.0 collective-permute-done.11.refs_12_
  30.7 0.0 collective-permute-start.3
  30.7 0.0 collective-permute-done.4.refs_5_
  30.7 3.2 %collective-permute-start.6 = (bf16[1040,128]{1,0:T(8,128)(2,1)S(1)}, bf16[1040,128]{1,0:T(8,128)(2,1)S(1)}, u32[]{:S(2)}, u32[]{:S(2)}) collective-permute-start(bf16[1040,128]{1,0:T(8,128)(2,1)S(1)} %collective-permute-done.4.refs_5_), channel_id=1, source_target_pairs={{0,12},{1,13},{2,14},{3,15},{4,0},{5,1},{6,2},{7,3},{8,4},{9,5},{1... | collective-permute-start | bytes 798728 | tf_op jit(solution)/shard_map/ppermute | solution.py:38
  33.9 0.0 collective-permute-done.8.refs_9_
  33.9 0.0 collective-permute-start.13
  33.9 0.0 collective-permute-done.5.refs_6_
  33.9 0.5 collective-permute-start.12
  34.4 5.9 %collective-permute-done.10.refs_11_ = bf16[512,256]{1,0:T(8,128)(2,1)S(1)} collective-permute-done((bf16[512,256]{1,0:T(8,128)(2,1)S(1)}, bf16[512,256]{1,0:T(8,128)(2,1)S(1)}, u32[]{:S(2)}, u32[]{:S(2)}) %collective-permute-start.10) | collective-permute-done | bytes 262176 | tf_op jit(solution)/shard_map/ppermute | solution.py:38
  40.3 0.0 collective-permute-start.14
  40.3 0.1 collective-permute-done.3.refs_4_
  40.4 0.0 collective-permute-done.13.refs_14_
  40.4 0.0 collective-permute-done.12.refs_13_
  40.4 0.0 collective-permute-done.6.refs_7_
  40.4 1.4 %collective-permute-done.14.refs_15_ = bf16[512,256]{1,0:T(8,128)(2,1)S(1)} collective-permute-done((bf16[512,256]{1,0:T(8,128)(2,1)S(1)}, bf16[512,256]{1,0:T(8,128)(2,1)S(1)}, u32[]{:S(2)}, u32[]{:S(2)}) %collective-permute-start.14) | collective-permute-done | bytes 262176 | tf_op jit(solution)/shard_map/ppermute | solution.py:38
  41.8 0.0 copy-start
  41.8 0.9 %copy-done = bf16[1040,128]{1,0:T(8,128)(2,1)S(1)} copy-done((bf16[1040,128]{1,0:T(8,128)(2,1)S(1)}, bf16[1040,128]{1,0:T(8,128)(2,1)}, u32[]{:S(2)}) %copy-start) | copy-done | bytes 266264
  42.8 15.9 %shard_map.66 = (f32[128,1024]{1,0:T(8,128)S(1)}, f32[128,1024]{1,0:T(8,128)S(1)}, f32[128,1024]{1,0:T(8,128)S(1)}, f32[128,1024]{1,0:T(8,128)S(1)}, bf16[512,1024]{1,0:T(8,128)(2,1)S(1)}) custom-call(bf16[1040,128]{1,0:T(8,128)(2,1)S(1)} %copy-done, bf16[1040,128]{1,0:T(8,128)(2,1)S(1)} %collective-permute-done.refs_1_, ...), custom_call_target="tpu_custom_call" | custom-call | flops 12000000000 | bytes 8388608 | tf_op jit(solution)/shard_map/pallas_call | solution.py:262
  58.7 0.2 collective-permute-start.15
  58.9 2.5 %collective-permute-done.15 = bf16[512,1024]{1,0:T(8,128)(2,1)S(1)} collective-permute-done((bf16[512,1024]{1,0:T(8,128)(2,1)S(1)}, bf16[512,1024]{1,0:T(8,128)(2,1)S(1)}, u32[]{:S(2)}, u32[]{:S(2)}) %collective-permute-start.15) | collective-permute-done | bytes 1048608 | tf_op jit(solution)/shard_map/ppermute | solution.py:38
  61.5 0.3 convert_add_fusion.2
  61.8 1.6 %collective-permute-start.18 = (bf16[64,1024]{1,0:T(8,128)(2,1)S(1)}, bf16[64,1024]{1,0:T(8,128)(2,1)S(1)}, u32[]{:S(2)}, u32[]{:S(2)}) collective-permute-start(bf16[64,1024]{1,0:T(8,128)(2,1)S(1)} %get-tuple-element.24), channel_id=1, source_target_pairs={{0,12},{1,13},{2,14},{3,15},{4,0},{5,1},{6,2},{7,3},{8,4},{9,5},{1... | collective-permute-start | bytes 393224 | tf_op jit(solution)/shard_map/ppermute | solution.py:38
  63.5 0.8 collective-permute-start.16
  64.3 3.2 %collective-permute-done.18 = bf16[64,1024]{1,0:T(8,128)(2,1)S(1)} collective-permute-done((bf16[64,1024]{1,0:T(8,128)(2,1)S(1)}, bf16[64,1024]{1,0:T(8,128)(2,1)S(1)}, u32[]{:S(2)}, u32[]{:S(2)}) %collective-permute-start.18) | collective-permute-done | bytes 131104 | tf_op jit(solution)/shard_map/ppermute | solution.py:38
  67.5 2.8 %collective-permute-start.19 = (bf16[128,1024]{1,0:T(8,128)(2,1)S(1)}, bf16[128,1024]{1,0:T(8,128)(2,1)S(1)}, u32[]{:S(2)}, u32[]{:S(2)}) collective-permute-start(bf16[128,1024]{1,0:T(8,128)(2,1)S(1)} %pad_maximum_fusion.1), channel_id=1, source_target_pairs={{0,12},{1,13},{2,14},{3,15},{4,0},{5,1},{6,2},{7,3},{8,4},{9,5},{1... | collective-permute-start | bytes 786440 | tf_op jit(solution)/shard_map/ppermute | solution.py:38
  70.3 0.0 collective-permute-done.16
  70.4 0.1 collective-permute-start.17
  70.5 4.9 %collective-permute-done.19 = bf16[128,1024]{1,0:T(8,128)(2,1)S(1)} collective-permute-done((bf16[128,1024]{1,0:T(8,128)(2,1)S(1)}, bf16[128,1024]{1,0:T(8,128)(2,1)S(1)}, u32[]{:S(2)}, u32[]{:S(2)}) %collective-permute-start.19) | collective-permute-done | bytes 262176 | tf_op jit(solution)/shard_map/ppermute | solution.py:38
  75.4 3.6 %collective-permute-done.17 = bf16[128,1024]{1,0:T(8,128)(2,1)S(1)} collective-permute-done((bf16[128,1024]{1,0:T(8,128)(2,1)S(1)}, bf16[128,1024]{1,0:T(8,128)(2,1)S(1)}, u32[]{:S(2)}, u32[]{:S(2)}) %collective-permute-start.17) | collective-permute-done | bytes 262176 | tf_op jit(solution)/shard_map/ppermute | solution.py:38
  78.9 0.1 fusion.2
  79.1 0.1 collective-permute-start.22
  79.2 0.1 collective-permute-start.20
  79.3 0.1 collective-permute-start.21
  79.4 4.1 %collective-permute-done.22 = bf16[32,1024]{1,0:T(8,128)(2,1)S(1)} collective-permute-done((bf16[32,1024]{1,0:T(8,128)(2,1)S(1)}, bf16[32,1024]{1,0:T(8,128)(2,1)S(1)}, u32[]{:S(2)}, u32[]{:S(2)}) %collective-permute-start.22) | collective-permute-done | bytes 65568 | tf_op jit(solution)/shard_map/ppermute | solution.py:38
  83.5 3.7 %collective-permute-done.20 = bf16[32,1024]{1,0:T(8,128)(2,1)S(1)} collective-permute-done((bf16[32,1024]{1,0:T(8,128)(2,1)S(1)}, bf16[32,1024]{1,0:T(8,128)(2,1)S(1)}, u32[]{:S(2)}, u32[]{:S(2)}) %collective-permute-start.20) | collective-permute-done | bytes 65568 | tf_op jit(solution)/shard_map/ppermute | solution.py:38
  87.1 1.8 %collective-permute-done.21 = bf16[32,1024]{1,0:T(8,128)(2,1)S(1)} collective-permute-done((bf16[32,1024]{1,0:T(8,128)(2,1)S(1)}, bf16[32,1024]{1,0:T(8,128)(2,1)S(1)}, u32[]{:S(2)}, u32[]{:S(2)}) %collective-permute-start.21) | collective-permute-done | bytes 65568 | tf_op jit(solution)/shard_map/ppermute | solution.py:38
  89.0 0.7 pad_maximum_fusion.2
  (11 shorter events, 0.2 us)
Async XLA Ops:
  1.7 13.5 %collective-permute-start.7 = (bf16[512,256]{1,0:T(8,128)(2,1)}, bf16[512,256]{1,0:T(8,128)(2,1)S(1)}, u32[]{:S(2)}, u32[]{:S(2)}) collective-permute-start(bf16[512,256]{1,0:T(8,128)(2,1)} %shard_map.64.unused_ref), channel_id=1, source_target_pairs={{0,48},{1,96},{2,176},{3,224},{4,16},{5,80},{6,144},{7,208},{8,112... | collective-permute-start | bytes 786440 | tf_op jit(solution)/shard_map/ppermute | solution.py:38
  9.1 8.7 %collective-permute-start = (bf16[1040,128]{1,0:T(8,128)(2,1)}, bf16[1040,128]{1,0:T(8,128)(2,1)S(1)}, u32[]{:S(2)}, u32[]{:S(2)}) collective-permute-start(bf16[1040,128]{1,0:T(8,128)(2,1)} %shard_map.65.refs_0_), channel_id=1, source_target_pairs={{0,2},{1,3},{2,0},{3,1},{4,6},{5,7},{6,4},{7,5},{8,10},{9,11},{10,... | collective-permute-start | bytes 798728 | tf_op jit(solution)/shard_map/ppermute | solution.py:38
  9.9 12.9 %collective-permute-start.1 = (bf16[1040,128]{1,0:T(8,128)(2,1)}, bf16[1040,128]{1,0:T(8,128)(2,1)S(1)}, u32[]{:S(2)}, u32[]{:S(2)}) collective-permute-start(bf16[1040,128]{1,0:T(8,128)(2,1)} %shard_map.65.refs_0_), channel_id=1, source_target_pairs={{0,4},{1,5},{2,6},{3,7},{4,8},{5,9},{6,10},{7,11},{8,12},{9,13},{1... | collective-permute-start | bytes 798728 | tf_op jit(solution)/shard_map/ppermute | solution.py:38
  9.9 13.3 %collective-permute-start.2 = (bf16[1040,128]{1,0:T(8,128)(2,1)}, bf16[1040,128]{1,0:T(8,128)(2,1)S(1)}, u32[]{:S(2)}, u32[]{:S(2)}) collective-permute-start(bf16[1040,128]{1,0:T(8,128)(2,1)} %shard_map.65.refs_0_), channel_id=1, source_target_pairs={{0,12},{1,13},{2,14},{3,15},{4,0},{5,1},{6,2},{7,3},{8,4},{9,5},{1... | collective-permute-start | bytes 798728 | tf_op jit(solution)/shard_map/ppermute | solution.py:38
  15.2 15.5 %collective-permute-start.9 = (bf16[512,256]{1,0:T(8,128)(2,1)S(1)}, bf16[512,256]{1,0:T(8,128)(2,1)S(1)}, u32[]{:S(2)}, u32[]{:S(2)}) collective-permute-start(bf16[512,256]{1,0:T(8,128)(2,1)S(1)} %collective-permute-done.7.refs_8_), channel_id=1, source_target_pairs={{0,16},{1,17},{2,18},{3,19},{4,20},{5,21},{6,22},{7,23},{8,24},{9,... | collective-permute-start | bytes 786440 | tf_op jit(solution)/shard_map/ppermute | solution.py:38
  17.8 12.9 %collective-permute-start.4 = (bf16[1040,128]{1,0:T(8,128)(2,1)S(1)}, bf16[1040,128]{1,0:T(8,128)(2,1)S(1)}, u32[]{:S(2)}, u32[]{:S(2)}) collective-permute-start(bf16[1040,128]{1,0:T(8,128)(2,1)S(1)} %collective-permute-done.refs_1_), channel_id=1, source_target_pairs={{0,12},{1,13},{2,14},{3,15},{4,0},{5,1},{6,2},{7,3},{8,4},{9,5},{1... | collective-permute-start | bytes 798728 | tf_op jit(solution)/shard_map/ppermute | solution.py:38
  21.0 9.7 %collective-permute-start.11 = (bf16[512,256]{1,0:T(8,128)(2,1)S(1)}, bf16[512,256]{1,0:T(8,128)(2,1)S(1)}, u32[]{:S(2)}, u32[]{:S(2)}) collective-permute-start(bf16[512,256]{1,0:T(8,128)(2,1)S(1)} %collective-permute-done.7.refs_8_), channel_id=1, source_target_pairs={{0,1},{1,0},{2,3},{3,2},{4,5},{5,4},{6,7},{7,6},{8,9},{9,8},{10,11... | collective-permute-start | bytes 786440 | tf_op jit(solution)/shard_map/ppermute | solution.py:38
  22.8 11.1 %collective-permute-start.5 = (bf16[1040,128]{1,0:T(8,128)(2,1)S(1)}, bf16[1040,128]{1,0:T(8,128)(2,1)S(1)}, u32[]{:S(2)}, u32[]{:S(2)}) collective-permute-start(bf16[1040,128]{1,0:T(8,128)(2,1)S(1)} %collective-permute-done.1.refs_2_), channel_id=1, source_target_pairs={{0,4},{1,5},{2,6},{3,7},{4,8},{5,9},{6,10},{7,11},{8,12},{9,13},{1... | collective-permute-start | bytes 798728 | tf_op jit(solution)/shard_map/ppermute | solution.py:38
  23.2 10.7 %collective-permute-start.8 = (bf16[512,256]{1,0:T(8,128)(2,1)S(1)}, bf16[512,256]{1,0:T(8,128)(2,1)S(1)}, u32[]{:S(2)}, u32[]{:S(2)}) collective-permute-start(bf16[512,256]{1,0:T(8,128)(2,1)S(1)} %collective-permute-done.7.refs_8_), channel_id=1, source_target_pairs={{0,112},{1,113},{2,114},{3,115},{4,116},{5,117},{6,118},{7,119},{8... | collective-permute-start | bytes 786440 | tf_op jit(solution)/shard_map/ppermute | solution.py:38
  30.7 9.6 %collective-permute-start.10 = (bf16[512,256]{1,0:T(8,128)(2,1)S(1)}, bf16[512,256]{1,0:T(8,128)(2,1)S(1)}, u32[]{:S(2)}, u32[]{:S(2)}) collective-permute-start(bf16[512,256]{1,0:T(8,128)(2,1)S(1)} %collective-permute-done.9.refs_10_), channel_id=1, source_target_pairs={{0,16},{1,17},{2,18},{3,19},{4,20},{5,21},{6,22},{7,23},{8,24},{9,... | collective-permute-start | bytes 786440 | tf_op jit(solution)/shard_map/ppermute | solution.py:38
  30.7 9.7 %collective-permute-start.3 = (bf16[1040,128]{1,0:T(8,128)(2,1)S(1)}, bf16[1040,128]{1,0:T(8,128)(2,1)S(1)}, u32[]{:S(2)}, u32[]{:S(2)}) collective-permute-start(bf16[1040,128]{1,0:T(8,128)(2,1)S(1)} %collective-permute-done.refs_1_), channel_id=1, source_target_pairs={{0,4},{1,5},{2,6},{3,7},{4,8},{5,9},{6,10},{7,11},{8,12},{9,13},{1... | collective-permute-start | bytes 798728 | tf_op jit(solution)/shard_map/ppermute | solution.py:38
  30.7 9.7 %collective-permute-start.6 = (bf16[1040,128]{1,0:T(8,128)(2,1)S(1)}, bf16[1040,128]{1,0:T(8,128)(2,1)S(1)}, u32[]{:S(2)}, u32[]{:S(2)}) collective-permute-start(bf16[1040,128]{1,0:T(8,128)(2,1)S(1)} %collective-permute-done.4.refs_5_), channel_id=1, source_target_pairs={{0,12},{1,13},{2,14},{3,15},{4,0},{5,1},{6,2},{7,3},{8,4},{9,5},{1... | collective-permute-start | bytes 798728 | tf_op jit(solution)/shard_map/ppermute | solution.py:38
  33.9 6.5 %collective-permute-start.13 = (bf16[512,256]{1,0:T(8,128)(2,1)S(1)}, bf16[512,256]{1,0:T(8,128)(2,1)S(1)}, u32[]{:S(2)}, u32[]{:S(2)}) collective-permute-start(bf16[512,256]{1,0:T(8,128)(2,1)S(1)} %collective-permute-done.9.refs_10_), channel_id=1, source_target_pairs={{0,1},{1,0},{2,3},{3,2},{4,5},{5,4},{6,7},{7,6},{8,9},{9,8},{10,11... | collective-permute-start | bytes 786440 | tf_op jit(solution)/shard_map/ppermute | solution.py:38
  33.9 6.5 %collective-permute-start.12 = (bf16[512,256]{1,0:T(8,128)(2,1)S(1)}, bf16[512,256]{1,0:T(8,128)(2,1)S(1)}, u32[]{:S(2)}, u32[]{:S(2)}) collective-permute-start(bf16[512,256]{1,0:T(8,128)(2,1)S(1)} %collective-permute-done.8.refs_9_), channel_id=1, source_target_pairs={{0,1},{1,0},{2,3},{3,2},{4,5},{5,4},{6,7},{7,6},{8,9},{9,8},{10,11... | collective-permute-start | bytes 786440 | tf_op jit(solution)/shard_map/ppermute | solution.py:38
  40.3 1.5 %collective-permute-start.14 = (bf16[512,256]{1,0:T(8,128)(2,1)S(1)}, bf16[512,256]{1,0:T(8,128)(2,1)S(1)}, u32[]{:S(2)}, u32[]{:S(2)}) collective-permute-start(bf16[512,256]{1,0:T(8,128)(2,1)S(1)} %collective-permute-done.10.refs_11_), channel_id=1, source_target_pairs={{0,1},{1,0},{2,3},{3,2},{4,5},{5,4},{6,7},{7,6},{8,9},{9,8},{10,11... | collective-permute-start | bytes 786440 | tf_op jit(solution)/shard_map/ppermute | solution.py:38
  41.8 1.0 %copy-start = (bf16[1040,128]{1,0:T(8,128)(2,1)S(1)}, bf16[1040,128]{1,0:T(8,128)(2,1)}, u32[]{:S(2)}) copy-start(bf16[1040,128]{1,0:T(8,128)(2,1)} %shard_map.65.refs_0_) | copy-start | bytes 798724
  58.7 2.7 %collective-permute-start.15 = (bf16[512,1024]{1,0:T(8,128)(2,1)S(1)}, bf16[512,1024]{1,0:T(8,128)(2,1)S(1)}, u32[]{:S(2)}, u32[]{:S(2)}) collective-permute-start(bf16[512,1024]{1,0:T(8,128)(2,1)S(1)} %get-tuple-element.11), channel_id=1, source_target_pairs={{0,1},{1,0},{2,3},{3,2},{4,5},{5,4},{6,7},{7,6},{8,9},{9,8},{10,11... | collective-permute-start | bytes 3145736 | tf_op jit(solution)/shard_map/ppermute | solution.py:38
  61.8 5.6 %collective-permute-start.18 = (bf16[64,1024]{1,0:T(8,128)(2,1)S(1)}, bf16[64,1024]{1,0:T(8,128)(2,1)S(1)}, u32[]{:S(2)}, u32[]{:S(2)}) collective-permute-start(bf16[64,1024]{1,0:T(8,128)(2,1)S(1)} %get-tuple-element.24), channel_id=1, source_target_pairs={{0,12},{1,13},{2,14},{3,15},{4,0},{5,1},{6,2},{7,3},{8,4},{9,5},{1... | collective-permute-start | bytes 393224 | tf_op jit(solution)/shard_map/ppermute | solution.py:38
  63.5 6.9 %collective-permute-start.16 = (bf16[64,1024]{1,0:T(8,128)(2,1)S(1)}, bf16[64,1024]{1,0:T(8,128)(2,1)S(1)}, u32[]{:S(2)}, u32[]{:S(2)}) collective-permute-start(bf16[64,1024]{1,0:T(8,128)(2,1)S(1)} %get-tuple-element.23), channel_id=1, source_target_pairs={{0,4},{1,5},{2,6},{3,7},{4,8},{5,9},{6,10},{7,11},{8,12},{9,13},{1... | collective-permute-start | bytes 393224 | tf_op jit(solution)/shard_map/ppermute | solution.py:38
  67.5 7.9 %collective-permute-start.19 = (bf16[128,1024]{1,0:T(8,128)(2,1)S(1)}, bf16[128,1024]{1,0:T(8,128)(2,1)S(1)}, u32[]{:S(2)}, u32[]{:S(2)}) collective-permute-start(bf16[128,1024]{1,0:T(8,128)(2,1)S(1)} %pad_maximum_fusion.1), channel_id=1, source_target_pairs={{0,12},{1,13},{2,14},{3,15},{4,0},{5,1},{6,2},{7,3},{8,4},{9,5},{1... | collective-permute-start | bytes 786440 | tf_op jit(solution)/shard_map/ppermute | solution.py:38
  70.4 8.5 %collective-permute-start.17 = (bf16[128,1024]{1,0:T(8,128)(2,1)S(1)}, bf16[128,1024]{1,0:T(8,128)(2,1)S(1)}, u32[]{:S(2)}, u32[]{:S(2)}) collective-permute-start(bf16[128,1024]{1,0:T(8,128)(2,1)S(1)} %pad_maximum_fusion), channel_id=1, source_target_pairs={{0,4},{1,5},{2,6},{3,7},{4,8},{5,9},{6,10},{7,11},{8,12},{9,13},{1... | collective-permute-start | bytes 786440 | tf_op jit(solution)/shard_map/ppermute | solution.py:38
  79.1 4.4 %collective-permute-start.22 = (bf16[32,1024]{1,0:T(8,128)(2,1)S(1)}, bf16[32,1024]{1,0:T(8,128)(2,1)S(1)}, u32[]{:S(2)}, u32[]{:S(2)}) collective-permute-start(bf16[32,1024]{1,0:T(8,128)(2,1)S(1)} %get-tuple-element.21), channel_id=1, source_target_pairs={{0,2},{1,3},{2,0},{3,1},{4,6},{5,7},{6,4},{7,5},{8,10},{9,11},{10,... | collective-permute-start | bytes 196616 | tf_op jit(solution)/shard_map/ppermute | solution.py:38
  79.2 8.0 %collective-permute-start.20 = (bf16[32,1024]{1,0:T(8,128)(2,1)S(1)}, bf16[32,1024]{1,0:T(8,128)(2,1)S(1)}, u32[]{:S(2)}, u32[]{:S(2)}) collective-permute-start(bf16[32,1024]{1,0:T(8,128)(2,1)S(1)} %get-tuple-element.20), channel_id=1, source_target_pairs={{0,16},{1,17},{2,18},{3,19},{4,20},{5,21},{6,22},{7,23},{8,24},{9,... | collective-permute-start | bytes 196616 | tf_op jit(solution)/shard_map/ppermute | solution.py:38
  79.3 9.6 %collective-permute-start.21 = (bf16[32,1024]{1,0:T(8,128)(2,1)S(1)}, bf16[32,1024]{1,0:T(8,128)(2,1)S(1)}, u32[]{:S(2)}, u32[]{:S(2)}) collective-permute-start(bf16[32,1024]{1,0:T(8,128)(2,1)S(1)} %get-tuple-element.22), channel_id=1, source_target_pairs={{0,18},{1,19},{2,16},{3,17},{4,22},{5,23},{6,20},{7,21},{8,26},{9,... | collective-permute-start | bytes 196616 | tf_op jit(solution)/shard_map/ppermute | solution.py:38

commit v2 on v1

--- a/solution.py
+++ b/solution.py
@@ -143,7 +143,7 @@
     vmem = pl.BlockSpec(memory_space=pltpu.VMEM)
     return pl.pallas_call(
         pack_kernel,
-        out_shape=jax.ShapeDtypeStruct((PAY, 128), BF),
+        out_shape=pltpu.VMEM((PAY, 128), BF),
         in_specs=[smem, smem, smem, vmem, pl.BlockSpec(memory_space=pl.ANY)],
         out_specs=vmem,
         scratch_shapes=[pltpu.SMEM((TILES,), jnp.int32)],
@@ -155,8 +155,8 @@
 
 def chi_kernel(*refs):
     tile_parts, green_parts = refs[:8], refs[8:16]
-    keep_refs, send_ref = refs[16:20], refs[20]
-    tiles_ref, green_ref, occ_ref, vir_ref, flat_ref, meta_ref, sems = refs[21:]
+    send_ref, occ_ref, vir_ref = refs[16:19]
+    tiles_ref, green_ref, flat_ref, meta_ref, sems = refs[19:]
     ao, pair = lax.axis_index("ao"), lax.axis_index("pair")
     my_z, my_y, my_x, my_core = lax.rem(ao, 8), pair // 4, lax.rem(pair // 2, 2), lax.rem(pair, 2)
 
@@ -246,36 +246,49 @@
         def _():
             slots_of(base, number, 4)
 
-    def chi(row, rows):
-        return lax.dot_general(
-            occ_ref[pl.ds(row, rows), :], vir_ref[...], (((1,), (1,)), ((), ())), preferred_element_type=F32
-        )
-
-    send_ref[...] = chi(512, 512).astype(BF)
-    product = chi(0, 512)
+    send_ref[...] = chi_rows(occ_ref, vir_ref, 512).astype(BF)
+
+
+def chi_rows(occ_ref, vir_ref, row):
+    return lax.dot_general(
+        occ_ref[pl.ds(row, 512), :], vir_ref[...], (((1,), (1,)), ((), ())), preferred_element_type=F32
+    )
+
+
+def keep_kernel(occ_ref, vir_ref, *keep_refs):
+    product = chi_rows(occ_ref, vir_ref, 0)
     for quarter in range(4):
         keep_refs[quarter][...] = product[quarter * 128:(quarter + 1) * 128]
 
 
 def chi_call(tiles, parts):
     vmem = pl.BlockSpec(memory_space=pltpu.VMEM)
-    return pl.pallas_call(
+    send, occ, vir = pl.pallas_call(
         chi_kernel,
-        out_shape=(jax.ShapeDtypeStruct((128, RW), F32),) * 4 + (jax.ShapeDtypeStruct((512, RW), BF),),
+        out_shape=(
+            jax.ShapeDtypeStruct((512, RW), BF), pltpu.VMEM((RW, DEPTH), BF), pltpu.VMEM((RW, DEPTH), BF)
+        ),
         in_specs=[pl.BlockSpec(memory_space=pl.ANY)] * 16,
-        out_specs=(vmem,) * 5,
+        out_specs=(vmem,) * 3,
         scratch_shapes=[
             pltpu.VMEM((GROUPS * PAY, 128), BF),
             pltpu.VMEM((NAO, 512), BF),
-            pltpu.VMEM((RW, DEPTH), BF),
-            pltpu.VMEM((RW, DEPTH), BF),
             pltpu.VMEM((GROUPS, 128), jnp.int32),
             pltpu.SMEM((GROUPS, 128), jnp.int32),
             pltpu.SemaphoreType.DMA((25,)),
         ],
-        compiler_params=pltpu.CompilerParams(vmem_limit_bytes=32 * 1024 * 1024),
-        cost_estimate=pl.CostEstimate(flops=12 * 10**9, bytes_accessed=8 * 2**20, transcendentals=0),
+        compiler_params=pltpu.CompilerParams(vmem_limit_bytes=20 * 1024 * 1024),
+        cost_estimate=pl.CostEstimate(flops=8 * 10**9, bytes_accessed=8 * 2**20, transcendentals=0),
     )(*tiles, *parts)
+    keeps = pl.pallas_call(
+        keep_kernel,
+        out_shape=(jax.ShapeDtypeStruct((128, RW), F32),) * 4,
+        in_specs=[vmem, vmem],
+        out_specs=(vmem,) * 4,
+        compiler_params=pltpu.CompilerParams(vmem_limit_bytes=12 * 1024 * 1024),
+        cost_estimate=pl.CostEstimate(flops=4 * 10**9, bytes_accessed=4 * 2**20, transcendentals=0),
+    )(occ, vir)
+    return keeps, send
 
 
 def gather_tiles(payload):
@@ -312,7 +325,7 @@
     pieces = cut_pieces(green_occ, green_virtual)
     payload = pack(tile_orbital, tile_window, tile_count, tile_values, pieces)
     tiles, parts = gather_tiles(payload), gather_green(pieces)
-    *keeps, send = chi_call(tiles, parts)
+    keeps, send = chi_call(tiles, parts)
     return reduce_band(keeps, send)
 
 

time: 90.3 us -> 87.3 us (0.967)
  waiting for transfers between devices: 36.9 us -> 34.8 us
  starting transfers between devices: 29.9 us -> 31 us
  local copies, waits for them, and re-layouts: 1.02 us -> 0.07 us
    ppermute x23, waiting for transfers between devices: 36.9 us -> 34.8 us  [permute(): return lax.ppermute(value, AXES, pairs)]
    ppermute x23, starting transfers between devices: 29.9 us -> 31 us  [permute(): return lax.ppermute(value, AXES, pairs)]
    unnamed x2 -> x0, local copies, waits for them, and re-layouts: 0.95 us -> none
    pallas_call x2 -> x3, Pallas kernels: 18 us -> 17.8 us  [the longest x1 11.9 us: chi_call(): pl.pallas_call(chi_kernel, out_shape=(jax.ShapeDtypeStruct((512, RW), BF)...]
  transfers between devices with their start and end apart: 23 -> 23, of which waited for: 12 -> 11; matrix products, arithmetic and copies ran while one was open for 0% -> 0% of each run, Pallas kernels for 2% -> 7%
where the time goes in v2:
time: 87.3 us; the launch traced here: 87.4 us
  waiting for transfers between devices  34.8 us (40%)
  starting transfers between devices  31 us (36%)
  Pallas kernels  19.5 us (22%)
  other arithmetic  1.28 us (1%)
    ppermute x23, waiting for transfers between devices, permute(): return lax.ppermute(value, AXES, pairs)  34.8 us
    ppermute x23, starting transfers between devices, permute(): return lax.ppermute(value, AXES, pairs)  31 us
    pallas_call x1, Pallas kernels, chi_call(): pl.pallas_call(chi_kernel, out_shape=(jax.ShapeDtypeStruct((512, RW), BF)...  11.9 us
    pallas_call x1, Pallas kernels, chi_call(): pl.pallas_call(keep_kernel, out_shape=(jax.ShapeDtypeStruct((128, RW), F3...  4.52 us
  transfers between devices with their start and end apart: 23, of which 11 were waited for; matrix products, arithmetic and copies ran while one was open for 0% of the time, Pallas kernels for 7%

profile of v2, /device:TPU:6, one launch (start us, length us, event | category | flops | bytes accessed | tf_op | source)
XLA Modules:
  0.0 87.4 jit_solution(10153204399749116118)
XLA Ops:
  0.0 1.7 %shard_map.64.unused_ref = bf16[512,256]{1,0:T(8,128)(2,1)} custom-call(bf16[2048,128]{1,0:T(8,128)(2,1)} %occ_ref.1, bf16[2048,128]{1,0:T(8,128)(2,1)} %vir_ref.1), custom_call_target="tpu_custom_call" | custom-call | tf_op jit(solution)/shard_map/pallas_call | solution.py:101
  1.7 4.7 %collective-permute-start.7 = (bf16[512,256]{1,0:T(8,128)(2,1)}, bf16[512,256]{1,0:T(8,128)(2,1)S(1)}, u32[]{:S(2)}, u32[]{:S(2)}) collective-permute-start(bf16[512,256]{1,0:T(8,128)(2,1)} %shard_map.64.unused_ref), channel_id=1, source_target_pairs={{0,48},{1,96},{2,176},{3,224},{4,16},{5,80},{6,144},{7,208},{8,112... | collective-permute-start | bytes 786440 | tf_op jit(solution)/shard_map/ppermute | solution.py:38
  7.0 1.4 %shard_map.65.refs_0_ = bf16[1040,128]{1,0:T(8,128)(2,1)S(1)} custom-call(s32[16]{0:T(128)} %orbital_ref.1, s32[16]{0:T(128)} %window_ref.1, s32[1]{0:T(128)S(6)} %copy.7.count_ref, bf16[16,64,128]{2,1,0:T(8,128)(2,1)} %tile_ref.1, bf16[512,256]{1,0:T(8,128)(2,1)} %shard_map.64.unused_ref), custom_call_target="tpu_custom_call" | custom-call | tf_op jit(solution)/shard_map/pallas_call | solution.py:144
  8.4 0.9 %collective-permute-start = (bf16[1040,128]{1,0:T(8,128)(2,1)S(1)}, bf16[1040,128]{1,0:T(8,128)(2,1)S(1)}, u32[]{:S(2)}, u32[]{:S(2)}) collective-permute-start(bf16[1040,128]{1,0:T(8,128)(2,1)S(1)} %shard_map.65.refs_0_), channel_id=1, source_target_pairs={{0,2},{1,3},{2,0},{3,1},{4,6},{5,7},{6,4},{7,5},{8,10},{9,11},{10,... | collective-permute-start | bytes 798728 | tf_op jit(solution)/shard_map/ppermute | solution.py:38
  9.3 0.0 collective-permute-start.1
  9.3 5.2 %collective-permute-start.2 = (bf16[1040,128]{1,0:T(8,128)(2,1)S(1)}, bf16[1040,128]{1,0:T(8,128)(2,1)S(1)}, u32[]{:S(2)}, u32[]{:S(2)}) collective-permute-start(bf16[1040,128]{1,0:T(8,128)(2,1)S(1)} %shard_map.65.refs_0_), channel_id=1, source_target_pairs={{0,12},{1,13},{2,14},{3,15},{4,0},{5,1},{6,2},{7,3},{8,4},{9,5},{1... | collective-permute-start | bytes 798728 | tf_op jit(solution)/shard_map/ppermute | solution.py:38
  14.5 0.0 collective-permute-done.7.refs_8_
  14.5 2.6 %collective-permute-start.9 = (bf16[512,256]{1,0:T(8,128)(2,1)S(1)}, bf16[512,256]{1,0:T(8,128)(2,1)S(1)}, u32[]{:S(2)}, u32[]{:S(2)}) collective-permute-start(bf16[512,256]{1,0:T(8,128)(2,1)S(1)} %collective-permute-done.7.refs_8_), channel_id=1, source_target_pairs={{0,16},{1,17},{2,18},{3,19},{4,20},{5,21},{6,22},{7,23},{8,24},{9,... | collective-permute-start | bytes 786440 | tf_op jit(solution)/shard_map/ppermute | solution.py:38
  17.1 0.0 collective-permute-done.refs_1_
  17.1 3.3 %collective-permute-start.4 = (bf16[1040,128]{1,0:T(8,128)(2,1)S(1)}, bf16[1040,128]{1,0:T(8,128)(2,1)S(1)}, u32[]{:S(2)}, u32[]{:S(2)}) collective-permute-start(bf16[1040,128]{1,0:T(8,128)(2,1)S(1)} %collective-permute-done.refs_1_), channel_id=1, source_target_pairs={{0,12},{1,13},{2,14},{3,15},{4,0},{5,1},{6,2},{7,3},{8,4},{9,5},{1... | collective-permute-start | bytes 798728 | tf_op jit(solution)/shard_map/ppermute | solution.py:38
  20.4 1.1 %collective-permute-start.11 = (bf16[512,256]{1,0:T(8,128)(2,1)S(1)}, bf16[512,256]{1,0:T(8,128)(2,1)S(1)}, u32[]{:S(2)}, u32[]{:S(2)}) collective-permute-start(bf16[512,256]{1,0:T(8,128)(2,1)S(1)} %collective-permute-done.7.refs_8_), channel_id=1, source_target_pairs={{0,1},{1,0},{2,3},{3,2},{4,5},{5,4},{6,7},{7,6},{8,9},{9,8},{10,11... | collective-permute-start | bytes 786440 | tf_op jit(solution)/shard_map/ppermute | solution.py:38
  21.5 0.9 collective-permute-done.1.refs_2_
  22.4 0.8 collective-permute-start.5
  23.2 0.0 collective-permute-done.2.refs_3_
  23.2 3.0 %collective-permute-start.8 = (bf16[512,256]{1,0:T(8,128)(2,1)S(1)}, bf16[512,256]{1,0:T(8,128)(2,1)S(1)}, u32[]{:S(2)}, u32[]{:S(2)}) collective-permute-start(bf16[512,256]{1,0:T(8,128)(2,1)S(1)} %collective-permute-done.7.refs_8_), channel_id=1, source_target_pairs={{0,112},{1,113},{2,114},{3,115},{4,116},{5,117},{6,118},{7,119},{8... | collective-permute-start | bytes 786440 | tf_op jit(solution)/shard_map/ppermute | solution.py:38
  26.1 4.4 %collective-permute-done.9.refs_10_ = bf16[512,256]{1,0:T(8,128)(2,1)S(1)} collective-permute-done((bf16[512,256]{1,0:T(8,128)(2,1)S(1)}, bf16[512,256]{1,0:T(8,128)(2,1)S(1)}, u32[]{:S(2)}, u32[]{:S(2)}) %collective-permute-start.9) | collective-permute-done | bytes 262176 | tf_op jit(solution)/shard_map/ppermute | solution.py:38
  30.5 0.0 collective-permute-start.10
  30.5 0.0 collective-permute-done.11.refs_12_
  30.5 0.0 collective-permute-start.3
  30.5 0.0 collective-permute-done.4.refs_5_
  30.5 3.2 %collective-permute-start.6 = (bf16[1040,128]{1,0:T(8,128)(2,1)S(1)}, bf16[1040,128]{1,0:T(8,128)(2,1)S(1)}, u32[]{:S(2)}, u32[]{:S(2)}) collective-permute-start(bf16[1040,128]{1,0:T(8,128)(2,1)S(1)} %collective-permute-done.4.refs_5_), channel_id=1, source_target_pairs={{0,12},{1,13},{2,14},{3,15},{4,0},{5,1},{6,2},{7,3},{8,4},{9,5},{1... | collective-permute-start | bytes 798728 | tf_op jit(solution)/shard_map/ppermute | solution.py:38
  33.8 0.0 collective-permute-done.8.refs_9_
  33.8 0.0 collective-permute-start.13
  33.8 0.0 collective-permute-done.5.refs_6_
  33.8 0.5 collective-permute-start.12
  34.3 5.9 %collective-permute-done.10.refs_11_ = bf16[512,256]{1,0:T(8,128)(2,1)S(1)} collective-permute-done((bf16[512,256]{1,0:T(8,128)(2,1)S(1)}, bf16[512,256]{1,0:T(8,128)(2,1)S(1)}, u32[]{:S(2)}, u32[]{:S(2)}) %collective-permute-start.10) | collective-permute-done | bytes 262176 | tf_op jit(solution)/shard_map/ppermute | solution.py:38
  40.2 0.0 collective-permute-start.14
  40.2 0.1 collective-permute-done.3.refs_4_
  40.3 0.0 collective-permute-done.13.refs_14_
  40.3 0.0 collective-permute-done.12.refs_13_
  40.3 0.0 collective-permute-done.6.refs_7_
  40.3 1.4 %collective-permute-done.14.refs_15_ = bf16[512,256]{1,0:T(8,128)(2,1)S(1)} collective-permute-done((bf16[512,256]{1,0:T(8,128)(2,1)S(1)}, bf16[512,256]{1,0:T(8,128)(2,1)S(1)}, u32[]{:S(2)}, u32[]{:S(2)}) %collective-permute-start.14) | collective-permute-done | bytes 262176 | tf_op jit(solution)/shard_map/ppermute | solution.py:38
  41.7 11.9 %shard_map.66 = (bf16[512,1024]{1,0:T(8,128)(2,1)S(1)}, bf16[1024,4096]{1,0:T(8,128)(2,1)S(1)}, bf16[1024,4096]{1,0:T(8,128)(2,1)S(1)}) custom-call(bf16[1040,128]{1,0:T(8,128)(2,1)S(1)} %shard_map.65.refs_0_, bf16[1040,128]{1,0:T(8,128)(2,1)S(1)} %collective-permute-done.refs_1_, bf16[1040,128]{1,0:T(8,128)(2,1)S(1)} %collective-permute-done.1.refs_2_, ...), custom_call_target="tpu_custom_call" | custom-call | flops 8000000000 | bytes 8388608 | tf_op jit(solution)/shard_map/pallas_call | solution.py:266
  53.7 0.1 collective-permute-start.15
  53.8 4.5 %shard_map.67 = (f32[128,1024]{1,0:T(8,128)S(1)}, f32[128,1024]{1,0:T(8,128)S(1)}, f32[128,1024]{1,0:T(8,128)S(1)}, f32[128,1024]{1,0:T(8,128)S(1)}) custom-call(bf16[1024,4096]{1,0:T(8,128)(2,1)S(1)} %get-tuple-element.12.occ_ref, bf16[1024,4096]{1,0:T(8,128)(2,1)S(1)} %get-tuple-element.13.vir_ref), custom_call_target="tpu_custom_call" | custom-call | flops 4000000000 | bytes 4194304 | tf_op jit(solution)/shard_map/pallas_call | solution.py:283
  58.3 0.0 collective-permute-done.15
  58.3 0.3 convert_add_fusion.2
  58.6 1.6 %collective-permute-start.18 = (bf16[64,1024]{1,0:T(8,128)(2,1)S(1)}, bf16[64,1024]{1,0:T(8,128)(2,1)S(1)}, u32[]{:S(2)}, u32[]{:S(2)}) collective-permute-start(bf16[64,1024]{1,0:T(8,128)(2,1)S(1)} %get-tuple-element.28), channel_id=1, source_target_pairs={{0,12},{1,13},{2,14},{3,15},{4,0},{5,1},{6,2},{7,3},{8,4},{9,5},{1... | collective-permute-start | bytes 393224 | tf_op jit(solution)/shard_map/ppermute | solution.py:38
  60.3 0.8 collective-permute-start.16
  61.1 3.5 %collective-permute-done.18 = bf16[64,1024]{1,0:T(8,128)(2,1)S(1)} collective-permute-done((bf16[64,1024]{1,0:T(8,128)(2,1)S(1)}, bf16[64,1024]{1,0:T(8,128)(2,1)S(1)}, u32[]{:S(2)}, u32[]{:S(2)}) %collective-permute-start.18) | collective-permute-done | bytes 131104 | tf_op jit(solution)/shard_map/ppermute | solution.py:38
  64.7 2.8 %collective-permute-start.19 = (bf16[128,1024]{1,0:T(8,128)(2,1)S(1)}, bf16[128,1024]{1,0:T(8,128)(2,1)S(1)}, u32[]{:S(2)}, u32[]{:S(2)}) collective-permute-start(bf16[128,1024]{1,0:T(8,128)(2,1)S(1)} %pad_maximum_fusion.1), channel_id=1, source_target_pairs={{0,12},{1,13},{2,14},{3,15},{4,0},{5,1},{6,2},{7,3},{8,4},{9,5},{1... | collective-permute-start | bytes 786440 | tf_op jit(solution)/shard_map/ppermute | solution.py:38
  67.5 0.0 collective-permute-done.16
  67.5 0.1 collective-permute-start.17
  67.6 5.3 %collective-permute-done.19 = bf16[128,1024]{1,0:T(8,128)(2,1)S(1)} collective-permute-done((bf16[128,1024]{1,0:T(8,128)(2,1)S(1)}, bf16[128,1024]{1,0:T(8,128)(2,1)S(1)}, u32[]{:S(2)}, u32[]{:S(2)}) %collective-permute-start.19) | collective-permute-done | bytes 262176 | tf_op jit(solution)/shard_map/ppermute | solution.py:38
  72.9 3.6 %collective-permute-done.17 = bf16[128,1024]{1,0:T(8,128)(2,1)S(1)} collective-permute-done((bf16[128,1024]{1,0:T(8,128)(2,1)S(1)}, bf16[128,1024]{1,0:T(8,128)(2,1)S(1)}, u32[]{:S(2)}, u32[]{:S(2)}) %collective-permute-start.17) | collective-permute-done | bytes 262176 | tf_op jit(solution)/shard_map/ppermute | solution.py:38
  76.5 0.2 fusion.2
  76.7 0.1 collective-permute-start.22
  76.8 0.1 collective-permute-start.20
  76.9 0.1 collective-permute-start.21
  76.9 4.8 %collective-permute-done.22 = bf16[32,1024]{1,0:T(8,128)(2,1)S(1)} collective-permute-done((bf16[32,1024]{1,0:T(8,128)(2,1)S(1)}, bf16[32,1024]{1,0:T(8,128)(2,1)S(1)}, u32[]{:S(2)}, u32[]{:S(2)}) %collective-permute-start.22) | collective-permute-done | bytes 65568 | tf_op jit(solution)/shard_map/ppermute | solution.py:38
  81.7 3.8 %collective-permute-done.20 = bf16[32,1024]{1,0:T(8,128)(2,1)S(1)} collective-permute-done((bf16[32,1024]{1,0:T(8,128)(2,1)S(1)}, bf16[32,1024]{1,0:T(8,128)(2,1)S(1)}, u32[]{:S(2)}, u32[]{:S(2)}) %collective-permute-start.20) | collective-permute-done | bytes 65568 | tf_op jit(solution)/shard_map/ppermute | solution.py:38
  85.5 1.2 %collective-permute-done.21 = bf16[32,1024]{1,0:T(8,128)(2,1)S(1)} collective-permute-done((bf16[32,1024]{1,0:T(8,128)(2,1)S(1)}, bf16[32,1024]{1,0:T(8,128)(2,1)S(1)}, u32[]{:S(2)}, u32[]{:S(2)}) %collective-permute-start.21) | collective-permute-done | bytes 65568 | tf_op jit(solution)/shard_map/ppermute | solution.py:38
  86.7 0.7 pad_maximum_fusion.2
  (11 shorter events, 0.2 us)
Async XLA Ops:
  1.7 12.9 %collective-permute-start.7 = (bf16[512,256]{1,0:T(8,128)(2,1)}, bf16[512,256]{1,0:T(8,128)(2,1)S(1)}, u32[]{:S(2)}, u32[]{:S(2)}) collective-permute-start(bf16[512,256]{1,0:T(8,128)(2,1)} %shard_map.64.unused_ref), channel_id=1, source_target_pairs={{0,48},{1,96},{2,176},{3,224},{4,16},{5,80},{6,144},{7,208},{8,112... | collective-permute-start | bytes 786440 | tf_op jit(solution)/shard_map/ppermute | solution.py:38
  8.4 8.7 %collective-permute-start = (bf16[1040,128]{1,0:T(8,128)(2,1)S(1)}, bf16[1040,128]{1,0:T(8,128)(2,1)S(1)}, u32[]{:S(2)}, u32[]{:S(2)}) collective-permute-start(bf16[1040,128]{1,0:T(8,128)(2,1)S(1)} %shard_map.65.refs_0_), channel_id=1, source_target_pairs={{0,2},{1,3},{2,0},{3,1},{4,6},{5,7},{6,4},{7,5},{8,10},{9,11},{10,... | collective-permute-start | bytes 798728 | tf_op jit(solution)/shard_map/ppermute | solution.py:38
  9.3 13.1 %collective-permute-start.1 = (bf16[1040,128]{1,0:T(8,128)(2,1)S(1)}, bf16[1040,128]{1,0:T(8,128)(2,1)S(1)}, u32[]{:S(2)}, u32[]{:S(2)}) collective-permute-start(bf16[1040,128]{1,0:T(8,128)(2,1)S(1)} %shard_map.65.refs_0_), channel_id=1, source_target_pairs={{0,4},{1,5},{2,6},{3,7},{4,8},{5,9},{6,10},{7,11},{8,12},{9,13},{1... | collective-permute-start | bytes 798728 | tf_op jit(solution)/shard_map/ppermute | solution.py:38
  9.3 13.9 %collective-permute-start.2 = (bf16[1040,128]{1,0:T(8,128)(2,1)S(1)}, bf16[1040,128]{1,0:T(8,128)(2,1)S(1)}, u32[]{:S(2)}, u32[]{:S(2)}) collective-permute-start(bf16[1040,128]{1,0:T(8,128)(2,1)S(1)} %shard_map.65.refs_0_), channel_id=1, source_target_pairs={{0,12},{1,13},{2,14},{3,15},{4,0},{5,1},{6,2},{7,3},{8,4},{9,5},{1... | collective-permute-start | bytes 798728 | tf_op jit(solution)/shard_map/ppermute | solution.py:38
  14.5 16.0 %collective-permute-start.9 = (bf16[512,256]{1,0:T(8,128)(2,1)S(1)}, bf16[512,256]{1,0:T(8,128)(2,1)S(1)}, u32[]{:S(2)}, u32[]{:S(2)}) collective-permute-start(bf16[512,256]{1,0:T(8,128)(2,1)S(1)} %collective-permute-done.7.refs_8_), channel_id=1, source_target_pairs={{0,16},{1,17},{2,18},{3,19},{4,20},{5,21},{6,22},{7,23},{8,24},{9,... | collective-permute-start | bytes 786440 | tf_op jit(solution)/shard_map/ppermute | solution.py:38
  17.1 13.4 %collective-permute-start.4 = (bf16[1040,128]{1,0:T(8,128)(2,1)S(1)}, bf16[1040,128]{1,0:T(8,128)(2,1)S(1)}, u32[]{:S(2)}, u32[]{:S(2)}) collective-permute-start(bf16[1040,128]{1,0:T(8,128)(2,1)S(1)} %collective-permute-done.refs_1_), channel_id=1, source_target_pairs={{0,12},{1,13},{2,14},{3,15},{4,0},{5,1},{6,2},{7,3},{8,4},{9,5},{1... | collective-permute-start | bytes 798728 | tf_op jit(solution)/shard_map/ppermute | solution.py:38
  20.4 10.1 %collective-permute-start.11 = (bf16[512,256]{1,0:T(8,128)(2,1)S(1)}, bf16[512,256]{1,0:T(8,128)(2,1)S(1)}, u32[]{:S(2)}, u32[]{:S(2)}) collective-permute-start(bf16[512,256]{1,0:T(8,128)(2,1)S(1)} %collective-permute-done.7.refs_8_), channel_id=1, source_target_pairs={{0,1},{1,0},{2,3},{3,2},{4,5},{5,4},{6,7},{7,6},{8,9},{9,8},{10,11... | collective-permute-start | bytes 786440 | tf_op jit(solution)/shard_map/ppermute | solution.py:38
  22.4 11.4 %collective-permute-start.5 = (bf16[1040,128]{1,0:T(8,128)(2,1)S(1)}, bf16[1040,128]{1,0:T(8,128)(2,1)S(1)}, u32[]{:S(2)}, u32[]{:S(2)}) collective-permute-start(bf16[1040,128]{1,0:T(8,128)(2,1)S(1)} %collective-permute-done.1.refs_2_), channel_id=1, source_target_pairs={{0,4},{1,5},{2,6},{3,7},{4,8},{5,9},{6,10},{7,11},{8,12},{9,13},{1... | collective-permute-start | bytes 798728 | tf_op jit(solution)/shard_map/ppermute | solution.py:38
  23.2 10.6 %collective-permute-start.8 = (bf16[512,256]{1,0:T(8,128)(2,1)S(1)}, bf16[512,256]{1,0:T(8,128)(2,1)S(1)}, u32[]{:S(2)}, u32[]{:S(2)}) collective-permute-start(bf16[512,256]{1,0:T(8,128)(2,1)S(1)} %collective-permute-done.7.refs_8_), channel_id=1, source_target_pairs={{0,112},{1,113},{2,114},{3,115},{4,116},{5,117},{6,118},{7,119},{8... | collective-permute-start | bytes 786440 | tf_op jit(solution)/shard_map/ppermute | solution.py:38
  30.5 9.7 %collective-permute-start.10 = (bf16[512,256]{1,0:T(8,128)(2,1)S(1)}, bf16[512,256]{1,0:T(8,128)(2,1)S(1)}, u32[]{:S(2)}, u32[]{:S(2)}) collective-permute-start(bf16[512,256]{1,0:T(8,128)(2,1)S(1)} %collective-permute-done.9.refs_10_), channel_id=1, source_target_pairs={{0,16},{1,17},{2,18},{3,19},{4,20},{5,21},{6,22},{7,23},{8,24},{9,... | collective-permute-start | bytes 786440 | tf_op jit(solution)/shard_map/ppermute | solution.py:38
  30.5 9.8 %collective-permute-start.3 = (bf16[1040,128]{1,0:T(8,128)(2,1)S(1)}, bf16[1040,128]{1,0:T(8,128)(2,1)S(1)}, u32[]{:S(2)}, u32[]{:S(2)}) collective-permute-start(bf16[1040,128]{1,0:T(8,128)(2,1)S(1)} %collective-permute-done.refs_1_), channel_id=1, source_target_pairs={{0,4},{1,5},{2,6},{3,7},{4,8},{5,9},{6,10},{7,11},{8,12},{9,13},{1... | collective-permute-start | bytes 798728 | tf_op jit(solution)/shard_map/ppermute | solution.py:38
  30.5 9.8 %collective-permute-start.6 = (bf16[1040,128]{1,0:T(8,128)(2,1)S(1)}, bf16[1040,128]{1,0:T(8,128)(2,1)S(1)}, u32[]{:S(2)}, u32[]{:S(2)}) collective-permute-start(bf16[1040,128]{1,0:T(8,128)(2,1)S(1)} %collective-permute-done.4.refs_5_), channel_id=1, source_target_pairs={{0,12},{1,13},{2,14},{3,15},{4,0},{5,1},{6,2},{7,3},{8,4},{9,5},{1... | collective-permute-start | bytes 798728 | tf_op jit(solution)/shard_map/ppermute | solution.py:38
  33.8 6.6 %collective-permute-start.13 = (bf16[512,256]{1,0:T(8,128)(2,1)S(1)}, bf16[512,256]{1,0:T(8,128)(2,1)S(1)}, u32[]{:S(2)}, u32[]{:S(2)}) collective-permute-start(bf16[512,256]{1,0:T(8,128)(2,1)S(1)} %collective-permute-done.9.refs_10_), channel_id=1, source_target_pairs={{0,1},{1,0},{2,3},{3,2},{4,5},{5,4},{6,7},{7,6},{8,9},{9,8},{10,11... | collective-permute-start | bytes 786440 | tf_op jit(solution)/shard_map/ppermute | solution.py:38
  33.8 6.5 %collective-permute-start.12 = (bf16[512,256]{1,0:T(8,128)(2,1)S(1)}, bf16[512,256]{1,0:T(8,128)(2,1)S(1)}, u32[]{:S(2)}, u32[]{:S(2)}) collective-permute-start(bf16[512,256]{1,0:T(8,128)(2,1)S(1)} %collective-permute-done.8.refs_9_), channel_id=1, source_target_pairs={{0,1},{1,0},{2,3},{3,2},{4,5},{5,4},{6,7},{7,6},{8,9},{9,8},{10,11... | collective-permute-start | bytes 786440 | tf_op jit(solution)/shard_map/ppermute | solution.py:38
  40.2 1.5 %collective-permute-start.14 = (bf16[512,256]{1,0:T(8,128)(2,1)S(1)}, bf16[512,256]{1,0:T(8,128)(2,1)S(1)}, u32[]{:S(2)}, u32[]{:S(2)}) collective-permute-start(bf16[512,256]{1,0:T(8,128)(2,1)S(1)} %collective-permute-done.10.refs_11_), channel_id=1, source_target_pairs={{0,1},{1,0},{2,3},{3,2},{4,5},{5,4},{6,7},{7,6},{8,9},{9,8},{10,11... | collective-permute-start | bytes 786440 | tf_op jit(solution)/shard_map/ppermute | solution.py:38
  53.7 4.6 %collective-permute-start.15 = (bf16[512,1024]{1,0:T(8,128)(2,1)S(1)}, bf16[512,1024]{1,0:T(8,128)(2,1)S(1)}, u32[]{:S(2)}, u32[]{:S(2)}) collective-permute-start(bf16[512,1024]{1,0:T(8,128)(2,1)S(1)} %get-tuple-element.15), channel_id=1, source_target_pairs={{0,1},{1,0},{2,3},{3,2},{4,5},{5,4},{6,7},{7,6},{8,9},{9,8},{10,11... | collective-permute-start | bytes 3145736 | tf_op jit(solution)/shard_map/ppermute | solution.py:38
  58.6 6.0 %collective-permute-start.18 = (bf16[64,1024]{1,0:T(8,128)(2,1)S(1)}, bf16[64,1024]{1,0:T(8,128)(2,1)S(1)}, u32[]{:S(2)}, u32[]{:S(2)}) collective-permute-start(bf16[64,1024]{1,0:T(8,128)(2,1)S(1)} %get-tuple-element.28), channel_id=1, source_target_pairs={{0,12},{1,13},{2,14},{3,15},{4,0},{5,1},{6,2},{7,3},{8,4},{9,5},{1... | collective-permute-start | bytes 393224 | tf_op jit(solution)/shard_map/ppermute | solution.py:38
  60.3 7.2 %collective-permute-start.16 = (bf16[64,1024]{1,0:T(8,128)(2,1)S(1)}, bf16[64,1024]{1,0:T(8,128)(2,1)S(1)}, u32[]{:S(2)}, u32[]{:S(2)}) collective-permute-start(bf16[64,1024]{1,0:T(8,128)(2,1)S(1)} %get-tuple-element.27), channel_id=1, source_target_pairs={{0,4},{1,5},{2,6},{3,7},{4,8},{5,9},{6,10},{7,11},{8,12},{9,13},{1... | collective-permute-start | bytes 393224 | tf_op jit(solution)/shard_map/ppermute | solution.py:38
  64.7 8.3 %collective-permute-start.19 = (bf16[128,1024]{1,0:T(8,128)(2,1)S(1)}, bf16[128,1024]{1,0:T(8,128)(2,1)S(1)}, u32[]{:S(2)}, u32[]{:S(2)}) collective-permute-start(bf16[128,1024]{1,0:T(8,128)(2,1)S(1)} %pad_maximum_fusion.1), channel_id=1, source_target_pairs={{0,12},{1,13},{2,14},{3,15},{4,0},{5,1},{6,2},{7,3},{8,4},{9,5},{1... | collective-permute-start | bytes 786440 | tf_op jit(solution)/shard_map/ppermute | solution.py:38
  67.5 8.9 %collective-permute-start.17 = (bf16[128,1024]{1,0:T(8,128)(2,1)S(1)}, bf16[128,1024]{1,0:T(8,128)(2,1)S(1)}, u32[]{:S(2)}, u32[]{:S(2)}) collective-permute-start(bf16[128,1024]{1,0:T(8,128)(2,1)S(1)} %pad_maximum_fusion), channel_id=1, source_target_pairs={{0,4},{1,5},{2,6},{3,7},{4,8},{5,9},{6,10},{7,11},{8,12},{9,13},{1... | collective-permute-start | bytes 786440 | tf_op jit(solution)/shard_map/ppermute | solution.py:38
  76.7 5.1 %collective-permute-start.22 = (bf16[32,1024]{1,0:T(8,128)(2,1)S(1)}, bf16[32,1024]{1,0:T(8,128)(2,1)S(1)}, u32[]{:S(2)}, u32[]{:S(2)}) collective-permute-start(bf16[32,1024]{1,0:T(8,128)(2,1)S(1)} %get-tuple-element.25), channel_id=1, source_target_pairs={{0,2},{1,3},{2,0},{3,1},{4,6},{5,7},{6,4},{7,5},{8,10},{9,11},{10,... | collective-permute-start | bytes 196616 | tf_op jit(solution)/shard_map/ppermute | solution.py:38
  76.8 8.7 %collective-permute-start.20 = (bf16[32,1024]{1,0:T(8,128)(2,1)S(1)}, bf16[32,1024]{1,0:T(8,128)(2,1)S(1)}, u32[]{:S(2)}, u32[]{:S(2)}) collective-permute-start(bf16[32,1024]{1,0:T(8,128)(2,1)S(1)} %get-tuple-element.24), channel_id=1, source_target_pairs={{0,16},{1,17},{2,18},{3,19},{4,20},{5,21},{6,22},{7,23},{8,24},{9,... | collective-permute-start | bytes 196616 | tf_op jit(solution)/shard_map/ppermute | solution.py:38
  76.9 9.8 %collective-permute-start.21 = (bf16[32,1024]{1,0:T(8,128)(2,1)S(1)}, bf16[32,1024]{1,0:T(8,128)(2,1)S(1)}, u32[]{:S(2)}, u32[]{:S(2)}) collective-permute-start(bf16[32,1024]{1,0:T(8,128)(2,1)S(1)} %get-tuple-element.26), channel_id=1, source_target_pairs={{0,18},{1,19},{2,16},{3,17},{4,22},{5,23},{6,20},{7,21},{8,26},{9,... | collective-permute-start | bytes 196616 | tf_op jit(solution)/shard_map/ppermute | solution.py:38

commit v3 on v2

--- a/solution.py
+++ b/solution.py
@@ -150,13 +150,14 @@
     )(tile_orbital, tile_window, tile_count, tile_values, pieces)
 
 
+SEND_ROW, KEEP_ROW = 256, 640
 PART_OFFSETS = ((0, 4), (1, 5), (7, 3), (6, 2))
 
 
 def chi_kernel(*refs):
     tile_parts, green_parts = refs[:8], refs[8:16]
-    send_ref, occ_ref, vir_ref = refs[16:19]
-    tiles_ref, green_ref, flat_ref, meta_ref, sems = refs[19:]
+    keep_ref, send_ref, occ_ref, vir_ref = refs[16:20]
+    tiles_ref, green_ref, flat_ref, meta_ref, sems = refs[20:]
     ao, pair = lax.axis_index("ao"), lax.axis_index("pair")
     my_z, my_y, my_x, my_core = lax.rem(ao, 8), pair // 4, lax.rem(pair // 2, 2), lax.rem(pair, 2)
 
@@ -192,7 +193,9 @@
     def store(block, window, column):
         high, y, x = window // 8, lax.rem(window // 2, 4), lax.rem(window, 2)
         dy, dx = lax.rem(y - my_y + 4, 4), lax.rem(x - my_x + 2, 2)
-        spot = ((dy * 2 + dx) * 2 + high) * 32
+        spot = (dx * 2 + high) * 32
+        far = dy == 2
+        rest = jnp.where(dy == 3, 256, dy * 128)
         vir_row = pl.multiple_of(window * BLK, BLK)
         for i in range(2):
             part = block[i * BLK:(i + 1) * BLK]
@@ -200,7 +203,10 @@
             vir = jnp.concatenate([part[:, 128:256], part[:, 384:512]], axis=1)
             vir_ref[pl.ds(vir_row, BLK), pl.ds(column + i * 256, 256)] = vir
             for core in range(2):
-                row = pl.multiple_of(jnp.where(my_core == core, 0, 512) + spot, 32)
+                row = jnp.where(
+                    my_core == core, jnp.where(far, 0, KEEP_ROW + rest), jnp.where(far, 128, SEND_ROW + rest)
+                )
+                row = pl.multiple_of(row + spot, 32)
                 occ_ref[pl.ds(row, 32), pl.ds(column + i * 256, 256)] = occ[core * 32:(core + 1) * 32]
 
     lane = lax.broadcasted_iota(jnp.int32, (1, 128), 1)
@@ -246,30 +252,45 @@
         def _():
             slots_of(base, number, 4)
 
-    send_ref[...] = chi_rows(occ_ref, vir_ref, 512).astype(BF)
-
-
-def chi_rows(occ_ref, vir_ref, row):
+    product = chi_rows(occ_ref, vir_ref, 0, SEND_ROW)
+    keep_ref[...] = product[:128]
+    send_ref[...] = product[128:].astype(BF)
+
+
+def chi_rows(occ_ref, vir_ref, row, rows):
     return lax.dot_general(
-        occ_ref[pl.ds(row, 512), :], vir_ref[...], (((1,), (1,)), ((), ())), preferred_element_type=F32
+        occ_ref[pl.ds(row, rows), :], vir_ref[...], (((1,), (1,)), ((), ())), preferred_element_type=F32
     )
 
 
-def keep_kernel(occ_ref, vir_ref, *keep_refs):
-    product = chi_rows(occ_ref, vir_ref, 0)
-    for quarter in range(4):
-        keep_refs[quarter][...] = product[quarter * 128:(quarter + 1) * 128]
+def send_kernel(occ_ref, vir_ref, send_ref):
+    send_ref[...] = chi_rows(occ_ref, vir_ref, SEND_ROW, KEEP_ROW - SEND_ROW).astype(BF)
+
+
+def first_kernel(keep_ref, got_ref, unused_ref, ahead_ref, behind_ref):
+    total = keep_ref[...] + got_ref[...].astype(F32)
+    ahead_ref[...] = total[:64].astype(BF)
+    behind_ref[...] = total[64:].astype(BF)
+
+
+def keep_kernel(occ_ref, vir_ref, unused_ref, *keep_refs):
+    product = chi_rows(occ_ref, vir_ref, KEEP_ROW, RW - KEEP_ROW)
+    for number, keep_ref in enumerate(keep_refs):
+        keep_ref[...] = product[number * 128:(number + 1) * 128]
 
 
 def chi_call(tiles, parts):
     vmem = pl.BlockSpec(memory_space=pltpu.VMEM)
-    send, occ, vir = pl.pallas_call(
+    limits = pltpu.CompilerParams(vmem_limit_bytes=12 * 1024 * 1024)
+    cost = pl.CostEstimate(flops=4 * 10**9, bytes_accessed=4 * 2**20, transcendentals=0)
+    keep, send, occ, vir = pl.pallas_call(
         chi_kernel,
         out_shape=(
-            jax.ShapeDtypeStruct((512, RW), BF), pltpu.VMEM((RW, DEPTH), BF), pltpu.VMEM((RW, DEPTH), BF)
+            jax.ShapeDtypeStruct((128, RW), F32), jax.ShapeDtypeStruct((128, RW), BF),
+            pltpu.VMEM((RW, DEPTH), BF), pltpu.VMEM((RW, DEPTH), BF),
         ),
         in_specs=[pl.BlockSpec(memory_space=pl.ANY)] * 16,
-        out_specs=(vmem,) * 3,
+        out_specs=(vmem,) * 4,
         scratch_shapes=[
             pltpu.VMEM((GROUPS * PAY, 128), BF),
             pltpu.VMEM((NAO, 512), BF),
@@ -280,15 +301,32 @@
         compiler_params=pltpu.CompilerParams(vmem_limit_bytes=20 * 1024 * 1024),
         cost_estimate=pl.CostEstimate(flops=8 * 10**9, bytes_accessed=8 * 2**20, transcendentals=0),
     )(*tiles, *parts)
+    got = swap_core(send)
+    send_rest = pl.pallas_call(
+        send_kernel,
+        out_shape=jax.ShapeDtypeStruct((KEEP_ROW - SEND_ROW, RW), BF),
+        in_specs=[vmem] * 2,
+        out_specs=vmem,
+        compiler_params=limits,
+        cost_estimate=cost,
+    )(occ, vir)
+    ahead, behind = pl.pallas_call(
+        first_kernel,
+        out_shape=(jax.ShapeDtypeStruct((64, RW), BF),) * 2,
+        in_specs=[vmem, vmem, pl.BlockSpec(memory_space=pl.ANY)],
+        out_specs=(vmem,) * 2,
+        compiler_params=limits,
+    )(keep, got, send_rest)
+    send_rest, ahead = lax.optimization_barrier((send_rest, ahead))
     keeps = pl.pallas_call(
         keep_kernel,
-        out_shape=(jax.ShapeDtypeStruct((128, RW), F32),) * 4,
-        in_specs=[vmem, vmem],
-        out_specs=(vmem,) * 4,
-        compiler_params=pltpu.CompilerParams(vmem_limit_bytes=12 * 1024 * 1024),
-        cost_estimate=pl.CostEstimate(flops=4 * 10**9, bytes_accessed=4 * 2**20, transcendentals=0),
-    )(occ, vir)
-    return keeps, send
+        out_shape=(jax.ShapeDtypeStruct((128, RW), F32),) * 3,
+        in_specs=[vmem, vmem, pl.BlockSpec(memory_space=pl.ANY)],
+        out_specs=(vmem,) * 3,
+        compiler_params=limits,
+        cost_estimate=cost,
+    )(occ, vir, ahead)
+    return along_y(ahead, 1), along_y(behind, -1), swap_core(send_rest), keeps
 
 
 def gather_tiles(payload):
@@ -305,17 +343,14 @@
     return parts + tuple(swap_core(part) for part in parts)
 
 
-def reduce_band(keeps, send):
-    got = swap_core(send)
-    parts = [got[quarter * 128:(quarter + 1) * 128] for quarter in range(4)]
-    across = keeps[2] + parts[2].astype(F32)
-    ahead = along_y(across[:64].astype(BF), 1)
-    behind = along_y(across[64:].astype(BF), -1)
-    one, three = keeps[1] + parts[1].astype(F32), keeps[3] + parts[3].astype(F32)
+def reduce_band(ahead, behind, got, keeps):
+    own, one, three = [
+        keep + got[number * 128:(number + 1) * 128].astype(F32) for number, keep in enumerate(keeps)
+    ]
     up = jnp.concatenate([one[:64] + ahead.astype(F32), one[64:]], axis=0).astype(BF)
     down = jnp.concatenate([three[:64], three[64:] + behind.astype(F32)], axis=0).astype(BF)
     up, down = along_y(up, 1), along_y(down, -1)
-    total = keeps[0] + parts[0].astype(F32) + up.astype(F32) + down.astype(F32)
+    total = own + up.astype(F32) + down.astype(F32)
     upper = total[:32] + swap_x(total[64:96].astype(BF)).astype(F32)
     lower = next_group(total[32:64].astype(BF), 0).astype(F32) + next_group(total[96:].astype(BF), 1).astype(F32)
     return jnp.concatenate([lower[:, :512], lower[:, 512:] + upper[:, :512], upper[:, 512:]], axis=1)
@@ -325,8 +360,7 @@
     pieces = cut_pieces(green_occ, green_virtual)
     payload = pack(tile_orbital, tile_window, tile_count, tile_values, pieces)
     tiles, parts = gather_tiles(payload), gather_green(pieces)
-    keeps, send = chi_call(tiles, parts)
-    return reduce_band(keeps, send)
+    return reduce_band(*chi_call(tiles, parts))
 
 
 def solution(mesh):

time: 87.3 us -> 86.2 us (0.987)
  waiting for transfers between devices: 34.8 us -> 30.3 us
  Pallas kernels: 19.5 us -> 21.4 us
  starting transfers between devices: 31 us -> 32.4 us
    ppermute x23 -> x24, waiting for transfers between devices: 34.8 us -> 30.3 us  [permute(): return lax.ppermute(value, AXES, pairs)]
    pallas_call x1 -> x3, Pallas kernels: 11.9 us -> 15 us  [the longest x1 11.5 us: chi_call(): pl.pallas_call(chi_kernel, out_shape=(jax.ShapeDtypeStruct((128, RW), F32...]
    ppermute x23 -> x24, starting transfers between devices: 31 us -> 32.4 us  [permute(): return lax.ppermute(value, AXES, pairs)]
    pallas_call x1, Pallas kernels: 4.52 us -> 3.44 us  [chi_call(): pl.pallas_call(keep_kernel, out_shape=(jax.ShapeDtypeStruct((128, RW), F3...]
  transfers between devices with their start and end apart: 23 -> 24, of which waited for: 11 -> 10; matrix products, arithmetic and copies ran while one was open for 0% -> 0% of each run, Pallas kernels for 7% -> 10%
where the time goes in v3:
time: 86.2 us
  starting transfers between devices  32.4 us (38%)
  waiting for transfers between devices  30.3 us (35%)
  Pallas kernels  21.4 us (25%)
  other arithmetic  1.17 us (1%)
  between operations  0.88 us (1%)
    ppermute x24, starting transfers between devices, permute(): return lax.ppermute(value, AXES, pairs)  32.4 us
    ppermute x24, waiting for transfers between devices, permute(): return lax.ppermute(value, AXES, pairs)  30.3 us
    pallas_call x1, Pallas kernels, chi_call(): pl.pallas_call(chi_kernel, out_shape=(jax.ShapeDtypeStruct((128, RW), F32...  11.5 us
    pallas_call x1, Pallas kernels, chi_call(): pl.pallas_call(send_kernel, out_shape=jax.ShapeDtypeStruct((KEEP_ROW - SE...  3.44 us
    pallas_call x1, Pallas kernels, chi_call(): pl.pallas_call(keep_kernel, out_shape=(jax.ShapeDtypeStruct((128, RW), F3...  3.44 us
  transfers between devices with their start and end apart: 24, of which 10 were waited for; matrix products, arithmetic and copies ran while one was open for 0% of the time, Pallas kernels for 10%

profile of v3, /device:TPU:6, one launch (start us, length us, event | category | flops | bytes accessed | tf_op | source)
XLA Modules:
  0.0 86.2 jit_solution(2332109238363907991)
XLA Ops:
  0.0 1.7 %shard_map.64.unused_ref = bf16[512,256]{1,0:T(8,128)(2,1)} custom-call(bf16[2048,128]{1,0:T(8,128)(2,1)} %occ_ref.1, bf16[2048,128]{1,0:T(8,128)(2,1)} %vir_ref.1), custom_call_target="tpu_custom_call" | custom-call | tf_op jit(solution)/shard_map/pallas_call | solution.py:101
  1.7 4.7 %collective-permute-start.7 = (bf16[512,256]{1,0:T(8,128)(2,1)}, bf16[512,256]{1,0:T(8,128)(2,1)S(1)}, u32[]{:S(2)}, u32[]{:S(2)}) collective-permute-start(bf16[512,256]{1,0:T(8,128)(2,1)} %shard_map.64.unused_ref), channel_id=1, source_target_pairs={{0,48},{1,96},{2,176},{3,224},{4,16},{5,80},{6,144},{7,208},{8,112... | collective-permute-start | bytes 786440 | tf_op jit(solution)/shard_map/ppermute | solution.py:38
  7.0 1.4 %shard_map.65.refs_0_ = bf16[1040,128]{1,0:T(8,128)(2,1)S(1)} custom-call(s32[16]{0:T(128)} %orbital_ref.1, s32[16]{0:T(128)} %window_ref.1, s32[1]{0:T(128)S(6)} %copy.7.count_ref, bf16[16,64,128]{2,1,0:T(8,128)(2,1)} %tile_ref.1, bf16[512,256]{1,0:T(8,128)(2,1)} %shard_map.64.unused_ref), custom_call_target="tpu_custom_call" | custom-call | tf_op jit(solution)/shard_map/pallas_call | solution.py:144
  8.4 0.9 %collective-permute-start = (bf16[1040,128]{1,0:T(8,128)(2,1)S(1)}, bf16[1040,128]{1,0:T(8,128)(2,1)S(1)}, u32[]{:S(2)}, u32[]{:S(2)}) collective-permute-start(bf16[1040,128]{1,0:T(8,128)(2,1)S(1)} %shard_map.65.refs_0_), channel_id=1, source_target_pairs={{0,2},{1,3},{2,0},{3,1},{4,6},{5,7},{6,4},{7,5},{8,10},{9,11},{10,... | collective-permute-start | bytes 798728 | tf_op jit(solution)/shard_map/ppermute | solution.py:38
  9.3 0.0 collective-permute-start.1
  9.3 5.2 %collective-permute-start.2 = (bf16[1040,128]{1,0:T(8,128)(2,1)S(1)}, bf16[1040,128]{1,0:T(8,128)(2,1)S(1)}, u32[]{:S(2)}, u32[]{:S(2)}) collective-permute-start(bf16[1040,128]{1,0:T(8,128)(2,1)S(1)} %shard_map.65.refs_0_), channel_id=1, source_target_pairs={{0,12},{1,13},{2,14},{3,15},{4,0},{5,1},{6,2},{7,3},{8,4},{9,5},{1... | collective-permute-start | bytes 798728 | tf_op jit(solution)/shard_map/ppermute | solution.py:38
  14.5 0.0 collective-permute-done.7.refs_8_
  14.5 2.6 %collective-permute-start.9 = (bf16[512,256]{1,0:T(8,128)(2,1)S(1)}, bf16[512,256]{1,0:T(8,128)(2,1)S(1)}, u32[]{:S(2)}, u32[]{:S(2)}) collective-permute-start(bf16[512,256]{1,0:T(8,128)(2,1)S(1)} %collective-permute-done.7.refs_8_), channel_id=1, source_target_pairs={{0,16},{1,17},{2,18},{3,19},{4,20},{5,21},{6,22},{7,23},{8,24},{9,... | collective-permute-start | bytes 786440 | tf_op jit(solution)/shard_map/ppermute | solution.py:38
  17.1 0.0 collective-permute-done.refs_1_
  17.1 3.3 %collective-permute-start.4 = (bf16[1040,128]{1,0:T(8,128)(2,1)S(1)}, bf16[1040,128]{1,0:T(8,128)(2,1)S(1)}, u32[]{:S(2)}, u32[]{:S(2)}) collective-permute-start(bf16[1040,128]{1,0:T(8,128)(2,1)S(1)} %collective-permute-done.refs_1_), channel_id=1, source_target_pairs={{0,12},{1,13},{2,14},{3,15},{4,0},{5,1},{6,2},{7,3},{8,4},{9,5},{1... | collective-permute-start | bytes 798728 | tf_op jit(solution)/shard_map/ppermute | solution.py:38
  20.4 1.1 %collective-permute-start.11 = (bf16[512,256]{1,0:T(8,128)(2,1)S(1)}, bf16[512,256]{1,0:T(8,128)(2,1)S(1)}, u32[]{:S(2)}, u32[]{:S(2)}) collective-permute-start(bf16[512,256]{1,0:T(8,128)(2,1)S(1)} %collective-permute-done.7.refs_8_), channel_id=1, source_target_pairs={{0,1},{1,0},{2,3},{3,2},{4,5},{5,4},{6,7},{7,6},{8,9},{9,8},{10,11... | collective-permute-start | bytes 786440 | tf_op jit(solution)/shard_map/ppermute | solution.py:38
  21.5 0.9 %collective-permute-done.1.refs_2_ = bf16[1040,128]{1,0:T(8,128)(2,1)S(1)} collective-permute-done((bf16[1040,128]{1,0:T(8,128)(2,1)S(1)}, bf16[1040,128]{1,0:T(8,128)(2,1)S(1)}, u32[]{:S(2)}, u32[]{:S(2)}) %collective-permute-start.1) | collective-permute-done | bytes 266272 | tf_op jit(solution)/shard_map/ppermute | solution.py:38
  22.4 0.8 collective-permute-start.5
  23.2 0.0 collective-permute-done.2.refs_3_
  23.2 3.0 %collective-permute-start.8 = (bf16[512,256]{1,0:T(8,128)(2,1)S(1)}, bf16[512,256]{1,0:T(8,128)(2,1)S(1)}, u32[]{:S(2)}, u32[]{:S(2)}) collective-permute-start(bf16[512,256]{1,0:T(8,128)(2,1)S(1)} %collective-permute-done.7.refs_8_), channel_id=1, source_target_pairs={{0,112},{1,113},{2,114},{3,115},{4,116},{5,117},{6,118},{7,119},{8... | collective-permute-start | bytes 786440 | tf_op jit(solution)/shard_map/ppermute | solution.py:38
  26.1 4.4 %collective-permute-done.9.refs_10_ = bf16[512,256]{1,0:T(8,128)(2,1)S(1)} collective-permute-done((bf16[512,256]{1,0:T(8,128)(2,1)S(1)}, bf16[512,256]{1,0:T(8,128)(2,1)S(1)}, u32[]{:S(2)}, u32[]{:S(2)}) %collective-permute-start.9) | collective-permute-done | bytes 262176 | tf_op jit(solution)/shard_map/ppermute | solution.py:38
  30.5 0.0 collective-permute-start.10
  30.5 0.0 collective-permute-done.11.refs_12_
  30.5 0.0 collective-permute-start.3
  30.5 0.0 collective-permute-done.4.refs_5_
  30.5 3.2 %collective-permute-start.6 = (bf16[1040,128]{1,0:T(8,128)(2,1)S(1)}, bf16[1040,128]{1,0:T(8,128)(2,1)S(1)}, u32[]{:S(2)}, u32[]{:S(2)}) collective-permute-start(bf16[1040,128]{1,0:T(8,128)(2,1)S(1)} %collective-permute-done.4.refs_5_), channel_id=1, source_target_pairs={{0,12},{1,13},{2,14},{3,15},{4,0},{5,1},{6,2},{7,3},{8,4},{9,5},{1... | collective-permute-start | bytes 798728 | tf_op jit(solution)/shard_map/ppermute | solution.py:38
  33.8 0.0 collective-permute-done.8.refs_9_
  33.8 0.0 collective-permute-start.13
  33.8 0.0 collective-permute-done.5.refs_6_
  33.8 0.5 collective-permute-start.12
  34.3 5.9 %collective-permute-done.10.refs_11_ = bf16[512,256]{1,0:T(8,128)(2,1)S(1)} collective-permute-done((bf16[512,256]{1,0:T(8,128)(2,1)S(1)}, bf16[512,256]{1,0:T(8,128)(2,1)S(1)}, u32[]{:S(2)}, u32[]{:S(2)}) %collective-permute-start.10) | collective-permute-done | bytes 262176 | tf_op jit(solution)/shard_map/ppermute | solution.py:38
  40.2 0.0 collective-permute-start.14
  40.2 0.1 collective-permute-done.3.refs_4_
  40.3 0.0 collective-permute-done.13.refs_14_
  40.3 0.0 collective-permute-done.12.refs_13_
  40.3 0.0 collective-permute-done.6.refs_7_
  40.3 1.4 %collective-permute-done.14.refs_15_ = bf16[512,256]{1,0:T(8,128)(2,1)S(1)} collective-permute-done((bf16[512,256]{1,0:T(8,128)(2,1)S(1)}, bf16[512,256]{1,0:T(8,128)(2,1)S(1)}, u32[]{:S(2)}, u32[]{:S(2)}) %collective-permute-start.14) | collective-permute-done | bytes 262176 | tf_op jit(solution)/shard_map/ppermute | solution.py:38
  41.8 11.5 %shard_map.66 = (f32[128,1024]{1,0:T(8,128)S(1)}, bf16[128,1024]{1,0:T(8,128)(2,1)S(1)}, bf16[1024,4096]{1,0:T(8,128)(2,1)S(1)}, bf16[1024,4096]{1,0:T(8,128)(2,1)S(1)}) custom-call(bf16[1040,128]{1,0:T(8,128)(2,1)S(1)} %shard_map.65.refs_0_, bf16[1040,128]{1,0:T(8,128)(2,1)S(1)} %collective-permute-done.refs_1_, ...), custom_call_target="tpu_custom_call" | custom-call | flops 8000000000 | bytes 8388608 | tf_op jit(solution)/shard_map/pallas_call | solution.py:286
  53.2 0.1 collective-permute-start.15
  53.3 3.4 %shard_map.67.unused_ref = bf16[384,1024]{1,0:T(8,128)(2,1)S(1)} custom-call(bf16[1024,4096]{1,0:T(8,128)(2,1)S(1)} %get-tuple-element.16.occ_ref, bf16[1024,4096]{1,0:T(8,128)(2,1)S(1)} %get-tuple-element.17.vir_ref), custom_call_target="tpu_custom_call" | custom-call | flops 4000000000 | bytes 4194304 | tf_op jit(solution)/shard_map/pallas_call | solution.py:305
  56.8 0.0 collective-permute-done.15.got_ref
  56.8 0.1 shard_map.68
  56.9 0.6 collective-permute-start.16
  57.4 0.0 collective-permute-start.17
  57.4 3.2 %collective-permute-start.19 = (bf16[64,1024]{1,0:T(8,128)(2,1)S(1)}, bf16[64,1024]{1,0:T(8,128)(2,1)S(1)}, u32[]{:S(2)}, u32[]{:S(2)}) collective-permute-start(bf16[64,1024]{1,0:T(8,128)(2,1)S(1)} %get-tuple-element.26), channel_id=1, source_target_pairs={{0,12},{1,13},{2,14},{3,15},{4,0},{5,1},{6,2},{7,3},{8,4},{9,5},{1... | collective-permute-start | bytes 393224 | tf_op jit(solution)/shard_map/ppermute | solution.py:38
  60.7 3.4 %shard_map.69 = (f32[128,1024]{1,0:T(8,128)S(1)}, f32[128,1024]{1,0:T(8,128)S(1)}, f32[128,1024]{1,0:T(8,128)S(1)}) custom-call(bf16[1024,4096]{1,0:T(8,128)(2,1)S(1)} %get-tuple-element.16.occ_ref, bf16[1024,4096]{1,0:T(8,128)(2,1)S(1)} %get-tuple-element.17.vir_ref, bf16[64,1024]{1,0:T(8,128)(2,1)S(1)} %get-tuple-element.21.unused_ref), custom_call_target="tpu_custom_call" | custom-call | flops 4000000000 | bytes 4194304 | tf_op jit(solution)/shard_map/pallas_call | solution.py:321
  64.1 0.0 collective-permute-done.16
  64.1 0.2 convert_add_fusion.2
  64.3 0.0 collective-permute-done.19
  64.4 2.8 %collective-permute-start.20 = (bf16[128,1024]{1,0:T(8,128)(2,1)S(1)}, bf16[128,1024]{1,0:T(8,128)(2,1)S(1)}, u32[]{:S(2)}, u32[]{:S(2)}) collective-permute-start(bf16[128,1024]{1,0:T(8,128)(2,1)S(1)} %pad_maximum_fusion.1), channel_id=1, source_target_pairs={{0,12},{1,13},{2,14},{3,15},{4,0},{5,1},{6,2},{7,3},{8,4},{9,5},{1... | collective-permute-start | bytes 786440 | tf_op jit(solution)/shard_map/ppermute | solution.py:38
  67.3 0.0 collective-permute-done.17
  67.3 0.1 collective-permute-start.18
  67.4 4.8 %collective-permute-done.20 = bf16[128,1024]{1,0:T(8,128)(2,1)S(1)} collective-permute-done((bf16[128,1024]{1,0:T(8,128)(2,1)S(1)}, bf16[128,1024]{1,0:T(8,128)(2,1)S(1)}, u32[]{:S(2)}, u32[]{:S(2)}) %collective-permute-start.20) | collective-permute-done | bytes 262176 | tf_op jit(solution)/shard_map/ppermute | solution.py:38
  72.3 3.2 %collective-permute-done.18 = bf16[128,1024]{1,0:T(8,128)(2,1)S(1)} collective-permute-done((bf16[128,1024]{1,0:T(8,128)(2,1)S(1)}, bf16[128,1024]{1,0:T(8,128)(2,1)S(1)}, u32[]{:S(2)}, u32[]{:S(2)}) %collective-permute-start.18) | collective-permute-done | bytes 262176 | tf_op jit(solution)/shard_map/ppermute | solution.py:38
  75.5 0.1 fusion.2
  75.7 0.1 collective-permute-start.23
  75.8 0.1 collective-permute-start.21
  75.9 0.1 collective-permute-start.22
  75.9 4.1 %collective-permute-done.23 = bf16[32,1024]{1,0:T(8,128)(2,1)S(1)} collective-permute-done((bf16[32,1024]{1,0:T(8,128)(2,1)S(1)}, bf16[32,1024]{1,0:T(8,128)(2,1)S(1)}, u32[]{:S(2)}, u32[]{:S(2)}) %collective-permute-start.23) | collective-permute-done | bytes 65568 | tf_op jit(solution)/shard_map/ppermute | solution.py:38
  80.0 3.7 %collective-permute-done.21 = bf16[32,1024]{1,0:T(8,128)(2,1)S(1)} collective-permute-done((bf16[32,1024]{1,0:T(8,128)(2,1)S(1)}, bf16[32,1024]{1,0:T(8,128)(2,1)S(1)}, u32[]{:S(2)}, u32[]{:S(2)}) %collective-permute-start.21) | collective-permute-done | bytes 65568 | tf_op jit(solution)/shard_map/ppermute | solution.py:38
  83.7 1.8 %collective-permute-done.22 = bf16[32,1024]{1,0:T(8,128)(2,1)S(1)} collective-permute-done((bf16[32,1024]{1,0:T(8,128)(2,1)S(1)}, bf16[32,1024]{1,0:T(8,128)(2,1)S(1)}, u32[]{:S(2)}, u32[]{:S(2)}) %collective-permute-start.22) | collective-permute-done | bytes 65568 | tf_op jit(solution)/shard_map/ppermute | solution.py:38
  85.6 0.7 pad_maximum_fusion.2
  (10 shorter events, 0.2 us)
Async XLA Ops:
  1.7 12.9 %collective-permute-start.7 = (bf16[512,256]{1,0:T(8,128)(2,1)}, bf16[512,256]{1,0:T(8,128)(2,1)S(1)}, u32[]{:S(2)}, u32[]{:S(2)}) collective-permute-start(bf16[512,256]{1,0:T(8,128)(2,1)} %shard_map.64.unused_ref), channel_id=1, source_target_pairs={{0,48},{1,96},{2,176},{3,224},{4,16},{5,80},{6,144},{7,208},{8,112... | collective-permute-start | bytes 786440 | tf_op jit(solution)/shard_map/ppermute | solution.py:38
  8.4 8.7 %collective-permute-start = (bf16[1040,128]{1,0:T(8,128)(2,1)S(1)}, bf16[1040,128]{1,0:T(8,128)(2,1)S(1)}, u32[]{:S(2)}, u32[]{:S(2)}) collective-permute-start(bf16[1040,128]{1,0:T(8,128)(2,1)S(1)} %shard_map.65.refs_0_), channel_id=1, source_target_pairs={{0,2},{1,3},{2,0},{3,1},{4,6},{5,7},{6,4},{7,5},{8,10},{9,11},{10,... | collective-permute-start | bytes 798728 | tf_op jit(solution)/shard_map/ppermute | solution.py:38
  9.3 13.1 %collective-permute-start.1 = (bf16[1040,128]{1,0:T(8,128)(2,1)S(1)}, bf16[1040,128]{1,0:T(8,128)(2,1)S(1)}, u32[]{:S(2)}, u32[]{:S(2)}) collective-permute-start(bf16[1040,128]{1,0:T(8,128)(2,1)S(1)} %shard_map.65.refs_0_), channel_id=1, source_target_pairs={{0,4},{1,5},{2,6},{3,7},{4,8},{5,9},{6,10},{7,11},{8,12},{9,13},{1... | collective-permute-start | bytes 798728 | tf_op jit(solution)/shard_map/ppermute | solution.py:38
  9.3 13.9 %collective-permute-start.2 = (bf16[1040,128]{1,0:T(8,128)(2,1)S(1)}, bf16[1040,128]{1,0:T(8,128)(2,1)S(1)}, u32[]{:S(2)}, u32[]{:S(2)}) collective-permute-start(bf16[1040,128]{1,0:T(8,128)(2,1)S(1)} %shard_map.65.refs_0_), channel_id=1, source_target_pairs={{0,12},{1,13},{2,14},{3,15},{4,0},{5,1},{6,2},{7,3},{8,4},{9,5},{1... | collective-permute-start | bytes 798728 | tf_op jit(solution)/shard_map/ppermute | solution.py:38
  14.5 16.0 %collective-permute-start.9 = (bf16[512,256]{1,0:T(8,128)(2,1)S(1)}, bf16[512,256]{1,0:T(8,128)(2,1)S(1)}, u32[]{:S(2)}, u32[]{:S(2)}) collective-permute-start(bf16[512,256]{1,0:T(8,128)(2,1)S(1)} %collective-permute-done.7.refs_8_), channel_id=1, source_target_pairs={{0,16},{1,17},{2,18},{3,19},{4,20},{5,21},{6,22},{7,23},{8,24},{9,... | collective-permute-start | bytes 786440 | tf_op jit(solution)/shard_map/ppermute | solution.py:38
  17.1 13.4 %collective-permute-start.4 = (bf16[1040,128]{1,0:T(8,128)(2,1)S(1)}, bf16[1040,128]{1,0:T(8,128)(2,1)S(1)}, u32[]{:S(2)}, u32[]{:S(2)}) collective-permute-start(bf16[1040,128]{1,0:T(8,128)(2,1)S(1)} %collective-permute-done.refs_1_), channel_id=1, source_target_pairs={{0,12},{1,13},{2,14},{3,15},{4,0},{5,1},{6,2},{7,3},{8,4},{9,5},{1... | collective-permute-start | bytes 798728 | tf_op jit(solution)/shard_map/ppermute | solution.py:38
  20.4 10.1 %collective-permute-start.11 = (bf16[512,256]{1,0:T(8,128)(2,1)S(1)}, bf16[512,256]{1,0:T(8,128)(2,1)S(1)}, u32[]{:S(2)}, u32[]{:S(2)}) collective-permute-start(bf16[512,256]{1,0:T(8,128)(2,1)S(1)} %collective-permute-done.7.refs_8_), channel_id=1, source_target_pairs={{0,1},{1,0},{2,3},{3,2},{4,5},{5,4},{6,7},{7,6},{8,9},{9,8},{10,11... | collective-permute-start | bytes 786440 | tf_op jit(solution)/shard_map/ppermute | solution.py:38
  22.4 11.4 %collective-permute-start.5 = (bf16[1040,128]{1,0:T(8,128)(2,1)S(1)}, bf16[1040,128]{1,0:T(8,128)(2,1)S(1)}, u32[]{:S(2)}, u32[]{:S(2)}) collective-permute-start(bf16[1040,128]{1,0:T(8,128)(2,1)S(1)} %collective-permute-done.1.refs_2_), channel_id=1, source_target_pairs={{0,4},{1,5},{2,6},{3,7},{4,8},{5,9},{6,10},{7,11},{8,12},{9,13},{1... | collective-permute-start | bytes 798728 | tf_op jit(solution)/shard_map/ppermute | solution.py:38
  23.2 10.6 %collective-permute-start.8 = (bf16[512,256]{1,0:T(8,128)(2,1)S(1)}, bf16[512,256]{1,0:T(8,128)(2,1)S(1)}, u32[]{:S(2)}, u32[]{:S(2)}) collective-permute-start(bf16[512,256]{1,0:T(8,128)(2,1)S(1)} %collective-permute-done.7.refs_8_), channel_id=1, source_target_pairs={{0,112},{1,113},{2,114},{3,115},{4,116},{5,117},{6,118},{7,119},{8... | collective-permute-start | bytes 786440 | tf_op jit(solution)/shard_map/ppermute | solution.py:38
  30.5 9.7 %collective-permute-start.10 = (bf16[512,256]{1,0:T(8,128)(2,1)S(1)}, bf16[512,256]{1,0:T(8,128)(2,1)S(1)}, u32[]{:S(2)}, u32[]{:S(2)}) collective-permute-start(bf16[512,256]{1,0:T(8,128)(2,1)S(1)} %collective-permute-done.9.refs_10_), channel_id=1, source_target_pairs={{0,16},{1,17},{2,18},{3,19},{4,20},{5,21},{6,22},{7,23},{8,24},{9,... | collective-permute-start | bytes 786440 | tf_op jit(solution)/shard_map/ppermute | solution.py:38
  30.5 9.8 %collective-permute-start.3 = (bf16[1040,128]{1,0:T(8,128)(2,1)S(1)}, bf16[1040,128]{1,0:T(8,128)(2,1)S(1)}, u32[]{:S(2)}, u32[]{:S(2)}) collective-permute-start(bf16[1040,128]{1,0:T(8,128)(2,1)S(1)} %collective-permute-done.refs_1_), channel_id=1, source_target_pairs={{0,4},{1,5},{2,6},{3,7},{4,8},{5,9},{6,10},{7,11},{8,12},{9,13},{1... | collective-permute-start | bytes 798728 | tf_op jit(solution)/shard_map/ppermute | solution.py:38
  30.5 9.8 %collective-permute-start.6 = (bf16[1040,128]{1,0:T(8,128)(2,1)S(1)}, bf16[1040,128]{1,0:T(8,128)(2,1)S(1)}, u32[]{:S(2)}, u32[]{:S(2)}) collective-permute-start(bf16[1040,128]{1,0:T(8,128)(2,1)S(1)} %collective-permute-done.4.refs_5_), channel_id=1, source_target_pairs={{0,12},{1,13},{2,14},{3,15},{4,0},{5,1},{6,2},{7,3},{8,4},{9,5},{1... | collective-permute-start | bytes 798728 | tf_op jit(solution)/shard_map/ppermute | solution.py:38
  33.8 6.6 %collective-permute-start.13 = (bf16[512,256]{1,0:T(8,128)(2,1)S(1)}, bf16[512,256]{1,0:T(8,128)(2,1)S(1)}, u32[]{:S(2)}, u32[]{:S(2)}) collective-permute-start(bf16[512,256]{1,0:T(8,128)(2,1)S(1)} %collective-permute-done.9.refs_10_), channel_id=1, source_target_pairs={{0,1},{1,0},{2,3},{3,2},{4,5},{5,4},{6,7},{7,6},{8,9},{9,8},{10,11... | collective-permute-start | bytes 786440 | tf_op jit(solution)/shard_map/ppermute | solution.py:38
  33.8 6.5 %collective-permute-start.12 = (bf16[512,256]{1,0:T(8,128)(2,1)S(1)}, bf16[512,256]{1,0:T(8,128)(2,1)S(1)}, u32[]{:S(2)}, u32[]{:S(2)}) collective-permute-start(bf16[512,256]{1,0:T(8,128)(2,1)S(1)} %collective-permute-done.8.refs_9_), channel_id=1, source_target_pairs={{0,1},{1,0},{2,3},{3,2},{4,5},{5,4},{6,7},{7,6},{8,9},{9,8},{10,11... | collective-permute-start | bytes 786440 | tf_op jit(solution)/shard_map/ppermute | solution.py:38
  40.2 1.5 %collective-permute-start.14 = (bf16[512,256]{1,0:T(8,128)(2,1)S(1)}, bf16[512,256]{1,0:T(8,128)(2,1)S(1)}, u32[]{:S(2)}, u32[]{:S(2)}) collective-permute-start(bf16[512,256]{1,0:T(8,128)(2,1)S(1)} %collective-permute-done.10.refs_11_), channel_id=1, source_target_pairs={{0,1},{1,0},{2,3},{3,2},{4,5},{5,4},{6,7},{7,6},{8,9},{9,8},{10,11... | collective-permute-start | bytes 786440 | tf_op jit(solution)/shard_map/ppermute | solution.py:38
  53.2 3.5 %collective-permute-start.15 = (bf16[128,1024]{1,0:T(8,128)(2,1)S(1)}, bf16[128,1024]{1,0:T(8,128)(2,1)S(1)}, u32[]{:S(2)}, u32[]{:S(2)}) collective-permute-start(bf16[128,1024]{1,0:T(8,128)(2,1)S(1)} %get-tuple-element.19), channel_id=1, source_target_pairs={{0,1},{1,0},{2,3},{3,2},{4,5},{5,4},{6,7},{7,6},{8,9},{9,8},{10,11... | collective-permute-start | bytes 786440 | tf_op jit(solution)/shard_map/ppermute | solution.py:38
  56.9 7.3 %collective-permute-start.16 = (bf16[384,1024]{1,0:T(8,128)(2,1)S(1)}, bf16[384,1024]{1,0:T(8,128)(2,1)S(1)}, u32[]{:S(2)}, u32[]{:S(2)}) collective-permute-start(bf16[384,1024]{1,0:T(8,128)(2,1)S(1)} %shard_map.67.unused_ref), channel_id=1, source_target_pairs={{0,1},{1,0},{2,3},{3,2},{4,5},{5,4},{6,7},{7,6},{8,9},{9,8},{10,11... | collective-permute-start | bytes 2359304 | tf_op jit(solution)/shard_map/ppermute | solution.py:38
  57.4 9.8 %collective-permute-start.17 = (bf16[64,1024]{1,0:T(8,128)(2,1)S(1)}, bf16[64,1024]{1,0:T(8,128)(2,1)S(1)}, u32[]{:S(2)}, u32[]{:S(2)}) collective-permute-start(bf16[64,1024]{1,0:T(8,128)(2,1)S(1)} %get-tuple-element.21.unused_ref), channel_id=1, source_target_pairs={{0,4},{1,5},{2,6},{3,7},{4,8},{5,9},{6,10},{7,11},{8,12},{9,13},{1... | collective-permute-start | bytes 393224 | tf_op jit(solution)/shard_map/ppermute | solution.py:38
  57.4 6.9 %collective-permute-start.19 = (bf16[64,1024]{1,0:T(8,128)(2,1)S(1)}, bf16[64,1024]{1,0:T(8,128)(2,1)S(1)}, u32[]{:S(2)}, u32[]{:S(2)}) collective-permute-start(bf16[64,1024]{1,0:T(8,128)(2,1)S(1)} %get-tuple-element.26), channel_id=1, source_target_pairs={{0,12},{1,13},{2,14},{3,15},{4,0},{5,1},{6,2},{7,3},{8,4},{9,5},{1... | collective-permute-start | bytes 393224 | tf_op jit(solution)/shard_map/ppermute | solution.py:38
  64.4 7.8 %collective-permute-start.20 = (bf16[128,1024]{1,0:T(8,128)(2,1)S(1)}, bf16[128,1024]{1,0:T(8,128)(2,1)S(1)}, u32[]{:S(2)}, u32[]{:S(2)}) collective-permute-start(bf16[128,1024]{1,0:T(8,128)(2,1)S(1)} %pad_maximum_fusion.1), channel_id=1, source_target_pairs={{0,12},{1,13},{2,14},{3,15},{4,0},{5,1},{6,2},{7,3},{8,4},{9,5},{1... | collective-permute-start | bytes 786440 | tf_op jit(solution)/shard_map/ppermute | solution.py:38
  67.3 8.1 %collective-permute-start.18 = (bf16[128,1024]{1,0:T(8,128)(2,1)S(1)}, bf16[128,1024]{1,0:T(8,128)(2,1)S(1)}, u32[]{:S(2)}, u32[]{:S(2)}) collective-permute-start(bf16[128,1024]{1,0:T(8,128)(2,1)S(1)} %pad_maximum_fusion), channel_id=1, source_target_pairs={{0,4},{1,5},{2,6},{3,7},{4,8},{5,9},{6,10},{7,11},{8,12},{9,13},{1... | collective-permute-start | bytes 786440 | tf_op jit(solution)/shard_map/ppermute | solution.py:38
  75.7 4.4 %collective-permute-start.23 = (bf16[32,1024]{1,0:T(8,128)(2,1)S(1)}, bf16[32,1024]{1,0:T(8,128)(2,1)S(1)}, u32[]{:S(2)}, u32[]{:S(2)}) collective-permute-start(bf16[32,1024]{1,0:T(8,128)(2,1)S(1)} %get-tuple-element.32), channel_id=1, source_target_pairs={{0,2},{1,3},{2,0},{3,1},{4,6},{5,7},{6,4},{7,5},{8,10},{9,11},{10,... | collective-permute-start | bytes 196616 | tf_op jit(solution)/shard_map/ppermute | solution.py:38
  75.8 8.0 %collective-permute-start.21 = (bf16[32,1024]{1,0:T(8,128)(2,1)S(1)}, bf16[32,1024]{1,0:T(8,128)(2,1)S(1)}, u32[]{:S(2)}, u32[]{:S(2)}) collective-permute-start(bf16[32,1024]{1,0:T(8,128)(2,1)S(1)} %get-tuple-element.31), channel_id=1, source_target_pairs={{0,16},{1,17},{2,18},{3,19},{4,20},{5,21},{6,22},{7,23},{8,24},{9,... | collective-permute-start | bytes 196616 | tf_op jit(solution)/shard_map/ppermute | solution.py:38
  75.9 9.6 %collective-permute-start.22 = (bf16[32,1024]{1,0:T(8,128)(2,1)S(1)}, bf16[32,1024]{1,0:T(8,128)(2,1)S(1)}, u32[]{:S(2)}, u32[]{:S(2)}) collective-permute-start(bf16[32,1024]{1,0:T(8,128)(2,1)S(1)} %get-tuple-element.33), channel_id=1, source_target_pairs={{0,18},{1,19},{2,16},{3,17},{4,22},{5,23},{6,20},{7,21},{8,26},{9,... | collective-permute-start | bytes 196616 | tf_op jit(solution)/shard_map/ppermute | solution.py:38

commit v4 on v3

--- a/solution.py
+++ b/solution.py
@@ -161,30 +161,19 @@
     ao, pair = lax.axis_index("ao"), lax.axis_index("pair")
     my_z, my_y, my_x, my_core = lax.rem(ao, 8), pair // 4, lax.rem(pair // 2, 2), lax.rem(pair, 2)
 
-    copies = []
+    for number, ref in enumerate(tile_parts):
+        tiles_ref[pl.ds(number * PAY, PAY), :] = ref[...]
+        head = ref[pl.ds(BODY, META), :].astype(F32).astype(jnp.int32)
+        flat_ref[pl.ds(number, 1), :] = head[:1]
+    to_scalars = pltpu.make_async_copy(flat_ref, meta_ref, sems.at[0])
+    to_scalars.start()
     for number, ref in enumerate(green_parts):
         for spot, offset in enumerate(PART_OFFSETS[number % 4]):
             start = pl.multiple_of(lax.rem(my_z + offset, 8) * PIECE, PIECE)
             lanes = number // 4 * 256
-            copies.append((
-                ref.at[pl.ds(spot * PIECE, PIECE)], green_ref.at[pl.ds(start, PIECE), pl.ds(lanes, 256)]
-            ))
-    for number, ref in enumerate(tile_parts):
-        copies.append((ref, tiles_ref.at[pl.ds(number * PAY, PAY)]))
-    copies = [pltpu.make_async_copy(source, target, sems.at[k]) for k, (source, target) in enumerate(copies)]
-    for copy in copies:
-        copy.start()
+            green_ref[pl.ds(start, PIECE), lanes:lanes + 256] = ref[spot * PIECE:(spot + 1) * PIECE, :]
     occ_ref[...] = jnp.zeros_like(occ_ref)
-    for copy in copies[16:]:
-        copy.wait()
-    for number in range(GROUPS):
-        head = tiles_ref[pl.ds(number * PAY + BODY, META), :].astype(F32).astype(jnp.int32)
-        flat_ref[pl.ds(number, 1), :] = head[:1]
-    to_scalars = pltpu.make_async_copy(flat_ref, meta_ref, sems.at[24])
-    to_scalars.start()
     vir_ref[...] = jnp.zeros_like(vir_ref)
-    for copy in copies[:16]:
-        copy.wait()
     to_scalars.wait()
 
     def rows_of(orbital):
@@ -289,14 +278,14 @@
             jax.ShapeDtypeStruct((128, RW), F32), jax.ShapeDtypeStruct((128, RW), BF),
             pltpu.VMEM((RW, DEPTH), BF), pltpu.VMEM((RW, DEPTH), BF),
         ),
-        in_specs=[pl.BlockSpec(memory_space=pl.ANY)] * 16,
+        in_specs=[vmem] * 16,
         out_specs=(vmem,) * 4,
         scratch_shapes=[
             pltpu.VMEM((GROUPS * PAY, 128), BF),
             pltpu.VMEM((NAO, 512), BF),
             pltpu.VMEM((GROUPS, 128), jnp.int32),
             pltpu.SMEM((GROUPS, 128), jnp.int32),
-            pltpu.SemaphoreType.DMA((25,)),
+            pltpu.SemaphoreType.DMA((1,)),
         ],
         compiler_params=pltpu.CompilerParams(vmem_limit_bytes=20 * 1024 * 1024),
         cost_estimate=pl.CostEstimate(flops=8 * 10**9, bytes_accessed=8 * 2**20, transcendentals=0),

time: 86.2 us -> 84.9 us (0.985)
  Pallas kernels: 21.4 us -> 20.3 us
    pallas_call x1, Pallas kernels: 11.5 us -> 10.3 us  [chi_call(): pl.pallas_call(chi_kernel, out_shape=(jax.ShapeDtypeStruct((128, RW), F32...]
where the time goes in v4:
time: 84.9 us; the launch traced here: 85.1 us
  starting transfers between devices  32.4 us (38%)
  waiting for transfers between devices  30.3 us (36%)
  Pallas kernels  20.3 us (24%)
  other arithmetic  1.17 us (1%)
  between operations  0.88 us (1%)
    ppermute x24, starting transfers between devices, permute(): return lax.ppermute(value, AXES, pairs)  32.4 us
    ppermute x24, waiting for transfers between devices, permute(): return lax.ppermute(value, AXES, pairs)  30.3 us
    pallas_call x1, Pallas kernels, chi_call(): pl.pallas_call(chi_kernel, out_shape=(jax.ShapeDtypeStruct((128, RW), F32...  10.3 us
    pallas_call x1, Pallas kernels, chi_call(): pl.pallas_call(send_kernel, out_shape=jax.ShapeDtypeStruct((KEEP_ROW - SE...  3.44 us
    pallas_call x1, Pallas kernels, chi_call(): pl.pallas_call(keep_kernel, out_shape=(jax.ShapeDtypeStruct((128, RW), F3...  3.43 us
  transfers between devices with their start and end apart: 24, of which 10 were waited for; matrix products, arithmetic and copies ran while one was open for 0% of the time, Pallas kernels for 10%

profile of v4, /device:TPU:6, one launch (start us, length us, event | category | flops | bytes accessed | tf_op | source)
XLA Modules:
  0.0 85.1 jit_solution(7767143004018598773)
XLA Ops:
  0.0 1.7 %shard_map.64.unused_ref = bf16[512,256]{1,0:T(8,128)(2,1)} custom-call(bf16[2048,128]{1,0:T(8,128)(2,1)} %occ_ref.1, bf16[2048,128]{1,0:T(8,128)(2,1)} %vir_ref.1), custom_call_target="tpu_custom_call" | custom-call | tf_op jit(solution)/shard_map/pallas_call | solution.py:101
  1.7 4.7 %collective-permute-start.7 = (bf16[512,256]{1,0:T(8,128)(2,1)}, bf16[512,256]{1,0:T(8,128)(2,1)S(1)}, u32[]{:S(2)}, u32[]{:S(2)}) collective-permute-start(bf16[512,256]{1,0:T(8,128)(2,1)} %shard_map.64.unused_ref), channel_id=1, source_target_pairs={{0,48},{1,96},{2,176},{3,224},{4,16},{5,80},{6,144},{7,208},{8,112... | collective-permute-start | bytes 786440 | tf_op jit(solution)/shard_map/ppermute | solution.py:38
  7.0 1.4 %shard_map.65.refs_0_ = bf16[1040,128]{1,0:T(8,128)(2,1)S(1)} custom-call(s32[16]{0:T(128)} %orbital_ref.1, s32[16]{0:T(128)} %window_ref.1, s32[1]{0:T(128)S(6)} %copy.7.count_ref, bf16[16,64,128]{2,1,0:T(8,128)(2,1)} %tile_ref.1, bf16[512,256]{1,0:T(8,128)(2,1)} %shard_map.64.unused_ref), custom_call_target="tpu_custom_call" | custom-call | tf_op jit(solution)/shard_map/pallas_call | solution.py:144
  8.4 0.9 %collective-permute-start = (bf16[1040,128]{1,0:T(8,128)(2,1)S(1)}, bf16[1040,128]{1,0:T(8,128)(2,1)S(1)}, u32[]{:S(2)}, u32[]{:S(2)}) collective-permute-start(bf16[1040,128]{1,0:T(8,128)(2,1)S(1)} %shard_map.65.refs_0_), channel_id=1, source_target_pairs={{0,2},{1,3},{2,0},{3,1},{4,6},{5,7},{6,4},{7,5},{8,10},{9,11},{10,... | collective-permute-start | bytes 798728 | tf_op jit(solution)/shard_map/ppermute | solution.py:38
  9.3 0.0 collective-permute-start.1
  9.3 5.2 %collective-permute-start.2 = (bf16[1040,128]{1,0:T(8,128)(2,1)S(1)}, bf16[1040,128]{1,0:T(8,128)(2,1)S(1)}, u32[]{:S(2)}, u32[]{:S(2)}) collective-permute-start(bf16[1040,128]{1,0:T(8,128)(2,1)S(1)} %shard_map.65.refs_0_), channel_id=1, source_target_pairs={{0,12},{1,13},{2,14},{3,15},{4,0},{5,1},{6,2},{7,3},{8,4},{9,5},{1... | collective-permute-start | bytes 798728 | tf_op jit(solution)/shard_map/ppermute | solution.py:38
  14.5 0.0 collective-permute-done.7.refs_8_
  14.5 2.6 %collective-permute-start.9 = (bf16[512,256]{1,0:T(8,128)(2,1)S(1)}, bf16[512,256]{1,0:T(8,128)(2,1)S(1)}, u32[]{:S(2)}, u32[]{:S(2)}) collective-permute-start(bf16[512,256]{1,0:T(8,128)(2,1)S(1)} %collective-permute-done.7.refs_8_), channel_id=1, source_target_pairs={{0,16},{1,17},{2,18},{3,19},{4,20},{5,21},{6,22},{7,23},{8,24},{9,... | collective-permute-start | bytes 786440 | tf_op jit(solution)/shard_map/ppermute | solution.py:38
  17.1 0.0 collective-permute-done.refs_1_
  17.1 3.3 %collective-permute-start.4 = (bf16[1040,128]{1,0:T(8,128)(2,1)S(1)}, bf16[1040,128]{1,0:T(8,128)(2,1)S(1)}, u32[]{:S(2)}, u32[]{:S(2)}) collective-permute-start(bf16[1040,128]{1,0:T(8,128)(2,1)S(1)} %collective-permute-done.refs_1_), channel_id=1, source_target_pairs={{0,12},{1,13},{2,14},{3,15},{4,0},{5,1},{6,2},{7,3},{8,4},{9,5},{1... | collective-permute-start | bytes 798728 | tf_op jit(solution)/shard_map/ppermute | solution.py:38
  20.4 1.1 %collective-permute-start.11 = (bf16[512,256]{1,0:T(8,128)(2,1)S(1)}, bf16[512,256]{1,0:T(8,128)(2,1)S(1)}, u32[]{:S(2)}, u32[]{:S(2)}) collective-permute-start(bf16[512,256]{1,0:T(8,128)(2,1)S(1)} %collective-permute-done.7.refs_8_), channel_id=1, source_target_pairs={{0,1},{1,0},{2,3},{3,2},{4,5},{5,4},{6,7},{7,6},{8,9},{9,8},{10,11... | collective-permute-start | bytes 786440 | tf_op jit(solution)/shard_map/ppermute | solution.py:38
  21.5 0.9 %collective-permute-done.1.refs_2_ = bf16[1040,128]{1,0:T(8,128)(2,1)S(1)} collective-permute-done((bf16[1040,128]{1,0:T(8,128)(2,1)S(1)}, bf16[1040,128]{1,0:T(8,128)(2,1)S(1)}, u32[]{:S(2)}, u32[]{:S(2)}) %collective-permute-start.1) | collective-permute-done | bytes 266272 | tf_op jit(solution)/shard_map/ppermute | solution.py:38
  22.4 0.8 collective-permute-start.5
  23.2 0.0 collective-permute-done.2.refs_3_
  23.2 3.0 %collective-permute-start.8 = (bf16[512,256]{1,0:T(8,128)(2,1)S(1)}, bf16[512,256]{1,0:T(8,128)(2,1)S(1)}, u32[]{:S(2)}, u32[]{:S(2)}) collective-permute-start(bf16[512,256]{1,0:T(8,128)(2,1)S(1)} %collective-permute-done.7.refs_8_), channel_id=1, source_target_pairs={{0,112},{1,113},{2,114},{3,115},{4,116},{5,117},{6,118},{7,119},{8... | collective-permute-start | bytes 786440 | tf_op jit(solution)/shard_map/ppermute | solution.py:38
  26.1 4.4 %collective-permute-done.9.refs_10_ = bf16[512,256]{1,0:T(8,128)(2,1)S(1)} collective-permute-done((bf16[512,256]{1,0:T(8,128)(2,1)S(1)}, bf16[512,256]{1,0:T(8,128)(2,1)S(1)}, u32[]{:S(2)}, u32[]{:S(2)}) %collective-permute-start.9) | collective-permute-done | bytes 262176 | tf_op jit(solution)/shard_map/ppermute | solution.py:38
  30.5 0.0 collective-permute-start.10
  30.5 0.0 collective-permute-done.11.refs_12_
  30.5 0.0 collective-permute-start.3
  30.5 0.0 collective-permute-done.4.refs_5_
  30.5 3.2 %collective-permute-start.6 = (bf16[1040,128]{1,0:T(8,128)(2,1)S(1)}, bf16[1040,128]{1,0:T(8,128)(2,1)S(1)}, u32[]{:S(2)}, u32[]{:S(2)}) collective-permute-start(bf16[1040,128]{1,0:T(8,128)(2,1)S(1)} %collective-permute-done.4.refs_5_), channel_id=1, source_target_pairs={{0,12},{1,13},{2,14},{3,15},{4,0},{5,1},{6,2},{7,3},{8,4},{9,5},{1... | collective-permute-start | bytes 798728 | tf_op jit(solution)/shard_map/ppermute | solution.py:38
  33.8 0.0 collective-permute-done.8.refs_9_
  33.8 0.0 collective-permute-start.13
  33.8 0.0 collective-permute-done.5.refs_6_
  33.8 0.5 collective-permute-start.12
  34.3 5.9 %collective-permute-done.10.refs_11_ = bf16[512,256]{1,0:T(8,128)(2,1)S(1)} collective-permute-done((bf16[512,256]{1,0:T(8,128)(2,1)S(1)}, bf16[512,256]{1,0:T(8,128)(2,1)S(1)}, u32[]{:S(2)}, u32[]{:S(2)}) %collective-permute-start.10) | collective-permute-done | bytes 262176 | tf_op jit(solution)/shard_map/ppermute | solution.py:38
  40.2 0.0 collective-permute-start.14
  40.2 0.1 collective-permute-done.3.refs_4_
  40.3 0.0 collective-permute-done.13.refs_14_
  40.3 0.0 collective-permute-done.12.refs_13_
  40.3 0.0 collective-permute-done.6.refs_7_
  40.3 1.4 %collective-permute-done.14.refs_15_ = bf16[512,256]{1,0:T(8,128)(2,1)S(1)} collective-permute-done((bf16[512,256]{1,0:T(8,128)(2,1)S(1)}, bf16[512,256]{1,0:T(8,128)(2,1)S(1)}, u32[]{:S(2)}, u32[]{:S(2)}) %collective-permute-start.14) | collective-permute-done | bytes 262176 | tf_op jit(solution)/shard_map/ppermute | solution.py:38
  41.8 10.3 %shard_map.66 = (f32[128,1024]{1,0:T(8,128)S(1)}, bf16[128,1024]{1,0:T(8,128)(2,1)S(1)}, bf16[1024,4096]{1,0:T(8,128)(2,1)S(1)}, bf16[1024,4096]{1,0:T(8,128)(2,1)S(1)}) custom-call(bf16[1040,128]{1,0:T(8,128)(2,1)S(1)} %shard_map.65.refs_0_, bf16[1040,128]{1,0:T(8,128)(2,1)S(1)} %collective-permute-done.refs_1_, ...), custom_call_target="tpu_custom_call" | custom-call | flops 8000000000 | bytes 8388608 | tf_op jit(solution)/shard_map/pallas_call | solution.py:275
  52.1 0.1 collective-permute-start.15
  52.2 3.4 %shard_map.67.unused_ref = bf16[384,1024]{1,0:T(8,128)(2,1)S(1)} custom-call(bf16[1024,4096]{1,0:T(8,128)(2,1)S(1)} %get-tuple-element.16.occ_ref, bf16[1024,4096]{1,0:T(8,128)(2,1)S(1)} %get-tuple-element.17.vir_ref), custom_call_target="tpu_custom_call" | custom-call | flops 4000000000 | bytes 4194304 | tf_op jit(solution)/shard_map/pallas_call | solution.py:294
  55.6 0.0 collective-permute-done.15.got_ref
  55.7 0.1 shard_map.68
  55.7 0.6 collective-permute-start.16
  56.3 0.0 collective-permute-start.17
  56.3 3.2 %collective-permute-start.19 = (bf16[64,1024]{1,0:T(8,128)(2,1)S(1)}, bf16[64,1024]{1,0:T(8,128)(2,1)S(1)}, u32[]{:S(2)}, u32[]{:S(2)}) collective-permute-start(bf16[64,1024]{1,0:T(8,128)(2,1)S(1)} %get-tuple-element.26), channel_id=1, source_target_pairs={{0,12},{1,13},{2,14},{3,15},{4,0},{5,1},{6,2},{7,3},{8,4},{9,5},{1... | collective-permute-start | bytes 393224 | tf_op jit(solution)/shard_map/ppermute | solution.py:38
  59.5 3.4 %shard_map.69 = (f32[128,1024]{1,0:T(8,128)S(1)}, f32[128,1024]{1,0:T(8,128)S(1)}, f32[128,1024]{1,0:T(8,128)S(1)}) custom-call(bf16[1024,4096]{1,0:T(8,128)(2,1)S(1)} %get-tuple-element.16.occ_ref, bf16[1024,4096]{1,0:T(8,128)(2,1)S(1)} %get-tuple-element.17.vir_ref, bf16[64,1024]{1,0:T(8,128)(2,1)S(1)} %get-tuple-element.21.unused_ref), custom_call_target="tpu_custom_call" | custom-call | flops 4000000000 | bytes 4194304 | tf_op jit(solution)/shard_map/pallas_call | solution.py:310
  63.0 0.0 collective-permute-done.16
  63.0 0.2 convert_add_fusion.2
  63.2 0.0 collective-permute-done.19
  63.3 2.8 %collective-permute-start.20 = (bf16[128,1024]{1,0:T(8,128)(2,1)S(1)}, bf16[128,1024]{1,0:T(8,128)(2,1)S(1)}, u32[]{:S(2)}, u32[]{:S(2)}) collective-permute-start(bf16[128,1024]{1,0:T(8,128)(2,1)S(1)} %pad_maximum_fusion.1), channel_id=1, source_target_pairs={{0,12},{1,13},{2,14},{3,15},{4,0},{5,1},{6,2},{7,3},{8,4},{9,5},{1... | collective-permute-start | bytes 786440 | tf_op jit(solution)/shard_map/ppermute | solution.py:38
  66.2 0.0 collective-permute-done.17
  66.2 0.1 collective-permute-start.18
  66.3 4.8 %collective-permute-done.20 = bf16[128,1024]{1,0:T(8,128)(2,1)S(1)} collective-permute-done((bf16[128,1024]{1,0:T(8,128)(2,1)S(1)}, bf16[128,1024]{1,0:T(8,128)(2,1)S(1)}, u32[]{:S(2)}, u32[]{:S(2)}) %collective-permute-start.20) | collective-permute-done | bytes 262176 | tf_op jit(solution)/shard_map/ppermute | solution.py:38
  71.1 3.2 %collective-permute-done.18 = bf16[128,1024]{1,0:T(8,128)(2,1)S(1)} collective-permute-done((bf16[128,1024]{1,0:T(8,128)(2,1)S(1)}, bf16[128,1024]{1,0:T(8,128)(2,1)S(1)}, u32[]{:S(2)}, u32[]{:S(2)}) %collective-permute-start.18) | collective-permute-done | bytes 262176 | tf_op jit(solution)/shard_map/ppermute | solution.py:38
  74.4 0.1 fusion.2
  74.5 0.1 collective-permute-start.23
  74.6 0.1 collective-permute-start.21
  74.7 0.1 collective-permute-start.22
  74.8 4.2 %collective-permute-done.23 = bf16[32,1024]{1,0:T(8,128)(2,1)S(1)} collective-permute-done((bf16[32,1024]{1,0:T(8,128)(2,1)S(1)}, bf16[32,1024]{1,0:T(8,128)(2,1)S(1)}, u32[]{:S(2)}, u32[]{:S(2)}) %collective-permute-start.23) | collective-permute-done | bytes 65568 | tf_op jit(solution)/shard_map/ppermute | solution.py:38
  79.0 3.6 %collective-permute-done.21 = bf16[32,1024]{1,0:T(8,128)(2,1)S(1)} collective-permute-done((bf16[32,1024]{1,0:T(8,128)(2,1)S(1)}, bf16[32,1024]{1,0:T(8,128)(2,1)S(1)}, u32[]{:S(2)}, u32[]{:S(2)}) %collective-permute-start.21) | collective-permute-done | bytes 65568 | tf_op jit(solution)/shard_map/ppermute | solution.py:38
  82.6 1.8 %collective-permute-done.22 = bf16[32,1024]{1,0:T(8,128)(2,1)S(1)} collective-permute-done((bf16[32,1024]{1,0:T(8,128)(2,1)S(1)}, bf16[32,1024]{1,0:T(8,128)(2,1)S(1)}, u32[]{:S(2)}, u32[]{:S(2)}) %collective-permute-start.22) | collective-permute-done | bytes 65568 | tf_op jit(solution)/shard_map/ppermute | solution.py:38
  84.4 0.7 pad_maximum_fusion.2
  (10 shorter events, 0.2 us)
Async XLA Ops:
  1.7 12.9 %collective-permute-start.7 = (bf16[512,256]{1,0:T(8,128)(2,1)}, bf16[512,256]{1,0:T(8,128)(2,1)S(1)}, u32[]{:S(2)}, u32[]{:S(2)}) collective-permute-start(bf16[512,256]{1,0:T(8,128)(2,1)} %shard_map.64.unused_ref), channel_id=1, source_target_pairs={{0,48},{1,96},{2,176},{3,224},{4,16},{5,80},{6,144},{7,208},{8,112... | collective-permute-start | bytes 786440 | tf_op jit(solution)/shard_map/ppermute | solution.py:38
  8.4 8.7 %collective-permute-start = (bf16[1040,128]{1,0:T(8,128)(2,1)S(1)}, bf16[1040,128]{1,0:T(8,128)(2,1)S(1)}, u32[]{:S(2)}, u32[]{:S(2)}) collective-permute-start(bf16[1040,128]{1,0:T(8,128)(2,1)S(1)} %shard_map.65.refs_0_), channel_id=1, source_target_pairs={{0,2},{1,3},{2,0},{3,1},{4,6},{5,7},{6,4},{7,5},{8,10},{9,11},{10,... | collective-permute-start | bytes 798728 | tf_op jit(solution)/shard_map/ppermute | solution.py:38
  9.3 13.1 %collective-permute-start.1 = (bf16[1040,128]{1,0:T(8,128)(2,1)S(1)}, bf16[1040,128]{1,0:T(8,128)(2,1)S(1)}, u32[]{:S(2)}, u32[]{:S(2)}) collective-permute-start(bf16[1040,128]{1,0:T(8,128)(2,1)S(1)} %shard_map.65.refs_0_), channel_id=1, source_target_pairs={{0,4},{1,5},{2,6},{3,7},{4,8},{5,9},{6,10},{7,11},{8,12},{9,13},{1... | collective-permute-start | bytes 798728 | tf_op jit(solution)/shard_map/ppermute | solution.py:38
  9.3 13.9 %collective-permute-start.2 = (bf16[1040,128]{1,0:T(8,128)(2,1)S(1)}, bf16[1040,128]{1,0:T(8,128)(2,1)S(1)}, u32[]{:S(2)}, u32[]{:S(2)}) collective-permute-start(bf16[1040,128]{1,0:T(8,128)(2,1)S(1)} %shard_map.65.refs_0_), channel_id=1, source_target_pairs={{0,12},{1,13},{2,14},{3,15},{4,0},{5,1},{6,2},{7,3},{8,4},{9,5},{1... | collective-permute-start | bytes 798728 | tf_op jit(solution)/shard_map/ppermute | solution.py:38
  14.5 16.0 %collective-permute-start.9 = (bf16[512,256]{1,0:T(8,128)(2,1)S(1)}, bf16[512,256]{1,0:T(8,128)(2,1)S(1)}, u32[]{:S(2)}, u32[]{:S(2)}) collective-permute-start(bf16[512,256]{1,0:T(8,128)(2,1)S(1)} %collective-permute-done.7.refs_8_), channel_id=1, source_target_pairs={{0,16},{1,17},{2,18},{3,19},{4,20},{5,21},{6,22},{7,23},{8,24},{9,... | collective-permute-start | bytes 786440 | tf_op jit(solution)/shard_map/ppermute | solution.py:38
  17.1 13.4 %collective-permute-start.4 = (bf16[1040,128]{1,0:T(8,128)(2,1)S(1)}, bf16[1040,128]{1,0:T(8,128)(2,1)S(1)}, u32[]{:S(2)}, u32[]{:S(2)}) collective-permute-start(bf16[1040,128]{1,0:T(8,128)(2,1)S(1)} %collective-permute-done.refs_1_), channel_id=1, source_target_pairs={{0,12},{1,13},{2,14},{3,15},{4,0},{5,1},{6,2},{7,3},{8,4},{9,5},{1... | collective-permute-start | bytes 798728 | tf_op jit(solution)/shard_map/ppermute | solution.py:38
  20.4 10.1 %collective-permute-start.11 = (bf16[512,256]{1,0:T(8,128)(2,1)S(1)}, bf16[512,256]{1,0:T(8,128)(2,1)S(1)}, u32[]{:S(2)}, u32[]{:S(2)}) collective-permute-start(bf16[512,256]{1,0:T(8,128)(2,1)S(1)} %collective-permute-done.7.refs_8_), channel_id=1, source_target_pairs={{0,1},{1,0},{2,3},{3,2},{4,5},{5,4},{6,7},{7,6},{8,9},{9,8},{10,11... | collective-permute-start | bytes 786440 | tf_op jit(solution)/shard_map/ppermute | solution.py:38
  22.4 11.4 %collective-permute-start.5 = (bf16[1040,128]{1,0:T(8,128)(2,1)S(1)}, bf16[1040,128]{1,0:T(8,128)(2,1)S(1)}, u32[]{:S(2)}, u32[]{:S(2)}) collective-permute-start(bf16[1040,128]{1,0:T(8,128)(2,1)S(1)} %collective-permute-done.1.refs_2_), channel_id=1, source_target_pairs={{0,4},{1,5},{2,6},{3,7},{4,8},{5,9},{6,10},{7,11},{8,12},{9,13},{1... | collective-permute-start | bytes 798728 | tf_op jit(solution)/shard_map/ppermute | solution.py:38
  23.2 10.6 %collective-permute-start.8 = (bf16[512,256]{1,0:T(8,128)(2,1)S(1)}, bf16[512,256]{1,0:T(8,128)(2,1)S(1)}, u32[]{:S(2)}, u32[]{:S(2)}) collective-permute-start(bf16[512,256]{1,0:T(8,128)(2,1)S(1)} %collective-permute-done.7.refs_8_), channel_id=1, source_target_pairs={{0,112},{1,113},{2,114},{3,115},{4,116},{5,117},{6,118},{7,119},{8... | collective-permute-start | bytes 786440 | tf_op jit(solution)/shard_map/ppermute | solution.py:38
  30.5 9.7 %collective-permute-start.10 = (bf16[512,256]{1,0:T(8,128)(2,1)S(1)}, bf16[512,256]{1,0:T(8,128)(2,1)S(1)}, u32[]{:S(2)}, u32[]{:S(2)}) collective-permute-start(bf16[512,256]{1,0:T(8,128)(2,1)S(1)} %collective-permute-done.9.refs_10_), channel_id=1, source_target_pairs={{0,16},{1,17},{2,18},{3,19},{4,20},{5,21},{6,22},{7,23},{8,24},{9,... | collective-permute-start | bytes 786440 | tf_op jit(solution)/shard_map/ppermute | solution.py:38
  30.5 9.8 %collective-permute-start.3 = (bf16[1040,128]{1,0:T(8,128)(2,1)S(1)}, bf16[1040,128]{1,0:T(8,128)(2,1)S(1)}, u32[]{:S(2)}, u32[]{:S(2)}) collective-permute-start(bf16[1040,128]{1,0:T(8,128)(2,1)S(1)} %collective-permute-done.refs_1_), channel_id=1, source_target_pairs={{0,4},{1,5},{2,6},{3,7},{4,8},{5,9},{6,10},{7,11},{8,12},{9,13},{1... | collective-permute-start | bytes 798728 | tf_op jit(solution)/shard_map/ppermute | solution.py:38
  30.5 9.8 %collective-permute-start.6 = (bf16[1040,128]{1,0:T(8,128)(2,1)S(1)}, bf16[1040,128]{1,0:T(8,128)(2,1)S(1)}, u32[]{:S(2)}, u32[]{:S(2)}) collective-permute-start(bf16[1040,128]{1,0:T(8,128)(2,1)S(1)} %collective-permute-done.4.refs_5_), channel_id=1, source_target_pairs={{0,12},{1,13},{2,14},{3,15},{4,0},{5,1},{6,2},{7,3},{8,4},{9,5},{1... | collective-permute-start | bytes 798728 | tf_op jit(solution)/shard_map/ppermute | solution.py:38
  33.8 6.6 %collective-permute-start.13 = (bf16[512,256]{1,0:T(8,128)(2,1)S(1)}, bf16[512,256]{1,0:T(8,128)(2,1)S(1)}, u32[]{:S(2)}, u32[]{:S(2)}) collective-permute-start(bf16[512,256]{1,0:T(8,128)(2,1)S(1)} %collective-permute-done.9.refs_10_), channel_id=1, source_target_pairs={{0,1},{1,0},{2,3},{3,2},{4,5},{5,4},{6,7},{7,6},{8,9},{9,8},{10,11... | collective-permute-start | bytes 786440 | tf_op jit(solution)/shard_map/ppermute | solution.py:38
  33.8 6.5 %collective-permute-start.12 = (bf16[512,256]{1,0:T(8,128)(2,1)S(1)}, bf16[512,256]{1,0:T(8,128)(2,1)S(1)}, u32[]{:S(2)}, u32[]{:S(2)}) collective-permute-start(bf16[512,256]{1,0:T(8,128)(2,1)S(1)} %collective-permute-done.8.refs_9_), channel_id=1, source_target_pairs={{0,1},{1,0},{2,3},{3,2},{4,5},{5,4},{6,7},{7,6},{8,9},{9,8},{10,11... | collective-permute-start | bytes 786440 | tf_op jit(solution)/shard_map/ppermute | solution.py:38
  40.2 1.5 %collective-permute-start.14 = (bf16[512,256]{1,0:T(8,128)(2,1)S(1)}, bf16[512,256]{1,0:T(8,128)(2,1)S(1)}, u32[]{:S(2)}, u32[]{:S(2)}) collective-permute-start(bf16[512,256]{1,0:T(8,128)(2,1)S(1)} %collective-permute-done.10.refs_11_), channel_id=1, source_target_pairs={{0,1},{1,0},{2,3},{3,2},{4,5},{5,4},{6,7},{7,6},{8,9},{9,8},{10,11... | collective-permute-start | bytes 786440 | tf_op jit(solution)/shard_map/ppermute | solution.py:38
  52.1 3.5 %collective-permute-start.15 = (bf16[128,1024]{1,0:T(8,128)(2,1)S(1)}, bf16[128,1024]{1,0:T(8,128)(2,1)S(1)}, u32[]{:S(2)}, u32[]{:S(2)}) collective-permute-start(bf16[128,1024]{1,0:T(8,128)(2,1)S(1)} %get-tuple-element.19), channel_id=1, source_target_pairs={{0,1},{1,0},{2,3},{3,2},{4,5},{5,4},{6,7},{7,6},{8,9},{9,8},{10,11... | collective-permute-start | bytes 786440 | tf_op jit(solution)/shard_map/ppermute | solution.py:38
  55.7 7.3 %collective-permute-start.16 = (bf16[384,1024]{1,0:T(8,128)(2,1)S(1)}, bf16[384,1024]{1,0:T(8,128)(2,1)S(1)}, u32[]{:S(2)}, u32[]{:S(2)}) collective-permute-start(bf16[384,1024]{1,0:T(8,128)(2,1)S(1)} %shard_map.67.unused_ref), channel_id=1, source_target_pairs={{0,1},{1,0},{2,3},{3,2},{4,5},{5,4},{6,7},{7,6},{8,9},{9,8},{10,11... | collective-permute-start | bytes 2359304 | tf_op jit(solution)/shard_map/ppermute | solution.py:38
  56.3 9.8 %collective-permute-start.17 = (bf16[64,1024]{1,0:T(8,128)(2,1)S(1)}, bf16[64,1024]{1,0:T(8,128)(2,1)S(1)}, u32[]{:S(2)}, u32[]{:S(2)}) collective-permute-start(bf16[64,1024]{1,0:T(8,128)(2,1)S(1)} %get-tuple-element.21.unused_ref), channel_id=1, source_target_pairs={{0,4},{1,5},{2,6},{3,7},{4,8},{5,9},{6,10},{7,11},{8,12},{9,13},{1... | collective-permute-start | bytes 393224 | tf_op jit(solution)/shard_map/ppermute | solution.py:38
  56.3 6.9 %collective-permute-start.19 = (bf16[64,1024]{1,0:T(8,128)(2,1)S(1)}, bf16[64,1024]{1,0:T(8,128)(2,1)S(1)}, u32[]{:S(2)}, u32[]{:S(2)}) collective-permute-start(bf16[64,1024]{1,0:T(8,128)(2,1)S(1)} %get-tuple-element.26), channel_id=1, source_target_pairs={{0,12},{1,13},{2,14},{3,15},{4,0},{5,1},{6,2},{7,3},{8,4},{9,5},{1... | collective-permute-start | bytes 393224 | tf_op jit(solution)/shard_map/ppermute | solution.py:38
  63.3 7.8 %collective-permute-start.20 = (bf16[128,1024]{1,0:T(8,128)(2,1)S(1)}, bf16[128,1024]{1,0:T(8,128)(2,1)S(1)}, u32[]{:S(2)}, u32[]{:S(2)}) collective-permute-start(bf16[128,1024]{1,0:T(8,128)(2,1)S(1)} %pad_maximum_fusion.1), channel_id=1, source_target_pairs={{0,12},{1,13},{2,14},{3,15},{4,0},{5,1},{6,2},{7,3},{8,4},{9,5},{1... | collective-permute-start | bytes 786440 | tf_op jit(solution)/shard_map/ppermute | solution.py:38
  66.2 8.1 %collective-permute-start.18 = (bf16[128,1024]{1,0:T(8,128)(2,1)S(1)}, bf16[128,1024]{1,0:T(8,128)(2,1)S(1)}, u32[]{:S(2)}, u32[]{:S(2)}) collective-permute-start(bf16[128,1024]{1,0:T(8,128)(2,1)S(1)} %pad_maximum_fusion), channel_id=1, source_target_pairs={{0,4},{1,5},{2,6},{3,7},{4,8},{5,9},{6,10},{7,11},{8,12},{9,13},{1... | collective-permute-start | bytes 786440 | tf_op jit(solution)/shard_map/ppermute | solution.py:38
  74.5 4.5 %collective-permute-start.23 = (bf16[32,1024]{1,0:T(8,128)(2,1)S(1)}, bf16[32,1024]{1,0:T(8,128)(2,1)S(1)}, u32[]{:S(2)}, u32[]{:S(2)}) collective-permute-start(bf16[32,1024]{1,0:T(8,128)(2,1)S(1)} %get-tuple-element.32), channel_id=1, source_target_pairs={{0,2},{1,3},{2,0},{3,1},{4,6},{5,7},{6,4},{7,5},{8,10},{9,11},{10,... | collective-permute-start | bytes 196616 | tf_op jit(solution)/shard_map/ppermute | solution.py:38
  74.6 8.0 %collective-permute-start.21 = (bf16[32,1024]{1,0:T(8,128)(2,1)S(1)}, bf16[32,1024]{1,0:T(8,128)(2,1)S(1)}, u32[]{:S(2)}, u32[]{:S(2)}) collective-permute-start(bf16[32,1024]{1,0:T(8,128)(2,1)S(1)} %get-tuple-element.31), channel_id=1, source_target_pairs={{0,16},{1,17},{2,18},{3,19},{4,20},{5,21},{6,22},{7,23},{8,24},{9,... | collective-permute-start | bytes 196616 | tf_op jit(solution)/shard_map/ppermute | solution.py:38
  74.7 9.6 %collective-permute-start.22 = (bf16[32,1024]{1,0:T(8,128)(2,1)S(1)}, bf16[32,1024]{1,0:T(8,128)(2,1)S(1)}, u32[]{:S(2)}, u32[]{:S(2)}) collective-permute-start(bf16[32,1024]{1,0:T(8,128)(2,1)S(1)} %get-tuple-element.33), channel_id=1, source_target_pairs={{0,18},{1,19},{2,16},{3,17},{4,22},{5,23},{6,20},{7,21},{8,26},{9,... | collective-permute-start | bytes 196616 | tf_op jit(solution)/shard_map/ppermute | solution.py:38

commit v5 on v4

--- a/solution.py
+++ b/solution.py
@@ -233,13 +233,10 @@
         base = number * PAY
         live = meta_ref[number, 2 * TILES]
 
-        @pl.when(live <= 8)
-        def _():
-            slots_of(base, number, 2)
-
-        @pl.when(live > 8)
-        def _():
-            slots_of(base, number, 4)
+        for quads in range(1, TILES // 4 + 1):
+            @pl.when((live > 4 * quads - 4) & (live <= 4 * quads))
+            def _(quads=quads):
+                slots_of(base, number, quads)
 
     product = chi_rows(occ_ref, vir_ref, 0, SEND_ROW)
     keep_ref[...] = product[:128]

time: 84.9 us -> 84.1 us (level)
  Pallas kernels: 20.3 us -> 18.4 us
    pallas_call x1, Pallas kernels: 10.3 us -> 8.43 us  [chi_call(): pl.pallas_call(chi_kernel, out_shape=(jax.ShapeDtypeStruct((128, RW), F32...]
where the time goes in v5:
time: 84.1 us
  starting transfers between devices  32.9 us (39%)
  waiting for transfers between devices  30.7 us (37%)
  Pallas kernels  18.4 us (22%)
  other arithmetic  1.17 us (1%)
  between operations  0.88 us (1%)
    ppermute x24, starting transfers between devices, permute(): return lax.ppermute(value, AXES, pairs)  32.9 us
    ppermute x24, waiting for transfers between devices, permute(): return lax.ppermute(value, AXES, pairs)  30.7 us
    pallas_call x1, Pallas kernels, chi_call(): pl.pallas_call(chi_kernel, out_shape=(jax.ShapeDtypeStruct((128, RW), F32...  8.43 us
    pallas_call x1, Pallas kernels, chi_call(): pl.pallas_call(keep_kernel, out_shape=(jax.ShapeDtypeStruct((128, RW), F3...  3.44 us
    pallas_call x1, Pallas kernels, chi_call(): pl.pallas_call(send_kernel, out_shape=jax.ShapeDtypeStruct((KEEP_ROW - SE...  3.43 us
  transfers between devices with their start and end apart: 24, of which 10 were waited for; matrix products, arithmetic and copies ran while one was open for 0% of the time, Pallas kernels for 10%

profile of v5, /device:TPU:6, one launch (start us, length us, event | category | flops | bytes accessed | tf_op | source)
XLA Modules:
  0.0 84.1 jit_solution(4205665310867651628)
XLA Ops:
  0.0 1.7 %shard_map.64.unused_ref = bf16[512,256]{1,0:T(8,128)(2,1)} custom-call(bf16[2048,128]{1,0:T(8,128)(2,1)} %occ_ref.1, bf16[2048,128]{1,0:T(8,128)(2,1)} %vir_ref.1), custom_call_target="tpu_custom_call" | custom-call | tf_op jit(solution)/shard_map/pallas_call | solution.py:101
  1.7 4.7 %collective-permute-start.7 = (bf16[512,256]{1,0:T(8,128)(2,1)}, bf16[512,256]{1,0:T(8,128)(2,1)S(1)}, u32[]{:S(2)}, u32[]{:S(2)}) collective-permute-start(bf16[512,256]{1,0:T(8,128)(2,1)} %shard_map.64.unused_ref), channel_id=1, source_target_pairs={{0,48},{1,96},{2,176},{3,224},{4,16},{5,80},{6,144},{7,208},{8,112... | collective-permute-start | bytes 786440 | tf_op jit(solution)/shard_map/ppermute | solution.py:38
  7.0 1.4 %shard_map.65.refs_0_ = bf16[1040,128]{1,0:T(8,128)(2,1)S(1)} custom-call(s32[16]{0:T(128)} %orbital_ref.1, s32[16]{0:T(128)} %window_ref.1, s32[1]{0:T(128)S(6)} %copy.7.count_ref, bf16[16,64,128]{2,1,0:T(8,128)(2,1)} %tile_ref.1, bf16[512,256]{1,0:T(8,128)(2,1)} %shard_map.64.unused_ref), custom_call_target="tpu_custom_call" | custom-call | tf_op jit(solution)/shard_map/pallas_call | solution.py:144
  8.4 0.9 %collective-permute-start = (bf16[1040,128]{1,0:T(8,128)(2,1)S(1)}, bf16[1040,128]{1,0:T(8,128)(2,1)S(1)}, u32[]{:S(2)}, u32[]{:S(2)}) collective-permute-start(bf16[1040,128]{1,0:T(8,128)(2,1)S(1)} %shard_map.65.refs_0_), channel_id=1, source_target_pairs={{0,2},{1,3},{2,0},{3,1},{4,6},{5,7},{6,4},{7,5},{8,10},{9,11},{10,... | collective-permute-start | bytes 798728 | tf_op jit(solution)/shard_map/ppermute | solution.py:38
  9.3 0.0 collective-permute-start.1
  9.3 5.2 %collective-permute-start.2 = (bf16[1040,128]{1,0:T(8,128)(2,1)S(1)}, bf16[1040,128]{1,0:T(8,128)(2,1)S(1)}, u32[]{:S(2)}, u32[]{:S(2)}) collective-permute-start(bf16[1040,128]{1,0:T(8,128)(2,1)S(1)} %shard_map.65.refs_0_), channel_id=1, source_target_pairs={{0,12},{1,13},{2,14},{3,15},{4,0},{5,1},{6,2},{7,3},{8,4},{9,5},{1... | collective-permute-start | bytes 798728 | tf_op jit(solution)/shard_map/ppermute | solution.py:38
  14.5 0.0 collective-permute-done.7.refs_8_
  14.5 2.6 %collective-permute-start.9 = (bf16[512,256]{1,0:T(8,128)(2,1)S(1)}, bf16[512,256]{1,0:T(8,128)(2,1)S(1)}, u32[]{:S(2)}, u32[]{:S(2)}) collective-permute-start(bf16[512,256]{1,0:T(8,128)(2,1)S(1)} %collective-permute-done.7.refs_8_), channel_id=1, source_target_pairs={{0,16},{1,17},{2,18},{3,19},{4,20},{5,21},{6,22},{7,23},{8,24},{9,... | collective-permute-start | bytes 786440 | tf_op jit(solution)/shard_map/ppermute | solution.py:38
  17.1 0.0 collective-permute-done.refs_1_
  17.1 3.3 %collective-permute-start.4 = (bf16[1040,128]{1,0:T(8,128)(2,1)S(1)}, bf16[1040,128]{1,0:T(8,128)(2,1)S(1)}, u32[]{:S(2)}, u32[]{:S(2)}) collective-permute-start(bf16[1040,128]{1,0:T(8,128)(2,1)S(1)} %collective-permute-done.refs_1_), channel_id=1, source_target_pairs={{0,12},{1,13},{2,14},{3,15},{4,0},{5,1},{6,2},{7,3},{8,4},{9,5},{1... | collective-permute-start | bytes 798728 | tf_op jit(solution)/shard_map/ppermute | solution.py:38
  20.4 1.1 %collective-permute-start.11 = (bf16[512,256]{1,0:T(8,128)(2,1)S(1)}, bf16[512,256]{1,0:T(8,128)(2,1)S(1)}, u32[]{:S(2)}, u32[]{:S(2)}) collective-permute-start(bf16[512,256]{1,0:T(8,128)(2,1)S(1)} %collective-permute-done.7.refs_8_), channel_id=1, source_target_pairs={{0,1},{1,0},{2,3},{3,2},{4,5},{5,4},{6,7},{7,6},{8,9},{9,8},{10,11... | collective-permute-start | bytes 786440 | tf_op jit(solution)/shard_map/ppermute | solution.py:38
  21.5 0.9 %collective-permute-done.1.refs_2_ = bf16[1040,128]{1,0:T(8,128)(2,1)S(1)} collective-permute-done((bf16[1040,128]{1,0:T(8,128)(2,1)S(1)}, bf16[1040,128]{1,0:T(8,128)(2,1)S(1)}, u32[]{:S(2)}, u32[]{:S(2)}) %collective-permute-start.1) | collective-permute-done | bytes 266272 | tf_op jit(solution)/shard_map/ppermute | solution.py:38
  22.4 0.8 collective-permute-start.5
  23.2 0.0 collective-permute-done.2.refs_3_
  23.2 3.0 %collective-permute-start.8 = (bf16[512,256]{1,0:T(8,128)(2,1)S(1)}, bf16[512,256]{1,0:T(8,128)(2,1)S(1)}, u32[]{:S(2)}, u32[]{:S(2)}) collective-permute-start(bf16[512,256]{1,0:T(8,128)(2,1)S(1)} %collective-permute-done.7.refs_8_), channel_id=1, source_target_pairs={{0,112},{1,113},{2,114},{3,115},{4,116},{5,117},{6,118},{7,119},{8... | collective-permute-start | bytes 786440 | tf_op jit(solution)/shard_map/ppermute | solution.py:38
  26.1 4.4 %collective-permute-done.9.refs_10_ = bf16[512,256]{1,0:T(8,128)(2,1)S(1)} collective-permute-done((bf16[512,256]{1,0:T(8,128)(2,1)S(1)}, bf16[512,256]{1,0:T(8,128)(2,1)S(1)}, u32[]{:S(2)}, u32[]{:S(2)}) %collective-permute-start.9) | collective-permute-done | bytes 262176 | tf_op jit(solution)/shard_map/ppermute | solution.py:38
  30.5 0.0 collective-permute-start.10
  30.5 0.0 collective-permute-done.11.refs_12_
  30.5 0.0 collective-permute-start.3
  30.5 0.0 collective-permute-done.4.refs_5_
  30.5 3.2 %collective-permute-start.6 = (bf16[1040,128]{1,0:T(8,128)(2,1)S(1)}, bf16[1040,128]{1,0:T(8,128)(2,1)S(1)}, u32[]{:S(2)}, u32[]{:S(2)}) collective-permute-start(bf16[1040,128]{1,0:T(8,128)(2,1)S(1)} %collective-permute-done.4.refs_5_), channel_id=1, source_target_pairs={{0,12},{1,13},{2,14},{3,15},{4,0},{5,1},{6,2},{7,3},{8,4},{9,5},{1... | collective-permute-start | bytes 798728 | tf_op jit(solution)/shard_map/ppermute | solution.py:38
  33.8 0.0 collective-permute-done.8.refs_9_
  33.8 0.0 collective-permute-start.13
  33.8 0.0 collective-permute-done.5.refs_6_
  33.8 0.5 collective-permute-start.12
  34.3 5.9 %collective-permute-done.10.refs_11_ = bf16[512,256]{1,0:T(8,128)(2,1)S(1)} collective-permute-done((bf16[512,256]{1,0:T(8,128)(2,1)S(1)}, bf16[512,256]{1,0:T(8,128)(2,1)S(1)}, u32[]{:S(2)}, u32[]{:S(2)}) %collective-permute-start.10) | collective-permute-done | bytes 262176 | tf_op jit(solution)/shard_map/ppermute | solution.py:38
  40.2 0.0 collective-permute-start.14
  40.2 0.1 collective-permute-done.3.refs_4_
  40.3 0.0 collective-permute-done.13.refs_14_
  40.3 0.0 collective-permute-done.12.refs_13_
  40.3 0.0 collective-permute-done.6.refs_7_
  40.3 1.4 %collective-permute-done.14.refs_15_ = bf16[512,256]{1,0:T(8,128)(2,1)S(1)} collective-permute-done((bf16[512,256]{1,0:T(8,128)(2,1)S(1)}, bf16[512,256]{1,0:T(8,128)(2,1)S(1)}, u32[]{:S(2)}, u32[]{:S(2)}) %collective-permute-start.14) | collective-permute-done | bytes 262176 | tf_op jit(solution)/shard_map/ppermute | solution.py:38
  41.8 8.4 %shard_map.66 = (f32[128,1024]{1,0:T(8,128)S(1)}, bf16[128,1024]{1,0:T(8,128)(2,1)S(1)}, bf16[1024,4096]{1,0:T(8,128)(2,1)S(1)}, bf16[1024,4096]{1,0:T(8,128)(2,1)S(1)}) custom-call(bf16[1040,128]{1,0:T(8,128)(2,1)S(1)} %shard_map.65.refs_0_, bf16[1040,128]{1,0:T(8,128)(2,1)S(1)} %collective-permute-done.refs_1_, ...), custom_call_target="tpu_custom_call" | custom-call | flops 8000000000 | bytes 8388608 | tf_op jit(solution)/shard_map/pallas_call | solution.py:272
  50.2 0.6 collective-permute-start.15
  50.8 3.4 %shard_map.67.unused_ref = bf16[384,1024]{1,0:T(8,128)(2,1)S(1)} custom-call(bf16[1024,4096]{1,0:T(8,128)(2,1)S(1)} %get-tuple-element.16.occ_ref, bf16[1024,4096]{1,0:T(8,128)(2,1)S(1)} %get-tuple-element.17.vir_ref), custom_call_target="tpu_custom_call" | custom-call | flops 4000000000 | bytes 4194304 | tf_op jit(solution)/shard_map/pallas_call | solution.py:291
  54.3 0.0 collective-permute-done.15.got_ref
  54.3 0.1 shard_map.68
  54.3 0.1 collective-permute-start.16
  54.5 0.1 collective-permute-start.17
  54.5 3.2 %collective-permute-start.19 = (bf16[64,1024]{1,0:T(8,128)(2,1)S(1)}, bf16[64,1024]{1,0:T(8,128)(2,1)S(1)}, u32[]{:S(2)}, u32[]{:S(2)}) collective-permute-start(bf16[64,1024]{1,0:T(8,128)(2,1)S(1)} %get-tuple-element.26), channel_id=1, source_target_pairs={{0,12},{1,13},{2,14},{3,15},{4,0},{5,1},{6,2},{7,3},{8,4},{9,5},{1... | collective-permute-start | bytes 393224 | tf_op jit(solution)/shard_map/ppermute | solution.py:38
  57.8 3.4 %shard_map.69 = (f32[128,1024]{1,0:T(8,128)S(1)}, f32[128,1024]{1,0:T(8,128)S(1)}, f32[128,1024]{1,0:T(8,128)S(1)}) custom-call(bf16[1024,4096]{1,0:T(8,128)(2,1)S(1)} %get-tuple-element.16.occ_ref, bf16[1024,4096]{1,0:T(8,128)(2,1)S(1)} %get-tuple-element.17.vir_ref, bf16[64,1024]{1,0:T(8,128)(2,1)S(1)} %get-tuple-element.21.unused_ref), custom_call_target="tpu_custom_call" | custom-call | flops 4000000000 | bytes 4194304 | tf_op jit(solution)/shard_map/pallas_call | solution.py:307
  61.2 0.0 collective-permute-done.16
  61.2 0.2 convert_add_fusion.2
  61.4 0.0 collective-permute-done.19
  61.5 3.2 %collective-permute-start.20 = (bf16[128,1024]{1,0:T(8,128)(2,1)S(1)}, bf16[128,1024]{1,0:T(8,128)(2,1)S(1)}, u32[]{:S(2)}, u32[]{:S(2)}) collective-permute-start(bf16[128,1024]{1,0:T(8,128)(2,1)S(1)} %pad_maximum_fusion.1), channel_id=1, source_target_pairs={{0,12},{1,13},{2,14},{3,15},{4,0},{5,1},{6,2},{7,3},{8,4},{9,5},{1... | collective-permute-start | bytes 786440 | tf_op jit(solution)/shard_map/ppermute | solution.py:38
  64.7 0.0 collective-permute-done.17
  64.8 0.1 collective-permute-start.18
  64.9 4.9 %collective-permute-done.20 = bf16[128,1024]{1,0:T(8,128)(2,1)S(1)} collective-permute-done((bf16[128,1024]{1,0:T(8,128)(2,1)S(1)}, bf16[128,1024]{1,0:T(8,128)(2,1)S(1)}, u32[]{:S(2)}, u32[]{:S(2)}) %collective-permute-start.20) | collective-permute-done | bytes 262176 | tf_op jit(solution)/shard_map/ppermute | solution.py:38
  69.8 3.6 %collective-permute-done.18 = bf16[128,1024]{1,0:T(8,128)(2,1)S(1)} collective-permute-done((bf16[128,1024]{1,0:T(8,128)(2,1)S(1)}, bf16[128,1024]{1,0:T(8,128)(2,1)S(1)}, u32[]{:S(2)}, u32[]{:S(2)}) %collective-permute-start.18) | collective-permute-done | bytes 262176 | tf_op jit(solution)/shard_map/ppermute | solution.py:38
  73.3 0.1 fusion.2
  73.5 0.1 collective-permute-start.23
  73.6 0.1 collective-permute-start.21
  73.7 0.1 collective-permute-start.22
  73.8 4.8 %collective-permute-done.23 = bf16[32,1024]{1,0:T(8,128)(2,1)S(1)} collective-permute-done((bf16[32,1024]{1,0:T(8,128)(2,1)S(1)}, bf16[32,1024]{1,0:T(8,128)(2,1)S(1)}, u32[]{:S(2)}, u32[]{:S(2)}) %collective-permute-start.23) | collective-permute-done | bytes 65568 | tf_op jit(solution)/shard_map/ppermute | solution.py:38
  78.6 3.0 %collective-permute-done.21 = bf16[32,1024]{1,0:T(8,128)(2,1)S(1)} collective-permute-done((bf16[32,1024]{1,0:T(8,128)(2,1)S(1)}, bf16[32,1024]{1,0:T(8,128)(2,1)S(1)}, u32[]{:S(2)}, u32[]{:S(2)}) %collective-permute-start.21) | collective-permute-done | bytes 65568 | tf_op jit(solution)/shard_map/ppermute | solution.py:38
  81.6 1.8 %collective-permute-done.22 = bf16[32,1024]{1,0:T(8,128)(2,1)S(1)} collective-permute-done((bf16[32,1024]{1,0:T(8,128)(2,1)S(1)}, bf16[32,1024]{1,0:T(8,128)(2,1)S(1)}, u32[]{:S(2)}, u32[]{:S(2)}) %collective-permute-start.22) | collective-permute-done | bytes 65568 | tf_op jit(solution)/shard_map/ppermute | solution.py:38
  83.4 0.7 pad_maximum_fusion.2
  (10 shorter events, 0.2 us)
Async XLA Ops:
  1.7 12.9 %collective-permute-start.7 = (bf16[512,256]{1,0:T(8,128)(2,1)}, bf16[512,256]{1,0:T(8,128)(2,1)S(1)}, u32[]{:S(2)}, u32[]{:S(2)}) collective-permute-start(bf16[512,256]{1,0:T(8,128)(2,1)} %shard_map.64.unused_ref), channel_id=1, source_target_pairs={{0,48},{1,96},{2,176},{3,224},{4,16},{5,80},{6,144},{7,208},{8,112... | collective-permute-start | bytes 786440 | tf_op jit(solution)/shard_map/ppermute | solution.py:38
  8.4 8.7 %collective-permute-start = (bf16[1040,128]{1,0:T(8,128)(2,1)S(1)}, bf16[1040,128]{1,0:T(8,128)(2,1)S(1)}, u32[]{:S(2)}, u32[]{:S(2)}) collective-permute-start(bf16[1040,128]{1,0:T(8,128)(2,1)S(1)} %shard_map.65.refs_0_), channel_id=1, source_target_pairs={{0,2},{1,3},{2,0},{3,1},{4,6},{5,7},{6,4},{7,5},{8,10},{9,11},{10,... | collective-permute-start | bytes 798728 | tf_op jit(solution)/shard_map/ppermute | solution.py:38
  9.3 13.1 %collective-permute-start.1 = (bf16[1040,128]{1,0:T(8,128)(2,1)S(1)}, bf16[1040,128]{1,0:T(8,128)(2,1)S(1)}, u32[]{:S(2)}, u32[]{:S(2)}) collective-permute-start(bf16[1040,128]{1,0:T(8,128)(2,1)S(1)} %shard_map.65.refs_0_), channel_id=1, source_target_pairs={{0,4},{1,5},{2,6},{3,7},{4,8},{5,9},{6,10},{7,11},{8,12},{9,13},{1... | collective-permute-start | bytes 798728 | tf_op jit(solution)/shard_map/ppermute | solution.py:38
  9.3 13.9 %collective-permute-start.2 = (bf16[1040,128]{1,0:T(8,128)(2,1)S(1)}, bf16[1040,128]{1,0:T(8,128)(2,1)S(1)}, u32[]{:S(2)}, u32[]{:S(2)}) collective-permute-start(bf16[1040,128]{1,0:T(8,128)(2,1)S(1)} %shard_map.65.refs_0_), channel_id=1, source_target_pairs={{0,12},{1,13},{2,14},{3,15},{4,0},{5,1},{6,2},{7,3},{8,4},{9,5},{1... | collective-permute-start | bytes 798728 | tf_op jit(solution)/shard_map/ppermute | solution.py:38
  14.5 16.0 %collective-permute-start.9 = (bf16[512,256]{1,0:T(8,128)(2,1)S(1)}, bf16[512,256]{1,0:T(8,128)(2,1)S(1)}, u32[]{:S(2)}, u32[]{:S(2)}) collective-permute-start(bf16[512,256]{1,0:T(8,128)(2,1)S(1)} %collective-permute-done.7.refs_8_), channel_id=1, source_target_pairs={{0,16},{1,17},{2,18},{3,19},{4,20},{5,21},{6,22},{7,23},{8,24},{9,... | collective-permute-start | bytes 786440 | tf_op jit(solution)/shard_map/ppermute | solution.py:38
  17.1 13.4 %collective-permute-start.4 = (bf16[1040,128]{1,0:T(8,128)(2,1)S(1)}, bf16[1040,128]{1,0:T(8,128)(2,1)S(1)}, u32[]{:S(2)}, u32[]{:S(2)}) collective-permute-start(bf16[1040,128]{1,0:T(8,128)(2,1)S(1)} %collective-permute-done.refs_1_), channel_id=1, source_target_pairs={{0,12},{1,13},{2,14},{3,15},{4,0},{5,1},{6,2},{7,3},{8,4},{9,5},{1... | collective-permute-start | bytes 798728 | tf_op jit(solution)/shard_map/ppermute | solution.py:38
  20.4 10.1 %collective-permute-start.11 = (bf16[512,256]{1,0:T(8,128)(2,1)S(1)}, bf16[512,256]{1,0:T(8,128)(2,1)S(1)}, u32[]{:S(2)}, u32[]{:S(2)}) collective-permute-start(bf16[512,256]{1,0:T(8,128)(2,1)S(1)} %collective-permute-done.7.refs_8_), channel_id=1, source_target_pairs={{0,1},{1,0},{2,3},{3,2},{4,5},{5,4},{6,7},{7,6},{8,9},{9,8},{10,11... | collective-permute-start | bytes 786440 | tf_op jit(solution)/shard_map/ppermute | solution.py:38
  22.4 11.4 %collective-permute-start.5 = (bf16[1040,128]{1,0:T(8,128)(2,1)S(1)}, bf16[1040,128]{1,0:T(8,128)(2,1)S(1)}, u32[]{:S(2)}, u32[]{:S(2)}) collective-permute-start(bf16[1040,128]{1,0:T(8,128)(2,1)S(1)} %collective-permute-done.1.refs_2_), channel_id=1, source_target_pairs={{0,4},{1,5},{2,6},{3,7},{4,8},{5,9},{6,10},{7,11},{8,12},{9,13},{1... | collective-permute-start | bytes 798728 | tf_op jit(solution)/shard_map/ppermute | solution.py:38
  23.2 10.6 %collective-permute-start.8 = (bf16[512,256]{1,0:T(8,128)(2,1)S(1)}, bf16[512,256]{1,0:T(8,128)(2,1)S(1)}, u32[]{:S(2)}, u32[]{:S(2)}) collective-permute-start(bf16[512,256]{1,0:T(8,128)(2,1)S(1)} %collective-permute-done.7.refs_8_), channel_id=1, source_target_pairs={{0,112},{1,113},{2,114},{3,115},{4,116},{5,117},{6,118},{7,119},{8... | collective-permute-start | bytes 786440 | tf_op jit(solution)/shard_map/ppermute | solution.py:38
  30.5 9.7 %collective-permute-start.10 = (bf16[512,256]{1,0:T(8,128)(2,1)S(1)}, bf16[512,256]{1,0:T(8,128)(2,1)S(1)}, u32[]{:S(2)}, u32[]{:S(2)}) collective-permute-start(bf16[512,256]{1,0:T(8,128)(2,1)S(1)} %collective-permute-done.9.refs_10_), channel_id=1, source_target_pairs={{0,16},{1,17},{2,18},{3,19},{4,20},{5,21},{6,22},{7,23},{8,24},{9,... | collective-permute-start | bytes 786440 | tf_op jit(solution)/shard_map/ppermute | solution.py:38
  30.5 9.8 %collective-permute-start.3 = (bf16[1040,128]{1,0:T(8,128)(2,1)S(1)}, bf16[1040,128]{1,0:T(8,128)(2,1)S(1)}, u32[]{:S(2)}, u32[]{:S(2)}) collective-permute-start(bf16[1040,128]{1,0:T(8,128)(2,1)S(1)} %collective-permute-done.refs_1_), channel_id=1, source_target_pairs={{0,4},{1,5},{2,6},{3,7},{4,8},{5,9},{6,10},{7,11},{8,12},{9,13},{1... | collective-permute-start | bytes 798728 | tf_op jit(solution)/shard_map/ppermute | solution.py:38
  30.5 9.8 %collective-permute-start.6 = (bf16[1040,128]{1,0:T(8,128)(2,1)S(1)}, bf16[1040,128]{1,0:T(8,128)(2,1)S(1)}, u32[]{:S(2)}, u32[]{:S(2)}) collective-permute-start(bf16[1040,128]{1,0:T(8,128)(2,1)S(1)} %collective-permute-done.4.refs_5_), channel_id=1, source_target_pairs={{0,12},{1,13},{2,14},{3,15},{4,0},{5,1},{6,2},{7,3},{8,4},{9,5},{1... | collective-permute-start | bytes 798728 | tf_op jit(solution)/shard_map/ppermute | solution.py:38
  33.8 6.6 %collective-permute-start.13 = (bf16[512,256]{1,0:T(8,128)(2,1)S(1)}, bf16[512,256]{1,0:T(8,128)(2,1)S(1)}, u32[]{:S(2)}, u32[]{:S(2)}) collective-permute-start(bf16[512,256]{1,0:T(8,128)(2,1)S(1)} %collective-permute-done.9.refs_10_), channel_id=1, source_target_pairs={{0,1},{1,0},{2,3},{3,2},{4,5},{5,4},{6,7},{7,6},{8,9},{9,8},{10,11... | collective-permute-start | bytes 786440 | tf_op jit(solution)/shard_map/ppermute | solution.py:38
  33.8 6.5 %collective-permute-start.12 = (bf16[512,256]{1,0:T(8,128)(2,1)S(1)}, bf16[512,256]{1,0:T(8,128)(2,1)S(1)}, u32[]{:S(2)}, u32[]{:S(2)}) collective-permute-start(bf16[512,256]{1,0:T(8,128)(2,1)S(1)} %collective-permute-done.8.refs_9_), channel_id=1, source_target_pairs={{0,1},{1,0},{2,3},{3,2},{4,5},{5,4},{6,7},{7,6},{8,9},{9,8},{10,11... | collective-permute-start | bytes 786440 | tf_op jit(solution)/shard_map/ppermute | solution.py:38
  40.2 1.5 %collective-permute-start.14 = (bf16[512,256]{1,0:T(8,128)(2,1)S(1)}, bf16[512,256]{1,0:T(8,128)(2,1)S(1)}, u32[]{:S(2)}, u32[]{:S(2)}) collective-permute-start(bf16[512,256]{1,0:T(8,128)(2,1)S(1)} %collective-permute-done.10.refs_11_), channel_id=1, source_target_pairs={{0,1},{1,0},{2,3},{3,2},{4,5},{5,4},{6,7},{7,6},{8,9},{9,8},{10,11... | collective-permute-start | bytes 786440 | tf_op jit(solution)/shard_map/ppermute | solution.py:38
  50.2 4.1 %collective-permute-start.15 = (bf16[128,1024]{1,0:T(8,128)(2,1)S(1)}, bf16[128,1024]{1,0:T(8,128)(2,1)S(1)}, u32[]{:S(2)}, u32[]{:S(2)}) collective-permute-start(bf16[128,1024]{1,0:T(8,128)(2,1)S(1)} %get-tuple-element.19), channel_id=1, source_target_pairs={{0,1},{1,0},{2,3},{3,2},{4,5},{5,4},{6,7},{7,6},{8,9},{9,8},{10,11... | collective-permute-start | bytes 786440 | tf_op jit(solution)/shard_map/ppermute | solution.py:38
  54.3 6.9 %collective-permute-start.16 = (bf16[384,1024]{1,0:T(8,128)(2,1)S(1)}, bf16[384,1024]{1,0:T(8,128)(2,1)S(1)}, u32[]{:S(2)}, u32[]{:S(2)}) collective-permute-start(bf16[384,1024]{1,0:T(8,128)(2,1)S(1)} %shard_map.67.unused_ref), channel_id=1, source_target_pairs={{0,1},{1,0},{2,3},{3,2},{4,5},{5,4},{6,7},{7,6},{8,9},{9,8},{10,11... | collective-permute-start | bytes 2359304 | tf_op jit(solution)/shard_map/ppermute | solution.py:38
  54.5 10.3 %collective-permute-start.17 = (bf16[64,1024]{1,0:T(8,128)(2,1)S(1)}, bf16[64,1024]{1,0:T(8,128)(2,1)S(1)}, u32[]{:S(2)}, u32[]{:S(2)}) collective-permute-start(bf16[64,1024]{1,0:T(8,128)(2,1)S(1)} %get-tuple-element.21.unused_ref), channel_id=1, source_target_pairs={{0,4},{1,5},{2,6},{3,7},{4,8},{5,9},{6,10},{7,11},{8,12},{9,13},{1... | collective-permute-start | bytes 393224 | tf_op jit(solution)/shard_map/ppermute | solution.py:38
  54.5 6.9 %collective-permute-start.19 = (bf16[64,1024]{1,0:T(8,128)(2,1)S(1)}, bf16[64,1024]{1,0:T(8,128)(2,1)S(1)}, u32[]{:S(2)}, u32[]{:S(2)}) collective-permute-start(bf16[64,1024]{1,0:T(8,128)(2,1)S(1)} %get-tuple-element.26), channel_id=1, source_target_pairs={{0,12},{1,13},{2,14},{3,15},{4,0},{5,1},{6,2},{7,3},{8,4},{9,5},{1... | collective-permute-start | bytes 393224 | tf_op jit(solution)/shard_map/ppermute | solution.py:38
  61.5 8.2 %collective-permute-start.20 = (bf16[128,1024]{1,0:T(8,128)(2,1)S(1)}, bf16[128,1024]{1,0:T(8,128)(2,1)S(1)}, u32[]{:S(2)}, u32[]{:S(2)}) collective-permute-start(bf16[128,1024]{1,0:T(8,128)(2,1)S(1)} %pad_maximum_fusion.1), channel_id=1, source_target_pairs={{0,12},{1,13},{2,14},{3,15},{4,0},{5,1},{6,2},{7,3},{8,4},{9,5},{1... | collective-permute-start | bytes 786440 | tf_op jit(solution)/shard_map/ppermute | solution.py:38
  64.8 8.5 %collective-permute-start.18 = (bf16[128,1024]{1,0:T(8,128)(2,1)S(1)}, bf16[128,1024]{1,0:T(8,128)(2,1)S(1)}, u32[]{:S(2)}, u32[]{:S(2)}) collective-permute-start(bf16[128,1024]{1,0:T(8,128)(2,1)S(1)} %pad_maximum_fusion), channel_id=1, source_target_pairs={{0,4},{1,5},{2,6},{3,7},{4,8},{5,9},{6,10},{7,11},{8,12},{9,13},{1... | collective-permute-start | bytes 786440 | tf_op jit(solution)/shard_map/ppermute | solution.py:38
  73.5 5.1 %collective-permute-start.23 = (bf16[32,1024]{1,0:T(8,128)(2,1)S(1)}, bf16[32,1024]{1,0:T(8,128)(2,1)S(1)}, u32[]{:S(2)}, u32[]{:S(2)}) collective-permute-start(bf16[32,1024]{1,0:T(8,128)(2,1)S(1)} %get-tuple-element.32), channel_id=1, source_target_pairs={{0,2},{1,3},{2,0},{3,1},{4,6},{5,7},{6,4},{7,5},{8,10},{9,11},{10,... | collective-permute-start | bytes 196616 | tf_op jit(solution)/shard_map/ppermute | solution.py:38
  73.6 8.0 %collective-permute-start.21 = (bf16[32,1024]{1,0:T(8,128)(2,1)S(1)}, bf16[32,1024]{1,0:T(8,128)(2,1)S(1)}, u32[]{:S(2)}, u32[]{:S(2)}) collective-permute-start(bf16[32,1024]{1,0:T(8,128)(2,1)S(1)} %get-tuple-element.31), channel_id=1, source_target_pairs={{0,16},{1,17},{2,18},{3,19},{4,20},{5,21},{6,22},{7,23},{8,24},{9,... | collective-permute-start | bytes 196616 | tf_op jit(solution)/shard_map/ppermute | solution.py:38
  73.7 9.6 %collective-permute-start.22 = (bf16[32,1024]{1,0:T(8,128)(2,1)S(1)}, bf16[32,1024]{1,0:T(8,128)(2,1)S(1)}, u32[]{:S(2)}, u32[]{:S(2)}) collective-permute-start(bf16[32,1024]{1,0:T(8,128)(2,1)S(1)} %get-tuple-element.33), channel_id=1, source_target_pairs={{0,18},{1,19},{2,16},{3,17},{4,22},{5,23},{6,20},{7,21},{8,26},{9,... | collective-permute-start | bytes 196616 | tf_op jit(solution)/shard_map/ppermute | solution.py:38
